TPU v7x, 128 devices: a whole 4x4x4 slice. The times are simulated.
128 devices in a mesh: pool: 32 (over x, z, core), tp: 4 (over y).
Axes of the slice: x: 4, y: 4, z: 4, core: 2. Of those that a mesh axis runs over, the one named last changes fastest.
Arguments:
- tokens: bfloat16 [4096, 7168], P('pool', 'tp'), may hold values from -6 to 6
- down_weight: bfloat16 [7168, 576], P('tp'), may hold values from -0.0625 to 0.0625
- kv_gain: float32 [512], replicated, may hold values from 0.4 to 1.6
- queries: bfloat16 [4096, 128, 576], P('pool', 'tp'), may hold values from -151 to 151
- value_weight: bfloat16 [128, 512, 128], P('tp'), may hold values from -1 to 1
- pool: bfloat16 [2048, 64, 576], P('pool', 'tp'), may hold values from -4 to 4
- block_holder: int32 [32, 32], replicated, may hold values from 0 to 31, as said below
- block_slot: int32 [32, 32], replicated, may hold values from 0 to 63, as said below
- prefix_blocks: int32 [32], replicated, may hold values from 1 to 30, as said below
- suffix_len: int32 [32], replicated, may hold values from 1 to 128, 3072 in all
Outputs:
- attn_out: bfloat16 [4096, 16384], P('pool', 'tp')
- new_pool: bfloat16 [2048, 64, 576], P('pool', 'tp')
Inputs may be any that keep to these rules, and one draw needn't show every extreme that they name: `block_holder`: table entries 2 * k to 2 * k + 1 of a request name one holder, and different such groups of one request name different holders, so at most 2 blocks of one request sit on one holder. `block_slot`: no two table entries name the same holder and slot. `prefix_blocks`: some request has 30 prefix blocks.
All inputs are finite; a program needn't handle non-finite values.
Results may differ from a plain program's by a relative error of at most 0.0063.
Values may be sent and summed in bfloat16 or wider, within the bound.
A program may use at most 128 MiB of HBM per device.

v0:
```python
import jax
import jax.numpy as jnp
from jax import lax
from jax.sharding import PartitionSpec as P

LATENT = 512
VALUE_DIM = 128
BLOCK = 64
SUFFIX = 128
TABLE = 32
LATENT_ROW_WIDTH = 576
NEW_BLOCKS = 2
PREFIX_SPAN = 30


logit_scale_factor = 192.0 ** (-0.5)
rope_base = 10000.0
epsilon = 1e-06


def make_keys(latent, positions, kv_gain, live):
    width = kv_gain.shape[0]
    content = latent[:, :width]
    rotary = latent[:, width:]
    inverse = lax.rsqrt(jnp.mean(content * content, axis=1, keepdims=True) + epsilon)
    normed = content * inverse * kv_gain[None, :]
    half_width = rotary.shape[1] // 2
    exponent = jnp.arange(half_width).astype(jnp.float32) * (2.0 / rotary.shape[1])
    angles = positions[:, None] * (rope_base ** (-exponent))[None, :]
    cosine_part = jnp.cos(angles)
    sine_part = jnp.sin(angles)
    first_half = rotary[:, :half_width]
    second_half = rotary[:, half_width:]
    turned = jnp.concatenate(
        [
            first_half * cosine_part - second_half * sine_part,
            first_half * sine_part + second_half * cosine_part,
        ],
        axis=1,
    )
    joined = jnp.concatenate([normed, turned], axis=1)
    return jnp.where(live[:, None], joined, 0.0).astype(jnp.bfloat16)


def on_device(
    tokens,
    down_weight,
    kv_gain,
    queries,
    value_weight,
    pool,
    block_holder,
    block_slot,
    prefix_blocks,
    suffix_len,
):
    pool_count = lax.axis_size("pool")
    tp_count = lax.axis_size("tp")
    own_index = lax.axis_index("pool")
    tp_index = lax.axis_index("tp")
    requests = block_holder.shape[0]
    capacity = max(2, TABLE // pool_count)
    slot_count = pool.shape[0]
    block_rows = pool.shape[1]
    steps_index = jnp.arange(SUFFIX)
    prefix_count = prefix_blocks[own_index]
    length = suffix_len[own_index]
    partial_latent = jnp.dot(tokens, down_weight, preferred_element_type=jnp.float32)
    total = lax.psum(partial_latent, "tp")
    positions = (prefix_count * BLOCK + steps_index).astype(jnp.float32)
    new_keys = make_keys(total, positions, kv_gain, steps_index < length)
    own_rows = lax.dynamic_slice_in_dim(
        new_keys.reshape(NEW_BLOCKS, BLOCK, LATENT_ROW_WIDTH), tp_index * block_rows, block_rows, 1
    )
    entry = jnp.arange(TABLE)
    valid = entry[None, :] < prefix_blocks[:, None]
    before = entry[:, None] > entry[None, :]
    same_holder = (
        (block_holder[:, :, None] == block_holder[:, None, :]) & valid[:, None, :] & before[None]
    )
    ranking = jnp.minimum(jnp.sum(same_holder.astype(jnp.int32), axis=2), capacity - 1)
    held_here = valid & (block_holder == own_index)
    picked = held_here[:, None, :] & (ranking[:, None, :] == jnp.arange(capacity)[None, :, None])
    source_slot = jnp.sum(picked.astype(jnp.int32) * block_slot[:, None, :], axis=2)
    filled = jnp.any(picked, axis=2)
    outgoing = jnp.take(pool, source_slot.reshape(-1), axis=0).reshape(
        requests, capacity, block_rows, LATENT_ROW_WIDTH
    )
    outgoing = jnp.where(filled[:, :, None, None], outgoing, jnp.zeros((), jnp.bfloat16))
    copies = jnp.broadcast_to(
        outgoing[:, None], (requests, tp_count, capacity, block_rows, LATENT_ROW_WIDTH)
    )
    copies = copies.reshape(requests * tp_count, capacity, block_rows, LATENT_ROW_WIDTH)
    arrived = lax.all_to_all(copies, ("pool", "tp"), split_axis=0, concat_axis=2, tiled=True)
    arrived = arrived.reshape(capacity * pool_count, BLOCK, LATENT_ROW_WIDTH)
    own_holder = block_holder[own_index]
    own_rank = ranking[own_index]
    token_position = own_rank[:PREFIX_SPAN] * pool_count + own_holder[:PREFIX_SPAN]
    prefix_keys = jnp.take(arrived, token_position, axis=0).reshape(
        PREFIX_SPAN * BLOCK, LATENT_ROW_WIDTH
    )
    keys = jnp.concatenate([prefix_keys, new_keys], axis=0)
    latents = keys[:, :LATENT]
    key_index = jnp.arange(PREFIX_SPAN * BLOCK + SUFFIX)
    visible = jnp.where(
        key_index[None, :] < PREFIX_SPAN * BLOCK,
        (key_index < prefix_count * BLOCK)[None, :],
        key_index[None, :] - PREFIX_SPAN * BLOCK <= steps_index[:, None],
    )
    head_count = queries.shape[1]
    group = min(head_count, max(1, 1024 // SUFFIX))
    while head_count % group != 0:
        group = group - 1

    def one_group(index):
        query_part = lax.dynamic_slice_in_dim(queries, index * group, group, 1)
        value_portion = lax.dynamic_slice_in_dim(value_weight, index * group, group, 0)
        scores = (
            jnp.einsum("shk,tk->hst", query_part, keys, preferred_element_type=jnp.float32)
            * logit_scale_factor
        )
        scores = jnp.where(visible[None], scores, -jnp.inf)
        highest = jnp.max(scores, axis=2, keepdims=True)
        exponent = jnp.exp(scores - highest)
        weights = (exponent / jnp.sum(exponent, axis=2, keepdims=True)).astype(jnp.bfloat16)
        mixed_output = jnp.einsum(
            "hst,tk->hsk", weights, latents, preferred_element_type=jnp.float32
        ).astype(jnp.bfloat16)
        return jnp.einsum(
            "tnu,tux->ntx", mixed_output, value_portion, preferred_element_type=jnp.float32
        )

    grouped = lax.map(one_group, jnp.arange(head_count // group))
    value_rows = jnp.transpose(grouped, (1, 0, 2, 3)).reshape(SUFFIX, head_count * VALUE_DIM)
    attn_out = jnp.where((steps_index < length)[:, None], value_rows, 0.0).astype(jnp.bfloat16)
    every_new = lax.all_gather(own_rows, "pool", axis=0, tiled=True)
    places = prefix_blocks[:, None] + jnp.arange(NEW_BLOCKS)[None, :]
    target_holder = jnp.take_along_axis(block_holder, places, axis=1)
    target_slot = jnp.take_along_axis(block_slot, places, axis=1)
    destination = jnp.where(target_holder == own_index, target_slot, slot_count).reshape(-1)
    new_pool = pool.at[destination].set(every_new, mode="drop")
    return (attn_out, new_pool)


def solution(mesh):
    in_specs = (
        P("pool", "tp"),
        P("tp", None),
        P(),
        P("pool", "tp", None),
        P("tp", None, None),
        P("pool", "tp", None),
        P(),
        P(),
        P(),
        P(),
    )
    out_specs = (P("pool", "tp"), P("pool", "tp", None))
    return jax.shard_map(
        on_device, mesh=mesh, in_specs=in_specs, out_specs=out_specs, check_vma=False
    )
```

profile of v0, /device:TPU:0, one launch (start us, length us, event | category | flops | bytes accessed | tf_op | source)
XLA Modules:
  0.0 266.2 jit_solution(6644553686740862893)
XLA Ops:
  7.2 1.5 copy.76
  8.8 0.8 convert_reduce_fusion
  9.6 0.1 fusion.34
  9.7 0.1 select_reduce_fusion
  9.9 0.1 copy.47
  10.0 0.1 copy.46
  10.1 0.1 reshape.240
  10.3 1.8 gather_fusion
  12.0 1.6 select_select_fusion
  13.6 2.8 %broadcast_in_dim.150 = bf16[32,4,2,16,576]{4,3,2,1,0:T(8,128)(2,1)} broadcast(bf16[32,2,16,576]{3,2,1,0:T(8,128)(2,1)S(1)} %select_select_fusion), dimensions={0,2,3,4} | broadcast | bytes 5898240 | tf_op jit(solution)/shard_map/broadcast_in_dim | solution.py:90
  16.4 11.6 %all-to-all-start = ((bf16[128,2,16,576]{3,2,1,0:T(8,128)(2,1)}), bf16[128,2,16,576]{3,2,1,0:T(8,128)(2,1)}, u32[]{:S(2)}, u32[]{:S(2)}) async-start(bf16[128,2,16,576]{3,2,1,0:T(8,128)(2,1)} %bitcast.73), calls=%async_computation | async-start | bytes 10485760 | tf_op jit(solution)/shard_map/all_to_all | solution.py:94
  28.1 2.4 fusion.45
  30.6 0.2 all-gather.2.cloned.1.call-start
  30.8 0.6 dynamic_slice.26
  31.4 0.6 dynamic_slice.25
  32.7 0.6 add_compare_fusion
  33.3 71.3 %all-reduce.2.cloned.1.call-done = f32[128,576]{0,1:T(8,128)} async-done(((f32[128,576]{0,1:T(8,128)}), f32[128,576]{0,1:T(8,128)}) %all-reduce.2.cloned.1.call-update) | async-done | bytes 294928 | tf_op jit(solution)/shard_map/psum | solution.py:69
  104.6 0.9 fusion.39
  105.5 0.1 copy.63
  105.6 0.1 copy.64
  105.8 1.0 multiply_reduce_fusion
  106.8 1.1 multiply_multiply_fusion
  107.9 0.1 copy.59
  108.0 0.7 fusion.32
  109.0 0.8 gather_fusion.3
  109.8 0.8 gather_fusion.2
  110.7 0.6 broadcast_in_dim.144
  111.3 0.1 reshape.296
  111.5 0.1 reshape.301
  111.8 0.1 reshape.244
  111.9 0.6 iota_compare_fusion.6
  112.6 0.4 copy-done.7
  113.0 0.2 copy.50
  113.2 39.3 %all-gather.2.cloned.1.call-done = bf16[64,16,576]{2,1,0:T(8,128)(2,1)} async-done(((bf16[2,16,576]{2,1,0:T(8,128)(2,1)}), bf16[64,16,576]{2,1,0:T(8,128)(2,1)}) %all-gather.2.cloned.1.call-update) | async-done | bytes 1179664 | tf_op jit(solution)/shard_map/all_gather | solution.py:136
  152.5 6.5 %scatter_fusion = bf16[64,16,576]{2,1,0:T(8,128)(2,1)S(1)} fusion(bf16[64,16,576]{2,1,0:T(8,128)(2,1)S(1)} %copy.76, s32[64]{0:T(128)S(1)} %fusion.43, bf16[64,16,576]{2,1,0:T(8,128)(2,1)} %all-gather.2.cloned.1.call-done), kind=kCustom, calls=%fused_computation.4 | custom fusion | bytes 3539200 | tf_op jit(solution)/shard_map/scatter | solution.py:141
  159.0 5.7 %copy.49 = bf16[128,2,16,576]{3,2,0,1:T(8,128)(2,1)} copy(bf16[128,2,16,576]{3,2,1,0:T(8,128)(2,1)} %all-to-all-done) | data formatting | bytes 9437184 | tf_op jit(solution)/shard_map/all_to_all | solution.py:94
  164.7 4.9 %gather_fusion.1 = bf16[30,64,576]{2,1,0:T(8,128)(2,1)} fusion(bf16[64,64,576]{2,1,0:T(8,128)(2,1)} %bitcast.74, s32[1024]{0:T(1024)S(1)} %pad_clamp_fusion), kind=kCustom, calls=%fused_computation.3 | custom fusion | bytes 4423800 | tf_op jit(solution)/shard_map/jit(_take)/gather | solution.py:99
  169.6 2.4 bitcast_select_fusion
  171.9 1.5 fusion.27
  173.5 1.7 pad_maximum_fusion
  175.2 2.9 %copy.52 = bf16[2048,576]{0,1:T(8,128)(2,1)S(1)} copy(bf16[2048,576]{1,0:T(8,128)(2,1)} %pad_maximum_fusion) | data formatting | bytes 4718592
  178.2 78.3 %while.11 = (s32[]{:T(128)}, bf16[4,128,8,128]{1,3,2,0:T(8,128)(2,1)}, s32[4]{0:T(128)S(1)}, bf16[32,512,128]{2,1,0:T(8,128)(2,1)}, bf16[128,32,576]{0,2,1:T(8,1...) while((s32[]{:T(128)}, ...), condition=%wide.region_8.9_spmd.clone, body=%wide.region_5.0_spmd.clone.sunk | while | flops 4715448320 | bytes 41308368 | solution.py:133
  178.2 0.6 dynamic_slice.62
  179.4 0.2 fusion.61
  179.6 4.8 %fusion.60 = f32[128,8,2048]{2,0,1:T(8,128)S(1)} fusion(bf16[2048,576]{0,1:T(8,128)(2,1)S(1)} %get-tuple-element.241, bf16[128,32,576]{0,2,1:T(8,128)(2,1)} %get-tuple-element.240, s32[]{:T(128)S(6)} %select_n.189), kind=kOutput, calls=%fused_computation.17.clone.1 | convolution fusion | flops 2415919104 | bytes 11927556 | tf_op jit(solution)/shard_map/while/body/eval_jaxpr/shk,tk->hst/dot_general | solution.py:119
  184.4 5.7 %fusion.62 = (f32[8,128]{1,0:T(8,128)S(1)}, f32[8,128,2048]{2,1,0:T(8,128)}) fusion(f32[128,8,2048]{2,0,1:T(8,128)S(1)} %fusion.60, pred[128,2048]{1,0:T(8,128)(4,1)S(1)} %fusion.61), kind=kOutput, calls=%fused_computation.94.clone.1 | output fusion | flops 12584959 | bytes 17043456 | tf_op jit(solution)/shard_map/while/body/eval_jaxpr/sub | solution.py:124
  190.1 7.7 %fusion.63 = bf16[4,128,8,128]{1,3,2,0:T(8,128)(2,1)} fusion(bf16[4,128,8,128]{1,3,2,0:T(8,128)(2,1)} %get-tuple-element.223, s32[]{:T(128)S(6)} %copy.70, bf16[2048,512]{1,0:T(8,128)(2,1)} %get-tuple-element.242, f32[8,128,2048]{2,1,0:T(8,128)} %get-tuple-element.206, f32[8,128]{1,0:T(8,128)S(1)} %get-tuple-element.207, ...), kind=kOutput, calls=%fused_computation.22.clone.1 | convolution fusion | flops 2286419968 | bytes 12062728 | tf_op jit(solution)/shard_map/while/body/eval_jaxpr/tnu,tux->ntx/dot_general | solution.py:129
  197.8 0.6 dynamic_slice.62
  199.0 0.2 fusion.61
  199.2 4.8 %fusion.60 = f32[128,8,2048]{2,0,1:T(8,128)S(1)} fusion(bf16[2048,576]{0,1:T(8,128)(2,1)S(1)} %get-tuple-element.241, bf16[128,32,576]{0,2,1:T(8,128)(2,1)} %get-tuple-element.240, s32[]{:T(128)S(6)} %select_n.189), kind=kOutput, calls=%fused_computation.17.clone.1 | convolution fusion | flops 2415919104 | bytes 11927556 | tf_op jit(solution)/shard_map/while/body/eval_jaxpr/shk,tk->hst/dot_general | solution.py:119
  204.0 5.7 %fusion.62 = (f32[8,128]{1,0:T(8,128)S(1)}, f32[8,128,2048]{2,1,0:T(8,128)}) fusion(f32[128,8,2048]{2,0,1:T(8,128)S(1)} %fusion.60, pred[128,2048]{1,0:T(8,128)(4,1)S(1)} %fusion.61), kind=kOutput, calls=%fused_computation.94.clone.1 | output fusion | flops 12584959 | bytes 17043456 | tf_op jit(solution)/shard_map/while/body/eval_jaxpr/sub | solution.py:124
  209.7 7.7 %fusion.63 = bf16[4,128,8,128]{1,3,2,0:T(8,128)(2,1)} fusion(bf16[4,128,8,128]{1,3,2,0:T(8,128)(2,1)} %get-tuple-element.223, s32[]{:T(128)S(6)} %copy.70, bf16[2048,512]{1,0:T(8,128)(2,1)} %get-tuple-element.242, f32[8,128,2048]{2,1,0:T(8,128)} %get-tuple-element.206, f32[8,128]{1,0:T(8,128)S(1)} %get-tuple-element.207, ...), kind=kOutput, calls=%fused_computation.22.clone.1 | convolution fusion | flops 2286419968 | bytes 12062728 | tf_op jit(solution)/shard_map/while/body/eval_jaxpr/tnu,tux->ntx/dot_general | solution.py:129
  217.3 0.6 dynamic_slice.62
  218.6 0.2 fusion.61
  218.8 4.8 %fusion.60 = f32[128,8,2048]{2,0,1:T(8,128)S(1)} fusion(bf16[2048,576]{0,1:T(8,128)(2,1)S(1)} %get-tuple-element.241, bf16[128,32,576]{0,2,1:T(8,128)(2,1)} %get-tuple-element.240, s32[]{:T(128)S(6)} %select_n.189), kind=kOutput, calls=%fused_computation.17.clone.1 | convolution fusion | flops 2415919104 | bytes 11927556 | tf_op jit(solution)/shard_map/while/body/eval_jaxpr/shk,tk->hst/dot_general | solution.py:119
  223.6 5.7 %fusion.62 = (f32[8,128]{1,0:T(8,128)S(1)}, f32[8,128,2048]{2,1,0:T(8,128)}) fusion(f32[128,8,2048]{2,0,1:T(8,128)S(1)} %fusion.60, pred[128,2048]{1,0:T(8,128)(4,1)S(1)} %fusion.61), kind=kOutput, calls=%fused_computation.94.clone.1 | output fusion | flops 12584959 | bytes 17043456 | tf_op jit(solution)/shard_map/while/body/eval_jaxpr/sub | solution.py:124
  229.2 7.7 %fusion.63 = bf16[4,128,8,128]{1,3,2,0:T(8,128)(2,1)} fusion(bf16[4,128,8,128]{1,3,2,0:T(8,128)(2,1)} %get-tuple-element.223, s32[]{:T(128)S(6)} %copy.70, bf16[2048,512]{1,0:T(8,128)(2,1)} %get-tuple-element.242, f32[8,128,2048]{2,1,0:T(8,128)} %get-tuple-element.206, f32[8,128]{1,0:T(8,128)S(1)} %get-tuple-element.207, ...), kind=kOutput, calls=%fused_computation.22.clone.1 | convolution fusion | flops 2286419968 | bytes 12062728 | tf_op jit(solution)/shard_map/while/body/eval_jaxpr/tnu,tux->ntx/dot_general | solution.py:129
  236.9 0.6 dynamic_slice.62
  238.2 0.2 fusion.61
  238.4 4.8 %fusion.60 = f32[128,8,2048]{2,0,1:T(8,128)S(1)} fusion(bf16[2048,576]{0,1:T(8,128)(2,1)S(1)} %get-tuple-element.241, bf16[128,32,576]{0,2,1:T(8,128)(2,1)} %get-tuple-element.240, s32[]{:T(128)S(6)} %select_n.189), kind=kOutput, calls=%fused_computation.17.clone.1 | convolution fusion | flops 2415919104 | bytes 11927556 | tf_op jit(solution)/shard_map/while/body/eval_jaxpr/shk,tk->hst/dot_general | solution.py:119
  243.1 5.7 %fusion.62 = (f32[8,128]{1,0:T(8,128)S(1)}, f32[8,128,2048]{2,1,0:T(8,128)}) fusion(f32[128,8,2048]{2,0,1:T(8,128)S(1)} %fusion.60, pred[128,2048]{1,0:T(8,128)(4,1)S(1)} %fusion.61), kind=kOutput, calls=%fused_computation.94.clone.1 | output fusion | flops 12584959 | bytes 17043456 | tf_op jit(solution)/shard_map/while/body/eval_jaxpr/sub | solution.py:124
  248.8 7.7 %fusion.63 = bf16[4,128,8,128]{1,3,2,0:T(8,128)(2,1)} fusion(bf16[4,128,8,128]{1,3,2,0:T(8,128)(2,1)} %get-tuple-element.223, s32[]{:T(128)S(6)} %copy.70, bf16[2048,512]{1,0:T(8,128)(2,1)} %get-tuple-element.242, f32[8,128,2048]{2,1,0:T(8,128)} %get-tuple-element.206, f32[8,128]{1,0:T(8,128)S(1)} %get-tuple-element.207, ...), kind=kOutput, calls=%fused_computation.22.clone.1 | convolution fusion | flops 2286419968 | bytes 12062728 | tf_op jit(solution)/shard_map/while/body/eval_jaxpr/tnu,tux->ntx/dot_general | solution.py:129
  256.5 1.6 copy.62
  258.1 1.2 select_convert_fusion
  (54 shorter events, 1.0 us)
Async XLA Ops:
  7.2 21.0 %copy-start = (bf16[1792,576]{0,1:T(8,128)(2,1)S(1)}, bf16[1792,576]{0,1:T(8,128)(2,1)}, u32[]{:S(2)}) copy-start(bf16[1792,576]{0,1:T(8,128)(2,1)} %param.15) | copy-start | bytes 6193156
  7.2 1.5 copy-start.2
  7.2 2.5 copy-start.3
  7.2 1.5 copy-start.9
  16.4 142.5 %all-to-all-start = ((bf16[128,2,16,576]{3,2,1,0:T(8,128)(2,1)}), bf16[128,2,16,576]{3,2,1,0:T(8,128)(2,1)}, u32[]{:S(2)}, u32[]{:S(2)}) async-start(bf16[128,2,16,576]{3,2,1,0:T(8,128)(2,1)} %bitcast.73), calls=%async_computation | async-start | bytes 10485760 | tf_op jit(solution)/shard_map/all_to_all | solution.py:94
  28.0 3.4 %copy-start.10 = (s32[32]{0:T(128)S(1)}, s32[32]{0:T(128)}, u32[]{:S(2)}) copy-start(s32[32]{0:T(128)} %param.23) | copy-start | bytes 388
  28.1 78.7 %copy-start.6 = (f32[512]{0:T(512)S(1)}, f32[512]{0:T(512)}, u32[]{:S(2)}) copy-start(f32[512]{0:T(512)} %param.16) | copy-start | bytes 6148
  28.1 76.6 %all-reduce.2.cloned.1.call-start = ((), (), s32[]{:S(2)}) async-start(), calls=%async_computation.1 | async-start | bytes 589824 | tf_op jit(solution)/shard_map/psum | solution.py:69
  30.6 121.9 %all-gather.2.cloned.1.call-start = ((), (), s32[]{:S(2)}) async-start(), calls=%async_computation.2 | async-start | bytes 1351680 | tf_op jit(solution)/shard_map/all_gather | solution.py:136
  112.5 0.5 copy-start.7
  159.0 5.8 %copy-start.4 = (bf16[64,16,576]{2,1,0:T(8,128)(2,1)}, bf16[64,16,576]{2,1,0:T(8,128)(2,1)S(1)}, u32[]{:S(2)}) copy-start(bf16[64,16,576]{2,1,0:T(8,128)(2,1)S(1)} %scatter_fusion) | copy-start | bytes 3538948
  164.7 4.9 %copy-start.5 = (pred[1920]{0:T(1024)(128)(4,1)S(1)}, pred[1920]{0:T(1024)(128)(4,1)}, u32[]{:S(2)}) copy-start(pred[1920]{0:T(1024)(128)(4,1)} %broadcast_in_dim.144) | copy-start | bytes 5764
  178.2 80.0 %copy-start.8 = (pred[128]{0:T(512)(128)(4,1)S(1)}, pred[128]{0:T(512)(128)(4,1)}, u32[]{:S(2)}) copy-start(pred[128]{0:T(512)(128)(4,1)} %copy-done.7) | copy-start | bytes 388
  256.5 2.9 %copy-start.1 = (bf16[1792,576]{0,1:T(8,128)(2,1)S(1)}, bf16[1792,576]{0,1:T(8,128)(2,1)}, u32[]{:S(2)}) copy-start(bf16[1792,576]{0,1:T(8,128)(2,1)} %param.15) | copy-start | bytes 6193156
Sparse Core Ops, SparseCore 0:
  31.8 72.7 all-reduce.1
  108.9 43.5 all-gather.1
where the time goes:
time: 268 us; the launch traced here: 266 us
  waiting for transfers between devices  111 us (41%)
  matrix products  52.3 us (20%)
  other arithmetic  38 us (14%)
  local copies, waits for them, and re-layouts  35.8 us (13%)
  between operations  15 us (6%)
  starting transfers between devices  11.9 us (4%)
    psum x1, waiting for transfers between devices, on_device(): total = lax.psum(partial_latent, 'tp')  71.3 us
    all_gather x1, waiting for transfers between devices, on_device(): every_new = lax.all_gather(own_rows, 'pool', axis=0, tiled=True)  39.3 us
    dot_general x4, matrix products, one_group(): jnp.einsum('tnu,tux->ntx', mixed_output, value_portion, preferred_element...  30.7 us
    sub x4, other arithmetic, one_group(): exponent = jnp.exp(scores - highest)  22.7 us
    dot_general x4, matrix products, one_group(): jnp.einsum('shk,tk->hst', query_part, keys, preferred_element_type=jnp.fl...  19.1 us
    all_to_all x1, starting transfers between devices, on_device(): lax.all_to_all(copies, ('pool', 'tp'), split_axis=0, concat_axis=2, tiled...  11.6 us
    scatter x1, local copies, waits for them, and re-layouts, on_device(): new_pool = pool.at[destination].set(every_new, mode='drop')  6.47 us
    all_to_all x1, local copies, waits for them, and re-layouts, on_device(): lax.all_to_all(copies, ('pool', 'tp'), split_axis=0, concat_axis=2, tiled...  5.74 us
  transfers between devices with their start and end apart: 3, of which 2 were waited for; matrix products, arithmetic and copies ran while one was open for 7% of the time, Pallas kernels for 0%

commit v1 on v0

v1 whole, which is shorter than its diff:
```python
import functools
import math

import jax
import jax.numpy as jnp
import numpy as np
from jax import lax
from jax.experimental import pallas as pl
from jax.experimental.pallas import tpu as pltpu
from jax.sharding import PartitionSpec as P

LATENT = 512
VALUE_DIM = 128
BLOCK = 64
SUFFIX = 128
TABLE = 32
WIDTH = 576
WIDE = 640
ROPE = WIDTH - LATENT
HALF = 256
ROWS = 256
SCALE = 192.0 ** (-0.5) * math.log2(math.e)
HIDDEN = -1e30
EPSILON = 1e-06
MESH = pl.DeviceIdType.MESH


def kernel(
    pool_count,
    tp_count,
    holder,
    slot,
    prefix,
    length,
    gain,
    frequency,
    tokens_h,
    down_h,
    queries_h,
    value_h,
    pool_h,
    out_h,
    new_pool_h,
    tokens_v,
    down_v,
    queries_raw,
    queries,
    value_v,
    pool_v,
    leaving,
    arrived_even,
    arrived_odd,
    partial_v,
    partial_in,
    fresh,
    fresh_in,
    own,
    near,
    far,
    acc,
    high,
    norm,
    out_v,
    new_pool_v,
    index_v,
    index_s,
    load_sem,
    index_sem,
    block_send,
    block_recv,
    sum_send,
    sum_recv,
    fresh_send,
    fresh_recv,
    near_send,
    near_recv,
    far_send,
    far_recv,
):
    me = lax.axis_index("pool")
    tp = lax.axis_index("tp")
    core, z, x = me % 2, (me // 2) % 4, me // 8
    ahead, behind = (tp + 1) % tp_count, (tp + tp_count - 1) % tp_count
    across = (tp + 2) % tp_count
    heads = value_v.shape[0]
    slots = pool_v.shape[0]
    piece = pool_v.shape[1]
    groups = TABLE // 2
    total_rows = queries.shape[0]
    arrived = (arrived_even, arrived_odd)

    def peer(step):
        to_core = (core + step % 2) % 2
        to_z = (z + (step // 2) % 4) % 4
        to_x = (x + step // 8) % 4
        return (to_x * 4 + to_z) * 2 + to_core

    loads = [
        pltpu.make_async_copy(pool_h, pool_v, load_sem.at[0]),
        pltpu.make_async_copy(tokens_h, tokens_v, load_sem.at[1]),
        pltpu.make_async_copy(down_h, down_v, load_sem.at[2]),
        pltpu.make_async_copy(queries_h, queries_raw, load_sem.at[3]),
        pltpu.make_async_copy(value_h, value_v, load_sem.at[4]),
    ]
    for load in loads:
        load.start()

    barrier = pltpu.get_barrier_semaphore()

    @pl.loop(1, pool_count)
    def _(step):
        pl.semaphore_signal(barrier, inc=1, device_id=(peer(step), tp), device_id_type=MESH)

    for step in range(1, tp_count):
        pl.semaphore_signal(
            barrier, inc=1, device_id=(me, (tp + step) % tp_count), device_id_type=MESH
        )
    pl.semaphore_wait(barrier, pool_count - 1 + tp_count - 1)

    loads[0].wait()

    def wanted(request):
        at = jnp.int32(0)
        for k in range(groups - 1):
            at = jnp.where(holder[request, 2 * k] == me, 2 * k, at)
        return at

    def send_blocks(parity):
        @pl.loop(1, pool_count)
        def _(step):
            request = peer(step)
            leaving[parity, request] = pool_v[slot[request, wanted(request) + parity]]
            pltpu.make_async_remote_copy(
                src_ref=leaving.at[parity, request],
                dst_ref=arrived[parity].at[me],
                send_sem=block_send.at[parity],
                recv_sem=block_recv.at[parity],
                device_id=(request, tp),
                device_id_type=MESH,
            ).start()

        arrived[parity][me] = pool_v[slot[me, wanted(me) + parity]]

    send_blocks(0)

    loads[1].wait()
    loads[2].wait()
    partial = jnp.dot(tokens_v[...], down_v[...], preferred_element_type=jnp.float32)
    for owner in range(tp_count):
        for b in range(2):
            partial_v[owner, b * piece : (b + 1) * piece, :] = partial[
                b * BLOCK + owner * piece : b * BLOCK + (owner + 1) * piece, :
            ]
    sums = []
    for step in range(1, tp_count):
        to = (tp + step) % tp_count
        copy = pltpu.make_async_remote_copy(
            src_ref=partial_v.at[to],
            dst_ref=partial_in.at[step - 1],
            send_sem=sum_send.at[step - 1],
            recv_sem=sum_recv.at[step - 1],
            device_id=(me, to),
            device_id_type=MESH,
        )
        copy.start()
        sums.append(copy)

    send_blocks(1)

    loads[3].wait()
    lane64 = lax.broadcasted_iota(jnp.int32, (ROWS, WIDE - WIDTH), 1)
    one_mark = jnp.where(lane64 == 0, 1.0, 0.0).astype(jnp.bfloat16)

    @pl.loop(0, total_rows // ROWS)
    def _(i):
        rows = pl.ds(pl.multiple_of(i * ROWS, ROWS), ROWS)
        queries[rows, :LATENT] = queries_raw[rows, :LATENT]
        queries[rows, LATENT:] = jnp.concatenate([queries_raw[rows, LATENT:], one_mark], axis=1)

    for copy in sums:
        copy.wait_recv()
    latent = partial_v[tp] + partial_in[0] + partial_in[1] + partial_in[2]
    content = latent[:, :LATENT]
    rotary = latent[:, LATENT:]
    inverse = lax.rsqrt(jnp.mean(content * content, axis=1, keepdims=True) + EPSILON)
    normed = content * inverse * gain[...]
    row = lax.broadcasted_iota(jnp.int32, (2 * piece, ROPE), 0)
    lane = lax.broadcasted_iota(jnp.int32, (2 * piece, ROPE), 1)
    token = (row // piece) * BLOCK + tp * piece + row % piece
    angles = (prefix[me] * BLOCK + token).astype(jnp.float32) * frequency[...]
    turned_by = jnp.concatenate([rotary[:, ROPE // 2 :], rotary[:, : ROPE // 2]], axis=1)
    sine = jnp.where(lane < ROPE // 2, -1.0, 1.0) * jnp.sin(angles)
    turned = rotary * jnp.cos(angles) + turned_by * sine
    row512 = lax.broadcasted_iota(jnp.int32, (2 * piece, LATENT), 0)
    token512 = (row512 // piece) * BLOCK + tp * piece + row512 % piece
    normed = jnp.where(token512 < length[me], normed, 0.0).astype(jnp.bfloat16)
    turned = jnp.where(token < length[me], turned, 0.0)
    plain = jnp.zeros((piece, WIDE - WIDTH), jnp.float32)
    for b in range(2):
        rows = slice(b * piece, (b + 1) * piece)
        last = jnp.concatenate([turned[rows], plain], axis=1).astype(jnp.bfloat16)
        fresh[b, :, :LATENT] = normed[rows]
        fresh[b, :, LATENT:] = last[:, :ROPE]
        own[b, (groups - 1) * piece : groups * piece, :LATENT] = normed[rows]
        own[b, (groups - 1) * piece : groups * piece, LATENT:] = last

    @pl.loop(1, pool_count)
    def _(step):
        pltpu.make_async_remote_copy(
            src_ref=fresh,
            dst_ref=fresh_in.at[pl.ds(2 * me, 2)],
            send_sem=fresh_send,
            recv_sem=fresh_recv,
            device_id=(peer(step), tp),
            device_id_type=MESH,
        ).start()

    fresh_in[pl.ds(2 * me, 2)] = fresh[...]

    lane_mark = lax.broadcasted_iota(jnp.int32, (piece, WIDE - WIDTH), 1)

    def gather_blocks(parity):
        others = arrived[parity].at[pl.ds(0, pool_count - 1)]
        pltpu.make_async_copy(others, others, block_recv.at[parity]).wait()

        @pl.loop(0, groups - 1)
        def _(k):
            block = arrived[parity][holder[me, 2 * k + parity]]
            mark = jnp.where(2 * k + parity < prefix[me], 0.0, HIDDEN)
            marks = jnp.where(lane_mark == 0, mark, 0.0).astype(jnp.bfloat16)
            rows = pl.ds(pl.multiple_of(k * piece, piece), piece)
            own[parity, rows, :LATENT] = block[:, :LATENT]
            own[parity, rows, LATENT:] = jnp.concatenate([block[:, LATENT:], marks], axis=1)

        for side, to in enumerate((ahead, behind)):
            near_copy(parity, side, to).start()

    def near_copy(parity, side, to):
        return pltpu.make_async_remote_copy(
            src_ref=own.at[parity],
            dst_ref=near.at[parity, side],
            send_sem=near_send.at[parity, side],
            recv_sem=near_recv.at[parity, side],
            device_id=(me, to),
            device_id_type=MESH,
        )

    def far_copy(parity, side, to):
        rows = pl.ds(side * (HALF // 2), HALF // 2)
        return pltpu.make_async_remote_copy(
            src_ref=near.at[parity, side, rows],
            dst_ref=far.at[parity, rows],
            send_sem=far_send.at[parity, side],
            recv_sem=far_recv.at[parity, side],
            device_id=(me, to),
            device_id_type=MESH,
        )

    def forward(parity):
        for side, to in enumerate((ahead, behind)):
            near_copy(parity, side, to).wait_recv()
            far_copy(parity, side, to).start()

    row_token = lax.broadcasted_iota(jnp.int32, (ROWS, 128), 0) // heads
    lane128 = lax.broadcasted_iota(jnp.int32, (ROWS, 128), 1)

    def attend(halves, first=False, last=False):
        def scores_of(rows):
            query = queries[rows, :]
            return [
                lax.dot_general(
                    query, keys[...], (((1,), (1,)), ((), ())), preferred_element_type=jnp.float32
                )
                for keys, _ in halves
            ]

        def weigh(i, rows, scores):
            tiles = []
            for score, (_, base) in zip(scores, halves):
                tiles.append(score[:, :128])
                seen_from = jnp.where(lane128 >= 128 - piece, base + lane128 - (128 - piece), -1)
                hide = seen_from > row_token + i * (ROWS // heads)
                tiles.append(jnp.where(hide, HIDDEN, score[:, 128:]))
            top = functools.reduce(jnp.maximum, tiles)
            top = jnp.max(top, axis=1, keepdims=True) * SCALE
            if first:
                new_high = jnp.broadcast_to(top, (ROWS, 128))
            else:
                old_high = high[rows, :]
                new_high = jnp.maximum(old_high, top)
                decay = jnp.exp2(old_high - new_high)
            raised = [jnp.exp2(tile * SCALE - new_high) for tile in tiles]
            count = functools.reduce(jnp.add, raised)
            if not first:
                count = count + norm[rows, :] * decay
            mixed = None
            for j, (keys, _) in enumerate(halves):
                weights = jnp.concatenate(
                    [r.astype(jnp.bfloat16) for r in raised[2 * j : 2 * j + 2]], axis=1
                )
                term = jnp.dot(weights, keys[:, :LATENT], preferred_element_type=jnp.float32)
                mixed = term if mixed is None else mixed + term
            if last:
                share = 1.0 / jnp.sum(count, axis=1, keepdims=True)
            else:
                high[rows, :] = new_high
                norm[rows, :] = count
            for j in range(LATENT // 128):
                part = mixed[:, j * 128 : (j + 1) * 128]
                if not first:
                    part = part + acc[j, rows, :] * decay
                if last:
                    part = part * share
                acc[j, rows, :] = part

        @pl.loop(0, total_rows // ROWS // 2)
        def _(pair):
            tiles = [2 * pair, 2 * pair + 1]
            places = [pl.ds(pl.multiple_of(i * ROWS, ROWS), ROWS) for i in tiles]
            scores = [scores_of(rows) for rows in places]
            for i, rows, score in zip(tiles, places, scores):
                weigh(i, rows, score)

    gather_blocks(0)
    attend([(own.at[0], tp * piece)], first=True)
    gather_blocks(1)
    attend([(own.at[1], BLOCK + tp * piece)])
    for parity in range(2):
        forward(parity)
        attend(
            [
                (near.at[parity, 0], parity * BLOCK + behind * piece),
                (near.at[parity, 1], parity * BLOCK + ahead * piece),
            ]
        )

    lane_slot = lax.broadcasted_iota(jnp.int32, (8, 128), 1)

    def mark_slot(request, index):
        for b in range(2):
            entry = prefix[request] + b
            here = holder[request, entry] == me
            target = jnp.where(here, slot[request, entry], -1)
            index = jnp.where(lane_slot == target, 2 * request + b, index)
        return index

    index_v[...] = lax.fori_loop(0, pool_count, mark_slot, jnp.full((8, 128), -1, jnp.int32))
    to_scalars = pltpu.make_async_copy(index_v, index_s, index_sem)
    to_scalars.start()
    arrivals = fresh_in.at[pl.ds(0, 2 * (pool_count - 1))]
    pltpu.make_async_copy(arrivals, arrivals, fresh_recv).wait()
    to_scalars.wait()

    @pl.loop(0, slots)
    def _(place):
        at = index_s[0, place]
        replaced = jnp.where(at >= 0, 1.0, 0.0)
        kept = pool_v[place]
        taken = fresh_in[jnp.maximum(at, 0)]
        new_pool_v[place] = jnp.where(replaced > 0.5, taken, kept)

    store_pool = pltpu.make_async_copy(new_pool_v, new_pool_h, load_sem.at[0])
    store_pool.start()

    for parity in range(2):
        for side, to in enumerate((ahead, behind)):
            far_copy(parity, side, to).wait_recv()
    attend(
        [(far.at[parity], parity * BLOCK + across * piece) for parity in range(2)], last=True
    )

    loads[4].wait()
    live = lax.broadcasted_iota(jnp.int32, (SUFFIX, VALUE_DIM), 0) < length[me]

    @pl.loop(0, heads // 4)
    def _(quad):
        for inner in range(4):
            head = quad * 4 + inner
            mixed = jnp.concatenate(
                [
                    acc[j, pl.ds(head, SUFFIX, stride=heads), :].astype(jnp.bfloat16)
                    for j in range(LATENT // 128)
                ],
                axis=1,
            )
            value = jnp.dot(mixed, value_v[head], preferred_element_type=jnp.float32)
            columns = pl.ds(pl.multiple_of(head * VALUE_DIM, VALUE_DIM), VALUE_DIM)
            out_v[:, columns] = jnp.where(live, value, 0.0).astype(jnp.bfloat16)

    store_out = pltpu.make_async_copy(out_v, out_h, load_sem.at[1])
    store_out.start()

    for copy in sums:
        copy.wait_send()
    for parity in range(2):
        sent = leaving.at[parity, pl.ds(0, pool_count - 1)]
        pltpu.make_async_copy(sent, sent, block_send.at[parity]).wait()
        for side, to in enumerate((ahead, behind)):
            near_copy(parity, side, to).wait_send()
            far_copy(parity, side, to).wait_send()
    pltpu.make_async_copy(arrivals, arrivals, fresh_send).wait()
    store_pool.wait()
    store_out.wait()


def on_device(
    pool_count,
    tp_count,
    tokens,
    down_weight,
    kv_gain,
    queries,
    value_weight,
    pool,
    block_holder,
    block_slot,
    prefix_blocks,
    suffix_len,
):
    heads = queries.shape[1]
    rows = queries.shape[0] * heads
    slots, piece, width = pool.shape
    exponent = np.arange(ROPE // 2).astype(np.float32) * np.float32(2.0 / ROPE)
    inverse_frequency = np.power(np.float32(10000.0), -exponent).astype(np.float32)
    frequency = np.tile(inverse_frequency, 2)[None, :]
    bf16, f32 = jnp.bfloat16, jnp.float32
    smem = pl.BlockSpec(memory_space=pltpu.SMEM)
    vmem = pl.BlockSpec(memory_space=pltpu.VMEM)
    anywhere = pl.BlockSpec(memory_space=pl.ANY)
    dma = pltpu.SemaphoreType.DMA
    return pl.pallas_call(
        functools.partial(kernel, pool_count, tp_count),
        out_shape=(
            jax.ShapeDtypeStruct((SUFFIX, heads * VALUE_DIM), bf16),
            jax.ShapeDtypeStruct(pool.shape, bf16),
        ),
        in_specs=[smem] * 4 + [vmem] * 2 + [anywhere] * 5,
        out_specs=(anywhere, anywhere),
        scratch_shapes=[
            pltpu.VMEM(tokens.shape, bf16),
            pltpu.VMEM(down_weight.shape, bf16),
            pltpu.VMEM((rows, WIDTH), bf16),
            pltpu.VMEM((rows, WIDE), bf16),
            pltpu.VMEM(value_weight.shape, bf16),
            pltpu.VMEM(pool.shape, bf16),
            pltpu.VMEM((2, pool_count, piece, WIDTH), bf16),
            pltpu.VMEM((pool_count, piece, WIDTH), bf16),
            pltpu.VMEM((pool_count, piece, WIDTH), bf16),
            pltpu.VMEM((tp_count, 2 * piece, WIDTH), f32),
            pltpu.VMEM((tp_count - 1, 2 * piece, WIDTH), f32),
            pltpu.VMEM((2, piece, WIDTH), bf16),
            pltpu.VMEM((2 * pool_count, piece, WIDTH), bf16),
            pltpu.VMEM((2, HALF, WIDE), bf16),
            pltpu.VMEM((2, 2, HALF, WIDE), bf16),
            pltpu.VMEM((2, HALF, WIDE), bf16),
            pltpu.VMEM((LATENT // 128, rows, 128), f32),
            pltpu.VMEM((rows, 128), f32),
            pltpu.VMEM((rows, 128), f32),
            pltpu.VMEM((SUFFIX, heads * VALUE_DIM), bf16),
            pltpu.VMEM(pool.shape, bf16),
            pltpu.VMEM((8, 128), jnp.int32),
            pltpu.SMEM((8, 128), jnp.int32),
            dma((5,)),
            dma,
            dma((2,)),
            dma((2,)),
            dma((tp_count - 1,)),
            dma((tp_count - 1,)),
            dma,
            dma,
            dma((2, 2)),
            dma((2, 2)),
            dma((2, 2)),
            dma((2, 2)),
        ],
        compiler_params=pltpu.CompilerParams(
            collective_id=0, has_side_effects=True, vmem_limit_bytes=60 * 1024 * 1024
        ),
        name="latent_attention",
    )(
        block_holder,
        block_slot,
        prefix_blocks,
        suffix_len,
        kv_gain.reshape(1, LATENT),
        jnp.asarray(frequency),
        tokens,
        down_weight,
        queries.reshape(rows, WIDTH),
        value_weight,
        pool,
    )


def solution(mesh):
    in_specs = (
        P("pool", "tp"),
        P("tp", None),
        P(),
        P("pool", "tp", None),
        P("tp", None, None),
        P("pool", "tp", None),
        P(),
        P(),
        P(),
        P(),
    )
    out_specs = (P("pool", "tp"), P("pool", "tp", None))
    return jax.shard_map(
        functools.partial(on_device, mesh.shape["pool"], mesh.shape["tp"]),
        mesh=mesh,
        in_specs=in_specs,
        out_specs=out_specs,
        check_vma=False,
    )
```

time: 268 us -> 89.5 us (0.33)
  waiting for transfers between devices: 111 us -> 0 us
  Pallas kernels: 0 us -> 70.7 us
  matrix products: 52.3 us -> 0 us
  other arithmetic: 38 us -> 0 us
  local copies, waits for them, and re-layouts: 35.8 us -> 16.5 us
  between operations: 15 us -> 0.65 us
  starting transfers between devices: 11.9 us -> 0 us
    psum x1 -> x0, waiting for transfers between devices: 71.3 us -> none  [on_device(): total = lax.psum(partial_latent, 'tp')]
    pallas_call x0 -> x1, Pallas kernels: none -> 70.7 us  [on_device(): pl.pallas_call(functools.partial(kernel, pool_count, tp_count), out_shape...]
    dot_general x9 -> x0, matrix products: 52.3 us -> none  [the longest x4 30.7 us: one_group(): jnp.einsum('tnu,tux->ntx', mixed_output, value_portion, preferred_element...]
    all_gather x1 -> x0, waiting for transfers between devices: 39.3 us -> none  [on_device(): every_new = lax.all_gather(own_rows, 'pool', axis=0, tiled=True)]
    sub x6 -> x0, other arithmetic: 23.6 us -> none  [the longest x4 22.7 us: one_group(): exponent = jnp.exp(scores - highest)]
    unnamed x24 -> x6, local copies, waits for them, and re-layouts: 4.88 us -> 16.5 us
    all_to_all x1 -> x0, starting transfers between devices: 11.6 us -> none  [on_device(): lax.all_to_all(copies, ('pool', 'tp'), split_axis=0, concat_axis=2, tiled...]
    gather x10 -> x0, local copies, waits for them, and re-layouts: 8.8 us -> none  [the longest x1 4.86 us: on_device(): jnp.take(arrived, token_position, axis=0)]
  transfers between devices with their start and end apart: 3 -> 0, of which waited for: 2 -> 0; matrix products, arithmetic and copies ran while one was open for 7% -> 0% of each run, Pallas kernels for 0% -> 0%
where the time goes in v1:
time: 89.5 us; the launch traced here: 87.9 us
  Pallas kernels  70.7 us (79%)
  local copies, waits for them, and re-layouts  16.5 us (18%)
    pallas_call x1, Pallas kernels, on_device(): pl.pallas_call(functools.partial(kernel, pool_count, tp_count), out_shape...  70.7 us
    unnamed x6, local copies, waits for them, and re-layouts  16.5 us

profile of v1, /device:TPU:0, one launch (start us, length us, event | category | flops | bytes accessed | tf_op | source)
XLA Modules:
  0.0 87.9 jit_solution(16423042655518516052)
XLA Ops:
  0.6 4.1 %copy.14.down_h = bf16[1792,576]{1,0:T(8,128)(2,1)} copy(bf16[1792,576]{0,1:T(8,128)(2,1)} %param.12) | data formatting | bytes 4128768 | tf_op args[1]
  4.7 9.0 %copy.13 = bf16[128,32,576]{2,1,0:T(8,128)(2,1)} copy(bf16[128,32,576]{0,2,1:T(8,128)(2,1)} %param.14) | data formatting | bytes 9437184 | tf_op args[3]
  13.7 70.7 %latent_attention.1 = (bf16[128,4096]{1,0:T(8,128)(2,1)}, bf16[64,16,576]{2,1,0:T(8,128)(2,1)}) custom-call(s32[32,32]{1,0:T(8,128)} %holder.1, s32[32,32]{1,0:T(8,128)} %slot.1, s32[32]{0:T(128)} %prefix.1, s32[32]{0:T(128)} %length.1, f32[1,512]{1,0:T(1,128)} %bitcast.3, f32[1,64]{1,0:T(1,128)} %constant.2.clone.frequency, bf16[128,1792]{1,0:T(8,128)(2,1)} %tokens_h.1, ...), custom_call_target="tpu_custom_call" | custom-call | tf_op jit(solution)/shard_map/latent_attention/pallas_call | solution.py:431
  84.4 0.0 copy-start
  84.4 2.4 %copy.17 = bf16[128,4096]{1,0:T(8,128)(2,1)} copy(bf16[128,4096]{1,0:T(8,128)(2,1)} %get-tuple-element.4) | data formatting | bytes 2097152
  86.8 0.0 copy-done
  86.8 1.1 %copy.18 = bf16[64,16,576]{2,1,0:T(8,128)(2,1)} copy(bf16[64,16,576]{2,1,0:T(8,128)(2,1)S(1)} %copy-done) | data formatting | bytes 2359296
Async XLA Ops:
  84.4 2.4 %copy-start = (bf16[64,16,576]{2,1,0:T(8,128)(2,1)S(1)}, bf16[64,16,576]{2,1,0:T(8,128)(2,1)}, u32[]{:S(2)}) copy-start(bf16[64,16,576]{2,1,0:T(8,128)(2,1)} %get-tuple-element.5) | copy-start | bytes 3538948

commit v2 on v1

--- a/solution.py
+++ b/solution.py
@@ -18,7 +18,6 @@
 WIDE = 640
 ROPE = WIDTH - LATENT
 HALF = 256
-ROWS = 256
 SCALE = 192.0 ** (-0.5) * math.log2(math.e)
 HIDDEN = -1e30
 EPSILON = 1e-06
@@ -43,9 +42,9 @@
     new_pool_h,
     tokens_v,
     down_v,
-    queries_raw,
     queries,
     value_v,
+    value_t,
     pool_v,
     leaving,
     arrived_even,
@@ -57,6 +56,7 @@
     own,
     near,
     far,
+    keys_t,
     acc,
     high,
     norm,
@@ -82,11 +82,10 @@
     core, z, x = me % 2, (me // 2) % 4, me // 8
     ahead, behind = (tp + 1) % tp_count, (tp + tp_count - 1) % tp_count
     across = (tp + 2) % tp_count
-    heads = value_v.shape[0]
+    heads = queries.shape[0]
     slots = pool_v.shape[0]
     piece = pool_v.shape[1]
     groups = TABLE // 2
-    total_rows = queries.shape[0]
     arrived = (arrived_even, arrived_odd)
 
     def peer(step):
@@ -99,7 +98,7 @@
         pltpu.make_async_copy(pool_h, pool_v, load_sem.at[0]),
         pltpu.make_async_copy(tokens_h, tokens_v, load_sem.at[1]),
         pltpu.make_async_copy(down_h, down_v, load_sem.at[2]),
-        pltpu.make_async_copy(queries_h, queries_raw, load_sem.at[3]),
+        pltpu.make_async_copy(queries_h, queries.at[:, pl.ds(0, WIDTH)], load_sem.at[3]),
         pltpu.make_async_copy(value_h, value_v, load_sem.at[4]),
     ]
     for load in loads:
@@ -145,7 +144,9 @@
 
     loads[1].wait()
     loads[2].wait()
-    partial = jnp.dot(tokens_v[...], down_v[...], preferred_element_type=jnp.float32)
+    partial = lax.dot_general(
+        tokens_v[...], down_v[...], (((1,), (1,)), ((), ())), preferred_element_type=jnp.float32
+    )
     for owner in range(tp_count):
         for b in range(2):
             partial_v[owner, b * piece : (b + 1) * piece, :] = partial[
@@ -167,15 +168,12 @@
 
     send_blocks(1)
 
-    loads[3].wait()
-    lane64 = lax.broadcasted_iota(jnp.int32, (ROWS, WIDE - WIDTH), 1)
-    one_mark = jnp.where(lane64 == 0, 1.0, 0.0).astype(jnp.bfloat16)
-
-    @pl.loop(0, total_rows // ROWS)
-    def _(i):
-        rows = pl.ds(pl.multiple_of(i * ROWS, ROWS), ROWS)
-        queries[rows, :LATENT] = queries_raw[rows, :LATENT]
-        queries[rows, LATENT:] = jnp.concatenate([queries_raw[rows, LATENT:], one_mark], axis=1)
+    mark_row = lax.broadcasted_iota(jnp.int32, (WIDE - WIDTH, SUFFIX), 0)
+    one_mark = jnp.where(mark_row == 0, 1.0, 0.0).astype(jnp.bfloat16)
+
+    @pl.loop(0, heads)
+    def _(head):
+        queries[head, WIDTH:, :] = one_mark
 
     for copy in sums:
         copy.wait_recv()
@@ -238,7 +236,7 @@
     def near_copy(parity, side, to):
         return pltpu.make_async_remote_copy(
             src_ref=own.at[parity],
-            dst_ref=near.at[parity, side],
+            dst_ref=near.at[parity, pl.ds(side * HALF, HALF)],
             send_sem=near_send.at[parity, side],
             recv_sem=near_recv.at[parity, side],
             device_id=(me, to),
@@ -246,10 +244,10 @@
         )
 
     def far_copy(parity, side, to):
-        rows = pl.ds(side * (HALF // 2), HALF // 2)
+        rows = HALF // 2
         return pltpu.make_async_remote_copy(
-            src_ref=near.at[parity, side, rows],
-            dst_ref=far.at[parity, rows],
+            src_ref=near.at[parity, pl.ds(side * (HALF + rows), rows)],
+            dst_ref=far.at[pl.ds(parity * HALF + side * rows, rows)],
             send_sem=far_send.at[parity, side],
             recv_sem=far_recv.at[parity, side],
             device_id=(me, to),
@@ -261,78 +259,87 @@
             near_copy(parity, side, to).wait_recv()
             far_copy(parity, side, to).start()
 
-    row_token = lax.broadcasted_iota(jnp.int32, (ROWS, 128), 0) // heads
-    lane128 = lax.broadcasted_iota(jnp.int32, (ROWS, 128), 1)
-
-    def attend(halves, first=False, last=False):
-        def scores_of(rows):
-            query = queries[rows, :]
-            return [
-                lax.dot_general(
-                    query, keys[...], (((1,), (1,)), ((), ())), preferred_element_type=jnp.float32
-                )
-                for keys, _ in halves
-            ]
-
-        def weigh(i, rows, scores):
-            tiles = []
-            for score, (_, base) in zip(scores, halves):
-                tiles.append(score[:, :128])
-                seen_from = jnp.where(lane128 >= 128 - piece, base + lane128 - (128 - piece), -1)
-                hide = seen_from > row_token + i * (ROWS // heads)
-                tiles.append(jnp.where(hide, HIDDEN, score[:, 128:]))
-            top = functools.reduce(jnp.maximum, tiles)
-            top = jnp.max(top, axis=1, keepdims=True) * SCALE
-            if first:
-                new_high = jnp.broadcast_to(top, (ROWS, 128))
-            else:
-                old_high = high[rows, :]
-                new_high = jnp.maximum(old_high, top)
-                decay = jnp.exp2(old_high - new_high)
-            raised = [jnp.exp2(tile * SCALE - new_high) for tile in tiles]
-            count = functools.reduce(jnp.add, raised)
-            if not first:
-                count = count + norm[rows, :] * decay
-            mixed = None
-            for j, (keys, _) in enumerate(halves):
-                weights = jnp.concatenate(
-                    [r.astype(jnp.bfloat16) for r in raised[2 * j : 2 * j + 2]], axis=1
-                )
-                term = jnp.dot(weights, keys[:, :LATENT], preferred_element_type=jnp.float32)
-                mixed = term if mixed is None else mixed + term
-            if last:
-                share = 1.0 / jnp.sum(count, axis=1, keepdims=True)
-            else:
-                high[rows, :] = new_high
-                norm[rows, :] = count
-            for j in range(LATENT // 128):
-                part = mixed[:, j * 128 : (j + 1) * 128]
+    loads[3].wait()
+    loads[4].wait()
+
+    @pl.loop(0, heads)
+    def _(head):
+        value_t[head] = value_v[head].T
+
+    new_row = lax.broadcasted_iota(jnp.int32, (piece, SUFFIX), 0)
+    token_lane = lax.broadcasted_iota(jnp.int32, (piece, SUFFIX), 1)
+    live = lax.broadcasted_iota(jnp.int32, (SUFFIX, VALUE_DIM), 0) < length[me]
+
+    def attend(keys, bases, first=False, last=False):
+        count = len(bases) * HALF
+        for half in range(len(bases)):
+            rows = slice(half * HALF, (half + 1) * HALF)
+            keys_t[:, rows] = keys[rows, :LATENT].T
+        hidden = [base + new_row > token_lane for base in bases]
+
+        def scores_of(group):
+            query = jnp.concatenate([queries[head] for head in group], axis=1)
+            return jnp.dot(keys[...], query, preferred_element_type=jnp.float32)
+
+        def weigh(group, scores):
+            weights, decays, sums_of = [], [], []
+            for j, head in enumerate(group):
+                score = scores[:, j * SUFFIX : (j + 1) * SUFFIX]
+                parts = []
+                for half, hide in enumerate(hidden):
+                    end = (half + 1) * HALF
+                    parts.append(score[half * HALF : end - piece])
+                    parts.append(jnp.where(hide, HIDDEN, score[end - piece : end]))
+                score = jnp.concatenate(parts, axis=0).reshape(count // 8, 8, SUFFIX)
+                top = jnp.max(jnp.max(score, axis=0), axis=0, keepdims=True) * SCALE
+                top = jnp.broadcast_to(top, (8, SUFFIX))
                 if not first:
-                    part = part + acc[j, rows, :] * decay
+                    old = high[head]
+                    top = jnp.maximum(old, top)
+                    decay = jnp.exp2(old - top)
+                    decays.append(decay)
+                raised = jnp.exp2(score * SCALE - top[None])
+                total = jnp.sum(raised, axis=0)
+                if not first:
+                    total = total + norm[head] * decay
                 if last:
-                    part = part * share
-                acc[j, rows, :] = part
-
-        @pl.loop(0, total_rows // ROWS // 2)
-        def _(pair):
-            tiles = [2 * pair, 2 * pair + 1]
-            places = [pl.ds(pl.multiple_of(i * ROWS, ROWS), ROWS) for i in tiles]
-            scores = [scores_of(rows) for rows in places]
-            for i, rows, score in zip(tiles, places, scores):
-                weigh(i, rows, score)
+                    total = 1.0 / jnp.sum(total, axis=0, keepdims=True)
+                    sums_of.append(jnp.broadcast_to(total, (8, SUFFIX)))
+                else:
+                    high[head] = top
+                    norm[head] = total
+                weights.append(raised.reshape(count, SUFFIX).astype(jnp.bfloat16))
+            mixed = jnp.dot(
+                keys_t[:, :count],
+                jnp.concatenate(weights, axis=1),
+                preferred_element_type=jnp.float32,
+            )
+            for j, head in enumerate(group):
+                part = mixed[:, j * SUFFIX : (j + 1) * SUFFIX].reshape(LATENT // 8, 8, SUFFIX)
+                if not first:
+                    part = part + acc[head].reshape(LATENT // 8, 8, SUFFIX) * decays[j][None]
+                if last:
+                    part = (part * sums_of[j][None]).reshape(LATENT, SUFFIX).astype(jnp.bfloat16)
+                    value = jnp.dot(value_t[head], part, preferred_element_type=jnp.float32).T
+                    columns = pl.ds(pl.multiple_of(head * VALUE_DIM, VALUE_DIM), VALUE_DIM)
+                    out_v[:, columns] = jnp.where(live, value, 0.0).astype(jnp.bfloat16)
+                else:
+                    acc[head] = part.reshape(LATENT, SUFFIX)
+
+        @pl.loop(0, heads // 4)
+        def _(quad):
+            groups_of = [[4 * quad + 2 * j, 4 * quad + 2 * j + 1] for j in range(2)]
+            scores = [scores_of(group) for group in groups_of]
+            for group, score in zip(groups_of, scores):
+                weigh(group, score)
 
     gather_blocks(0)
-    attend([(own.at[0], tp * piece)], first=True)
+    attend(own.at[0], [tp * piece], first=True)
     gather_blocks(1)
-    attend([(own.at[1], BLOCK + tp * piece)])
+    attend(own.at[1], [BLOCK + tp * piece])
     for parity in range(2):
         forward(parity)
-        attend(
-            [
-                (near.at[parity, 0], parity * BLOCK + behind * piece),
-                (near.at[parity, 1], parity * BLOCK + ahead * piece),
-            ]
-        )
+        attend(near.at[parity], [parity * BLOCK + side * piece for side in (behind, ahead)])
 
     lane_slot = lax.broadcasted_iota(jnp.int32, (8, 128), 1)
 
@@ -365,27 +372,7 @@
     for parity in range(2):
         for side, to in enumerate((ahead, behind)):
             far_copy(parity, side, to).wait_recv()
-    attend(
-        [(far.at[parity], parity * BLOCK + across * piece) for parity in range(2)], last=True
-    )
-
-    loads[4].wait()
-    live = lax.broadcasted_iota(jnp.int32, (SUFFIX, VALUE_DIM), 0) < length[me]
-
-    @pl.loop(0, heads // 4)
-    def _(quad):
-        for inner in range(4):
-            head = quad * 4 + inner
-            mixed = jnp.concatenate(
-                [
-                    acc[j, pl.ds(head, SUFFIX, stride=heads), :].astype(jnp.bfloat16)
-                    for j in range(LATENT // 128)
-                ],
-                axis=1,
-            )
-            value = jnp.dot(mixed, value_v[head], preferred_element_type=jnp.float32)
-            columns = pl.ds(pl.multiple_of(head * VALUE_DIM, VALUE_DIM), VALUE_DIM)
-            out_v[:, columns] = jnp.where(live, value, 0.0).astype(jnp.bfloat16)
+    attend(far, [parity * BLOCK + across * piece for parity in range(2)], last=True)
 
     store_out = pltpu.make_async_copy(out_v, out_h, load_sem.at[1])
     store_out.start()
@@ -418,8 +405,7 @@
     suffix_len,
 ):
     heads = queries.shape[1]
-    rows = queries.shape[0] * heads
-    slots, piece, width = pool.shape
+    piece = pool.shape[1]
     exponent = np.arange(ROPE // 2).astype(np.float32) * np.float32(2.0 / ROPE)
     inverse_frequency = np.power(np.float32(10000.0), -exponent).astype(np.float32)
     frequency = np.tile(inverse_frequency, 2)[None, :]
@@ -438,10 +424,10 @@
         out_specs=(anywhere, anywhere),
         scratch_shapes=[
             pltpu.VMEM(tokens.shape, bf16),
-            pltpu.VMEM(down_weight.shape, bf16),
-            pltpu.VMEM((rows, WIDTH), bf16),
-            pltpu.VMEM((rows, WIDE), bf16),
+            pltpu.VMEM(down_weight.shape[::-1], bf16),
+            pltpu.VMEM((heads, WIDE, SUFFIX), bf16),
             pltpu.VMEM(value_weight.shape, bf16),
+            pltpu.VMEM((heads, VALUE_DIM, LATENT), bf16),
             pltpu.VMEM(pool.shape, bf16),
             pltpu.VMEM((2, pool_count, piece, WIDTH), bf16),
             pltpu.VMEM((pool_count, piece, WIDTH), bf16),
@@ -451,11 +437,12 @@
             pltpu.VMEM((2, piece, WIDTH), bf16),
             pltpu.VMEM((2 * pool_count, piece, WIDTH), bf16),
             pltpu.VMEM((2, HALF, WIDE), bf16),
-            pltpu.VMEM((2, 2, HALF, WIDE), bf16),
-            pltpu.VMEM((2, HALF, WIDE), bf16),
-            pltpu.VMEM((LATENT // 128, rows, 128), f32),
-            pltpu.VMEM((rows, 128), f32),
-            pltpu.VMEM((rows, 128), f32),
+            pltpu.VMEM((2, 2 * HALF, WIDE), bf16),
+            pltpu.VMEM((2 * HALF, WIDE), bf16),
+            pltpu.VMEM((LATENT, 2 * HALF), bf16),
+            pltpu.VMEM((heads, LATENT, SUFFIX), f32),
+            pltpu.VMEM((heads, 8, SUFFIX), f32),
+            pltpu.VMEM((heads, 8, SUFFIX), f32),
             pltpu.VMEM((SUFFIX, heads * VALUE_DIM), bf16),
             pltpu.VMEM(pool.shape, bf16),
             pltpu.VMEM((8, 128), jnp.int32),
@@ -485,8 +472,8 @@
         kv_gain.reshape(1, LATENT),
         jnp.asarray(frequency),
         tokens,
-        down_weight,
-        queries.reshape(rows, WIDTH),
+        down_weight.T,
+        queries.transpose(1, 2, 0),
         value_weight,
         pool,
     )

time: 89.5 us -> 80.5 us (0.90)
  local copies, waits for them, and re-layouts: 16.5 us -> 3.45 us
  Pallas kernels: 70.7 us -> 75.6 us
    unnamed x6 -> x4, local copies, waits for them, and re-layouts: 16.5 us -> 3.45 us
    pallas_call x1, Pallas kernels: 70.7 us -> 75.6 us  [on_device(): pl.pallas_call(functools.partial(kernel, pool_count, tp_count), out_shape...]
where the time goes in v2:
time: 80.5 us; the launch traced here: 79.7 us
  Pallas kernels  75.6 us (94%)
  local copies, waits for them, and re-layouts  3.45 us (4%)
    pallas_call x1, Pallas kernels, on_device(): pl.pallas_call(functools.partial(kernel, pool_count, tp_count), out_shape...  75.6 us
    unnamed x4, local copies, waits for them, and re-layouts  3.45 us

profile of v2, /device:TPU:0, one launch (start us, length us, event | category | flops | bytes accessed | tf_op | source)
XLA Modules:
  0.0 79.7 jit_solution(10230507497731606351)
XLA Ops:
  0.6 75.6 %latent_attention.1 = (bf16[128,4096]{1,0:T(8,128)(2,1)}, bf16[64,16,576]{2,1,0:T(8,128)(2,1)}) custom-call(s32[32,32]{1,0:T(8,128)} %holder.1, s32[32,32]{1,0:T(8,128)} %slot.1, s32[32]{0:T(128)} %prefix.1, s32[32]{0:T(128)} %length.1, f32[1,512]{1,0:T(1,128)} %bitcast.5, f32[1,64]{1,0:T(1,128)} %constant.2.clone.frequency, bf16[128,1792]{1,0:T(8,128)(2,1)} %tokens_h.1, ...), custom_call_target="tpu_custom_call" | custom-call | tf_op jit(solution)/shard_map/latent_attention/pallas_call | solution.py:417
  76.3 0.0 copy-start
  76.3 2.4 %copy.15 = bf16[128,4096]{1,0:T(8,128)(2,1)} copy(bf16[128,4096]{1,0:T(8,128)(2,1)} %get-tuple-element.4) | data formatting | bytes 2097152
  78.7 0.0 copy-done
  78.7 1.1 %copy.16 = bf16[64,16,576]{2,1,0:T(8,128)(2,1)} copy(bf16[64,16,576]{2,1,0:T(8,128)(2,1)S(1)} %copy-done) | data formatting | bytes 2359296
Async XLA Ops:
  76.3 2.4 %copy-start = (bf16[64,16,576]{2,1,0:T(8,128)(2,1)S(1)}, bf16[64,16,576]{2,1,0:T(8,128)(2,1)}, u32[]{:S(2)}) copy-start(bf16[64,16,576]{2,1,0:T(8,128)(2,1)} %get-tuple-element.5) | copy-start | bytes 3538948

commit v3 on v2

--- a/solution.py
+++ b/solution.py
@@ -51,7 +51,6 @@
     arrived_odd,
     partial_v,
     partial_in,
-    fresh,
     fresh_in,
     own,
     near,
@@ -64,6 +63,7 @@
     new_pool_v,
     index_v,
     index_s,
+    entry_s,
     load_sem,
     index_sem,
     block_send,
@@ -118,17 +118,19 @@
 
     loads[0].wait()
 
-    def wanted(request):
-        at = jnp.int32(0)
-        for k in range(groups - 1):
-            at = jnp.where(holder[request, 2 * k] == me, 2 * k, at)
-        return at
+    def wanted(request, parity):
+        if parity == 0:
+            at = jnp.int32(0)
+            for k in range(groups - 1):
+                at = jnp.where(holder[request, 2 * k] == me, 2 * k, at)
+            entry_s[request] = at
+        return slot[request, entry_s[request] + parity]
 
     def send_blocks(parity):
         @pl.loop(1, pool_count)
         def _(step):
             request = peer(step)
-            leaving[parity, request] = pool_v[slot[request, wanted(request) + parity]]
+            leaving[parity, request] = pool_v[wanted(request, parity)]
             pltpu.make_async_remote_copy(
                 src_ref=leaving.at[parity, request],
                 dst_ref=arrived[parity].at[me],
@@ -138,7 +140,7 @@
                 device_id_type=MESH,
             ).start()
 
-        arrived[parity][me] = pool_v[slot[me, wanted(me) + parity]]
+        arrived[parity][me] = pool_v[wanted(me, parity)]
 
     send_blocks(0)
 
@@ -193,27 +195,56 @@
     token512 = (row512 // piece) * BLOCK + tp * piece + row512 % piece
     normed = jnp.where(token512 < length[me], normed, 0.0).astype(jnp.bfloat16)
     turned = jnp.where(token < length[me], turned, 0.0)
+    fresh_at = 2 * ((core * 4 + z) * 4 + x)
     plain = jnp.zeros((piece, WIDE - WIDTH), jnp.float32)
     for b in range(2):
         rows = slice(b * piece, (b + 1) * piece)
         last = jnp.concatenate([turned[rows], plain], axis=1).astype(jnp.bfloat16)
-        fresh[b, :, :LATENT] = normed[rows]
-        fresh[b, :, LATENT:] = last[:, :ROPE]
+        fresh_in[fresh_at + b, :, :LATENT] = normed[rows]
+        fresh_in[fresh_at + b, :, LATENT:] = last[:, :ROPE]
         own[b, (groups - 1) * piece : groups * piece, :LATENT] = normed[rows]
         own[b, (groups - 1) * piece : groups * piece, LATENT:] = last
 
-    @pl.loop(1, pool_count)
-    def _(step):
-        pltpu.make_async_remote_copy(
-            src_ref=fresh,
-            dst_ref=fresh_in.at[pl.ds(2 * me, 2)],
-            send_sem=fresh_send,
-            recv_sem=fresh_recv,
-            device_id=(peer(step), tp),
+    def fresh_place(at_core, at_z, at_x):
+        return 2 * ((at_core * 4 + at_z) * 4 + at_x)
+
+    def along_x(step):
+        here = fresh_in.at[pl.ds(fresh_place(core, z, x), 2)]
+        to = (((x + step) % 4) * 4 + z) * 2 + core
+        return pltpu.make_async_remote_copy(
+            src_ref=here,
+            dst_ref=here,
+            send_sem=fresh_send.at[step - 1],
+            recv_sem=fresh_recv.at[step - 1],
+            device_id=(to, tp),
             device_id_type=MESH,
-        ).start()
-
-    fresh_in[pl.ds(2 * me, 2)] = fresh[...]
+        )
+
+    def along_z(step):
+        here = fresh_in.at[pl.ds(fresh_place(core, z, 0), 8)]
+        to = (x * 4 + (z + step) % 4) * 2 + core
+        return pltpu.make_async_remote_copy(
+            src_ref=here,
+            dst_ref=here,
+            send_sem=fresh_send.at[step + 2],
+            recv_sem=fresh_recv.at[step + 2],
+            device_id=(to, tp),
+            device_id_type=MESH,
+        )
+
+    def to_other_core():
+        here = fresh_in.at[pl.ds(fresh_place(core, 0, 0), 32)]
+        return pltpu.make_async_remote_copy(
+            src_ref=here,
+            dst_ref=here,
+            send_sem=fresh_send.at[6],
+            recv_sem=fresh_recv.at[6],
+            device_id=((x * 4 + z) * 2 + 1 - core, tp),
+            device_id_type=MESH,
+        )
+
+    for step in range(1, 4):
+        along_x(step).start()
 
     lane_mark = lax.broadcasted_iota(jnp.int32, (piece, WIDE - WIDTH), 1)
 
@@ -337,9 +368,25 @@
     attend(own.at[0], [tp * piece], first=True)
     gather_blocks(1)
     attend(own.at[1], [BLOCK + tp * piece])
+    for step in range(1, 4):
+        along_x(step).wait_recv()
+    for step in range(1, 4):
+        along_z(step).start()
     for parity in range(2):
         forward(parity)
         attend(near.at[parity], [parity * BLOCK + side * piece for side in (behind, ahead)])
+
+    for step in range(1, 4):
+        along_z(step).wait_recv()
+    to_other_core().start()
+
+    for parity in range(2):
+        for side, to in enumerate((ahead, behind)):
+            far_copy(parity, side, to).wait_recv()
+    attend(far, [parity * BLOCK + across * piece for parity in range(2)], last=True)
+
+    store_out = pltpu.make_async_copy(out_v, out_h, load_sem.at[1])
+    store_out.start()
 
     lane_slot = lax.broadcasted_iota(jnp.int32, (8, 128), 1)
 
@@ -348,14 +395,13 @@
             entry = prefix[request] + b
             here = holder[request, entry] == me
             target = jnp.where(here, slot[request, entry], -1)
-            index = jnp.where(lane_slot == target, 2 * request + b, index)
+            index = jnp.where(lane_slot == target, fresh_place(request % 2, (request // 2) % 4, request // 8) + b, index)
         return index
 
     index_v[...] = lax.fori_loop(0, pool_count, mark_slot, jnp.full((8, 128), -1, jnp.int32))
     to_scalars = pltpu.make_async_copy(index_v, index_s, index_sem)
     to_scalars.start()
-    arrivals = fresh_in.at[pl.ds(0, 2 * (pool_count - 1))]
-    pltpu.make_async_copy(arrivals, arrivals, fresh_recv).wait()
+    to_other_core().wait_recv()
     to_scalars.wait()
 
     @pl.loop(0, slots)
@@ -369,13 +415,6 @@
     store_pool = pltpu.make_async_copy(new_pool_v, new_pool_h, load_sem.at[0])
     store_pool.start()
 
-    for parity in range(2):
-        for side, to in enumerate((ahead, behind)):
-            far_copy(parity, side, to).wait_recv()
-    attend(far, [parity * BLOCK + across * piece for parity in range(2)], last=True)
-
-    store_out = pltpu.make_async_copy(out_v, out_h, load_sem.at[1])
-    store_out.start()
 
     for copy in sums:
         copy.wait_send()
@@ -385,7 +424,10 @@
         for side, to in enumerate((ahead, behind)):
             near_copy(parity, side, to).wait_send()
             far_copy(parity, side, to).wait_send()
-    pltpu.make_async_copy(arrivals, arrivals, fresh_send).wait()
+    for step in range(1, 4):
+        along_x(step).wait_send()
+        along_z(step).wait_send()
+    to_other_core().wait_send()
     store_pool.wait()
     store_out.wait()
 
@@ -434,7 +476,6 @@
             pltpu.VMEM((pool_count, piece, WIDTH), bf16),
             pltpu.VMEM((tp_count, 2 * piece, WIDTH), f32),
             pltpu.VMEM((tp_count - 1, 2 * piece, WIDTH), f32),
-            pltpu.VMEM((2, piece, WIDTH), bf16),
             pltpu.VMEM((2 * pool_count, piece, WIDTH), bf16),
             pltpu.VMEM((2, HALF, WIDE), bf16),
             pltpu.VMEM((2, 2 * HALF, WIDE), bf16),
@@ -447,14 +488,15 @@
             pltpu.VMEM(pool.shape, bf16),
             pltpu.VMEM((8, 128), jnp.int32),
             pltpu.SMEM((8, 128), jnp.int32),
+            pltpu.SMEM((pool_count,), jnp.int32),
             dma((5,)),
             dma,
             dma((2,)),
             dma((2,)),
             dma((tp_count - 1,)),
             dma((tp_count - 1,)),
-            dma,
-            dma,
+            dma((7,)),
+            dma((7,)),
             dma((2, 2)),
             dma((2, 2)),
             dma((2, 2)),

time: 80.5 us -> 80 us (level)
  no operation moved by 1% of the time
where the time goes in v3:
time: 80 us; the launch traced here: 79.2 us
  Pallas kernels  75.1 us (94%)
  local copies, waits for them, and re-layouts  3.45 us (4%)
    pallas_call x1, Pallas kernels, on_device(): pl.pallas_call(functools.partial(kernel, pool_count, tp_count), out_shape...  75.1 us
    unnamed x4, local copies, waits for them, and re-layouts  3.45 us

profile of v3, /device:TPU:0, one launch (start us, length us, event | category | flops | bytes accessed | tf_op | source)
XLA Modules:
  0.0 79.2 jit_solution(8793534690060059079)
XLA Ops:
  0.6 75.1 %latent_attention.1 = (bf16[128,4096]{1,0:T(8,128)(2,1)}, bf16[64,16,576]{2,1,0:T(8,128)(2,1)}) custom-call(s32[32,32]{1,0:T(8,128)} %holder.1, s32[32,32]{1,0:T(8,128)} %slot.1, s32[32]{0:T(128)} %prefix.1, s32[32]{0:T(128)} %length.1, f32[1,512]{1,0:T(1,128)} %bitcast.5, f32[1,64]{1,0:T(1,128)} %constant.2.clone.frequency, bf16[128,1792]{1,0:T(8,128)(2,1)} %tokens_h.1, ...), custom_call_target="tpu_custom_call" | custom-call | tf_op jit(solution)/shard_map/latent_attention/pallas_call | solution.py:459
  75.8 0.0 copy-start
  75.8 2.4 %copy.15 = bf16[128,4096]{1,0:T(8,128)(2,1)} copy(bf16[128,4096]{1,0:T(8,128)(2,1)} %get-tuple-element.4) | data formatting | bytes 2097152
  78.2 0.0 copy-done
  78.2 1.1 %copy.16 = bf16[64,16,576]{2,1,0:T(8,128)(2,1)} copy(bf16[64,16,576]{2,1,0:T(8,128)(2,1)S(1)} %copy-done) | data formatting | bytes 2359296
Async XLA Ops:
  75.8 2.4 %copy-start = (bf16[64,16,576]{2,1,0:T(8,128)(2,1)S(1)}, bf16[64,16,576]{2,1,0:T(8,128)(2,1)}, u32[]{:S(2)}) copy-start(bf16[64,16,576]{2,1,0:T(8,128)(2,1)} %get-tuple-element.5) | copy-start | bytes 3538948

commit v4 on v3

--- a/solution.py
+++ b/solution.py
@@ -35,16 +35,11 @@
     frequency,
     tokens_h,
     down_h,
-    queries_h,
-    value_h,
     pool_h,
-    out_h,
+    keys_h,
     new_pool_h,
     tokens_v,
     down_v,
-    queries,
-    value_v,
-    value_t,
     pool_v,
     leaving,
     arrived_even,
@@ -55,11 +50,6 @@
     own,
     near,
     far,
-    keys_t,
-    acc,
-    high,
-    norm,
-    out_v,
     new_pool_v,
     index_v,
     index_s,
@@ -82,7 +72,6 @@
     core, z, x = me % 2, (me // 2) % 4, me // 8
     ahead, behind = (tp + 1) % tp_count, (tp + tp_count - 1) % tp_count
     across = (tp + 2) % tp_count
-    heads = queries.shape[0]
     slots = pool_v.shape[0]
     piece = pool_v.shape[1]
     groups = TABLE // 2
@@ -98,8 +87,6 @@
         pltpu.make_async_copy(pool_h, pool_v, load_sem.at[0]),
         pltpu.make_async_copy(tokens_h, tokens_v, load_sem.at[1]),
         pltpu.make_async_copy(down_h, down_v, load_sem.at[2]),
-        pltpu.make_async_copy(queries_h, queries.at[:, pl.ds(0, WIDTH)], load_sem.at[3]),
-        pltpu.make_async_copy(value_h, value_v, load_sem.at[4]),
     ]
     for load in loads:
         load.start()
@@ -170,13 +157,6 @@
 
     send_blocks(1)
 
-    mark_row = lax.broadcasted_iota(jnp.int32, (WIDE - WIDTH, SUFFIX), 0)
-    one_mark = jnp.where(mark_row == 0, 1.0, 0.0).astype(jnp.bfloat16)
-
-    @pl.loop(0, heads)
-    def _(head):
-        queries[head, WIDTH:, :] = one_mark
-
     for copy in sums:
         copy.wait_recv()
     latent = partial_v[tp] + partial_in[0] + partial_in[1] + partial_in[2]
@@ -196,7 +176,8 @@
     normed = jnp.where(token512 < length[me], normed, 0.0).astype(jnp.bfloat16)
     turned = jnp.where(token < length[me], turned, 0.0)
     fresh_at = 2 * ((core * 4 + z) * 4 + x)
-    plain = jnp.zeros((piece, WIDE - WIDTH), jnp.float32)
+    lane_plain = lax.broadcasted_iota(jnp.int32, (piece, WIDE - WIDTH), 1)
+    plain = jnp.where(lane_plain == 0, HIDDEN, 0.0)
     for b in range(2):
         rows = slice(b * piece, (b + 1) * piece)
         last = jnp.concatenate([turned[rows], plain], axis=1).astype(jnp.bfloat16)
@@ -278,7 +259,7 @@
         rows = HALF // 2
         return pltpu.make_async_remote_copy(
             src_ref=near.at[parity, pl.ds(side * (HALF + rows), rows)],
-            dst_ref=far.at[pl.ds(parity * HALF + side * rows, rows)],
+            dst_ref=far.at[parity, pl.ds(side * rows, rows)],
             send_sem=far_send.at[parity, side],
             recv_sem=far_recv.at[parity, side],
             device_id=(me, to),
@@ -290,103 +271,17 @@
             near_copy(parity, side, to).wait_recv()
             far_copy(parity, side, to).start()
 
-    loads[3].wait()
-    loads[4].wait()
-
-    @pl.loop(0, heads)
-    def _(head):
-        value_t[head] = value_v[head].T
-
-    new_row = lax.broadcasted_iota(jnp.int32, (piece, SUFFIX), 0)
-    token_lane = lax.broadcasted_iota(jnp.int32, (piece, SUFFIX), 1)
-    live = lax.broadcasted_iota(jnp.int32, (SUFFIX, VALUE_DIM), 0) < length[me]
-
-    def attend(keys, bases, first=False, last=False):
-        count = len(bases) * HALF
-        for half in range(len(bases)):
-            rows = slice(half * HALF, (half + 1) * HALF)
-            keys_t[:, rows] = keys[rows, :LATENT].T
-        hidden = [base + new_row > token_lane for base in bases]
-
-        def scores_of(group):
-            query = jnp.concatenate([queries[head] for head in group], axis=1)
-            return jnp.dot(keys[...], query, preferred_element_type=jnp.float32)
-
-        def weigh(group, scores):
-            weights, decays, sums_of = [], [], []
-            for j, head in enumerate(group):
-                score = scores[:, j * SUFFIX : (j + 1) * SUFFIX]
-                parts = []
-                for half, hide in enumerate(hidden):
-                    end = (half + 1) * HALF
-                    parts.append(score[half * HALF : end - piece])
-                    parts.append(jnp.where(hide, HIDDEN, score[end - piece : end]))
-                score = jnp.concatenate(parts, axis=0).reshape(count // 8, 8, SUFFIX)
-                top = jnp.max(jnp.max(score, axis=0), axis=0, keepdims=True) * SCALE
-                top = jnp.broadcast_to(top, (8, SUFFIX))
-                if not first:
-                    old = high[head]
-                    top = jnp.maximum(old, top)
-                    decay = jnp.exp2(old - top)
-                    decays.append(decay)
-                raised = jnp.exp2(score * SCALE - top[None])
-                total = jnp.sum(raised, axis=0)
-                if not first:
-                    total = total + norm[head] * decay
-                if last:
-                    total = 1.0 / jnp.sum(total, axis=0, keepdims=True)
-                    sums_of.append(jnp.broadcast_to(total, (8, SUFFIX)))
-                else:
-                    high[head] = top
-                    norm[head] = total
-                weights.append(raised.reshape(count, SUFFIX).astype(jnp.bfloat16))
-            mixed = jnp.dot(
-                keys_t[:, :count],
-                jnp.concatenate(weights, axis=1),
-                preferred_element_type=jnp.float32,
-            )
-            for j, head in enumerate(group):
-                part = mixed[:, j * SUFFIX : (j + 1) * SUFFIX].reshape(LATENT // 8, 8, SUFFIX)
-                if not first:
-                    part = part + acc[head].reshape(LATENT // 8, 8, SUFFIX) * decays[j][None]
-                if last:
-                    part = (part * sums_of[j][None]).reshape(LATENT, SUFFIX).astype(jnp.bfloat16)
-                    value = jnp.dot(value_t[head], part, preferred_element_type=jnp.float32).T
-                    columns = pl.ds(pl.multiple_of(head * VALUE_DIM, VALUE_DIM), VALUE_DIM)
-                    out_v[:, columns] = jnp.where(live, value, 0.0).astype(jnp.bfloat16)
-                else:
-                    acc[head] = part.reshape(LATENT, SUFFIX)
-
-        @pl.loop(0, heads // 4)
-        def _(quad):
-            groups_of = [[4 * quad + 2 * j, 4 * quad + 2 * j + 1] for j in range(2)]
-            scores = [scores_of(group) for group in groups_of]
-            for group, score in zip(groups_of, scores):
-                weigh(group, score)
-
     gather_blocks(0)
-    attend(own.at[0], [tp * piece], first=True)
     gather_blocks(1)
-    attend(own.at[1], [BLOCK + tp * piece])
     for step in range(1, 4):
         along_x(step).wait_recv()
     for step in range(1, 4):
         along_z(step).start()
     for parity in range(2):
         forward(parity)
-        attend(near.at[parity], [parity * BLOCK + side * piece for side in (behind, ahead)])
-
     for step in range(1, 4):
         along_z(step).wait_recv()
     to_other_core().start()
-
-    for parity in range(2):
-        for side, to in enumerate((ahead, behind)):
-            far_copy(parity, side, to).wait_recv()
-    attend(far, [parity * BLOCK + across * piece for parity in range(2)], last=True)
-
-    store_out = pltpu.make_async_copy(out_v, out_h, load_sem.at[1])
-    store_out.start()
 
     lane_slot = lax.broadcasted_iota(jnp.int32, (8, 128), 1)
 
@@ -414,6 +309,20 @@
 
     store_pool = pltpu.make_async_copy(new_pool_v, new_pool_h, load_sem.at[0])
     store_pool.start()
+
+    store_keys = [pltpu.make_async_copy(own, keys_h.at[tp], load_sem.at[1])]
+    for side, (to, source) in enumerate(((ahead, behind), (behind, ahead))):
+        store_keys.append(
+            pltpu.make_async_copy(
+                near.at[:, pl.ds(side * HALF, HALF)], keys_h.at[source], load_sem.at[2 + side]
+            )
+        )
+    for parity in range(2):
+        for side, to in enumerate((ahead, behind)):
+            far_copy(parity, side, to).wait_recv()
+    store_keys.append(pltpu.make_async_copy(far, keys_h.at[across], load_sem.at[4]))
+    for store in store_keys:
+        store.start()
 
 
     for copy in sums:
@@ -429,7 +338,94 @@
         along_z(step).wait_send()
     to_other_core().wait_send()
     store_pool.wait()
-    store_out.wait()
+    for store in store_keys:
+        store.wait()
+
+
+def attention(prefix, length, keys, queries, values, out, keys_t, scores_v, acc):
+    heads = queries.shape[0]
+    pieces = keys.shape[0]
+    piece = BLOCK // pieces
+    span = 4 * piece
+    chunk = 2 * pieces * span
+    me = lax.axis_index("pool")
+    fresh_count = 2 * BLOCK
+
+    @pl.when(pl.program_id(0) == 0)
+    def _():
+        for c in range(HALF // span):
+            rows = keys[:, :, c * span : (c + 1) * span, :LATENT].reshape(chunk, LATENT)
+            keys_t[c] = rows.T
+        rows = keys[:, :, HALF - piece :, :LATENT].reshape(fresh_count, LATENT)
+        keys_t[HALF // span, :, :fresh_count] = rows.T
+
+    mark_row = lax.broadcasted_iota(jnp.int32, (WIDE - WIDTH, 2 * SUFFIX), 0)
+    one_mark = jnp.where(mark_row == 0, 1.0, 0.0).astype(jnp.bfloat16)
+    pairs = [(j, j + 1) for j in range(0, heads, 2)]
+    query = [jnp.concatenate([queries[a], queries[b]], axis=1) for a, b in pairs]
+
+    def weigh(score, high, norm):
+        count = score.shape[0]
+        score = score.reshape(count // 8, 8, 2 * SUFFIX)
+        top = jnp.max(jnp.max(score, axis=0), axis=0, keepdims=True) * SCALE
+        top = jnp.broadcast_to(top, (8, 2 * SUFFIX))
+        decay = None
+        if high is not None:
+            top = jnp.maximum(high, top)
+            decay = jnp.exp2(high - top)
+        raised = jnp.exp2(score * SCALE - top[None])
+        total = jnp.sum(raised, axis=0)
+        if norm is not None:
+            total = total + norm * decay
+        return raised.reshape(count, 2 * SUFFIX).astype(jnp.bfloat16), top, total, decay
+
+    fresh_keys = keys[:, :, HALF - piece :, :].reshape(fresh_count, WIDE)[:, :WIDTH]
+    row = lax.broadcasted_iota(jnp.int32, (fresh_count, 2 * SUFFIX), 0)
+    lane = lax.broadcasted_iota(jnp.int32, (fresh_count, 2 * SUFFIX), 1) % SUFFIX
+    token = (row // piece % 2) * BLOCK + (row // (2 * piece)) * piece + row % piece
+    state = []
+    for j in range(len(pairs)):
+        score = jnp.dot(fresh_keys, query[j], preferred_element_type=jnp.float32)
+        score = jnp.where(token > lane, HIDDEN, score)
+        weights, top, total, _ = weigh(score, None, None)
+        acc[j] = jnp.dot(
+            keys_t[HALF // span, :, :fresh_count], weights, preferred_element_type=jnp.float32
+        )
+        state += [top, total]
+
+    chunks = ((prefix[me] + 1) // 2 * piece + span - 1) // span
+    wide = [jnp.concatenate([q, one_mark], axis=0) for q in query]
+
+    def step(c, state):
+        rows = pl.ds(pl.multiple_of(c * span, span), span)
+        here = keys[:, :, rows, :].reshape(chunk, WIDE)
+        for j in range(len(pairs)):
+            scores_v[j] = jnp.dot(here, wide[j], preferred_element_type=jnp.float32)
+        after = []
+        for j in range(len(pairs)):
+            weights, top, total, decay = weigh(scores_v[j], state[2 * j], state[2 * j + 1])
+            mixed = jnp.dot(keys_t[c], weights, preferred_element_type=jnp.float32)
+            old = acc[j].reshape(LATENT // 8, 8, 2 * SUFFIX) * decay[None]
+            acc[j] = old.reshape(LATENT, 2 * SUFFIX) + mixed
+            after += [top, total]
+        return tuple(after)
+
+    state = lax.fori_loop(0, chunks, step, tuple(state))
+
+    live = lax.broadcasted_iota(jnp.int32, (SUFFIX, VALUE_DIM), 0) < length[me]
+    for j, pair in enumerate(pairs):
+        share = 1.0 / jnp.sum(state[2 * j + 1], axis=0, keepdims=True)
+        mixed = (acc[j] * share).astype(jnp.bfloat16)
+        for side, head in enumerate(pair):
+            value = lax.dot_general(
+                mixed[:, side * SUFFIX : (side + 1) * SUFFIX],
+                values[head],
+                (((0,), (0,)), ((), ())),
+                preferred_element_type=jnp.float32,
+            )
+            out[:, head * VALUE_DIM : (head + 1) * VALUE_DIM] = jnp.where(live, value, 0.0).astype(
+                jnp.bfloat16
+            )
 
 
 def on_device(
@@ -456,20 +452,17 @@
     vmem = pl.BlockSpec(memory_space=pltpu.VMEM)
     anywhere = pl.BlockSpec(memory_space=pl.ANY)
     dma = pltpu.SemaphoreType.DMA
-    return pl.pallas_call(
+    keys, new_pool = pl.pallas_call(
         functools.partial(kernel, pool_count, tp_count),
         out_shape=(
-            jax.ShapeDtypeStruct((SUFFIX, heads * VALUE_DIM), bf16),
+            jax.ShapeDtypeStruct((tp_count, 2, HALF, WIDE), bf16),
             jax.ShapeDtypeStruct(pool.shape, bf16),
         ),
-        in_specs=[smem] * 4 + [vmem] * 2 + [anywhere] * 5,
+        in_specs=[smem] * 4 + [vmem] * 2 + [anywhere] * 3,
         out_specs=(anywhere, anywhere),
         scratch_shapes=[
             pltpu.VMEM(tokens.shape, bf16),
             pltpu.VMEM(down_weight.shape[::-1], bf16),
-            pltpu.VMEM((heads, WIDE, SUFFIX), bf16),
-            pltpu.VMEM(value_weight.shape, bf16),
-            pltpu.VMEM((heads, VALUE_DIM, LATENT), bf16),
             pltpu.VMEM(pool.shape, bf16),
             pltpu.VMEM((2, pool_count, piece, WIDTH), bf16),
             pltpu.VMEM((pool_count, piece, WIDTH), bf16),
@@ -479,12 +472,7 @@
             pltpu.VMEM((2 * pool_count, piece, WIDTH), bf16),
             pltpu.VMEM((2, HALF, WIDE), bf16),
             pltpu.VMEM((2, 2 * HALF, WIDE), bf16),
-            pltpu.VMEM((2 * HALF, WIDE), bf16),
-            pltpu.VMEM((LATENT, 2 * HALF), bf16),
-            pltpu.VMEM((heads, LATENT, SUFFIX), f32),
-            pltpu.VMEM((heads, 8, SUFFIX), f32),
-            pltpu.VMEM((heads, 8, SUFFIX), f32),
-            pltpu.VMEM((SUFFIX, heads * VALUE_DIM), bf16),
+            pltpu.VMEM((2, HALF, WIDE), bf16),
             pltpu.VMEM(pool.shape, bf16),
             pltpu.VMEM((8, 128), jnp.int32),
             pltpu.SMEM((8, 128), jnp.int32),
@@ -505,7 +493,7 @@
         compiler_params=pltpu.CompilerParams(
             collective_id=0, has_side_effects=True, vmem_limit_bytes=60 * 1024 * 1024
         ),
-        name="latent_attention",
+        name="move_blocks",
     )(
         block_holder,
         block_slot,
@@ -515,10 +503,32 @@
         jnp.asarray(frequency),
         tokens,
         down_weight.T,
-        queries.transpose(1, 2, 0),
-        value_weight,
         pool,
     )
+    group = 4
+    spec = pltpu.PrefetchScalarGridSpec(
+        num_scalar_prefetch=2,
+        grid=(heads // group,),
+        in_specs=[
+            pl.BlockSpec((tp_count, 2, HALF, WIDE), lambda i, *_: (0, 0, 0, 0)),
+            pl.BlockSpec((group, WIDTH, SUFFIX), lambda i, *_: (i, 0, 0)),
+            pl.BlockSpec((group, LATENT, VALUE_DIM), lambda i, *_: (i, 0, 0)),
+        ],
+        out_specs=pl.BlockSpec((SUFFIX, group * VALUE_DIM), lambda i, *_: (0, i)),
+        scratch_shapes=[
+            pltpu.VMEM((5, LATENT, 2 * HALF), bf16),
+            pltpu.VMEM((group // 2, 2 * HALF, 2 * SUFFIX), f32),
+            pltpu.VMEM((group // 2, LATENT, 2 * SUFFIX), f32),
+        ],
+    )
+    attn_out = pl.pallas_call(
+        attention,
+        out_shape=jax.ShapeDtypeStruct((SUFFIX, heads * VALUE_DIM), bf16),
+        grid_spec=spec,
+        compiler_params=pltpu.CompilerParams(vmem_limit_bytes=48 * 1024 * 1024),
+        name="attend",
+    )(prefix_blocks, suffix_len, keys, queries.transpose(1, 2, 0), value_weight)
+    return attn_out, new_pool
 
 
 def solution(mesh):

time: 80 us -> 99.4 us (1.24)
  the two profiles are of different devices: /device:TPU:0 before, /device:TPU:99 now
where the time goes in v4:
time: 99.4 us; the launch traced here: 99.1 us
  Pallas kernels  95.7 us (96%)
  local copies, waits for them, and re-layouts  2.8 us (3%)
    pallas_call x1, Pallas kernels, on_device(): pl.pallas_call(attention, out_shape=jax.ShapeDtypeStruct((SUFFIX, heads *...  50.8 us
    pallas_call x1, Pallas kernels, on_device(): pl.pallas_call(functools.partial(kernel, pool_count, tp_count), out_shape...  44.8 us
    unnamed x9, local copies, waits for them, and re-layouts  2.8 us

profile of v4, /device:TPU:99, one launch (start us, length us, event | category | flops | bytes accessed | tf_op | source)
XLA Modules:
  0.0 99.1 jit_solution(11470278890869827242)
XLA Ops:
  0.6 0.0 copy-start.2
  0.6 0.0 copy-start.1
  0.7 44.8 %move_blocks.1 = (bf16[4,2,256,640]{3,2,1,0:T(8,128)(2,1)}, bf16[64,16,576]{2,1,0:T(8,128)(2,1)}) custom-call(s32[32,32]{1,0:T(8,128)} %holder.1, s32[32,32]{1,0:T(8,128)} %slot.1, s32[32]{0:T(128)} %prefix.3, s32[32]{0:T(128)} %length.3, f32[1,512]{1,0:T(1,128)} %bitcast.5, f32[1,64]{1,0:T(1,128)} %constant.2.clone.frequency, bf16[128,1792]{1,0:T(8,128)(2,1)} %tokens_h.1, ...), custom_call_target="tpu_custom_call" | custom-call | tf_op jit(solution)/shard_map/move_blocks/pallas_call | solution.py:455
  45.5 0.0 copy-done.2
  45.5 0.0 copy-done.1
  45.5 0.0 copy-start
  45.5 1.7 %copy-done = bf16[4,2,256,640]{3,2,1,0:T(8,128)(2,1)S(1)} copy-done((bf16[4,2,256,640]{3,2,1,0:T(8,128)(2,1)S(1)}, bf16[4,2,256,640]{3,2,1,0:T(8,128)(2,1)}, u32[]{:S(2)}) %copy-start) | copy-done | bytes 2621464
  47.3 0.0 copy-start.3
  47.3 50.8 %attend.1 = bf16[128,4096]{1,0:T(8,128)(2,1)} custom-call(s32[32]{0:T(128)S(1)} %copy-done.1, s32[32]{0:T(128)S(1)} %copy-done.2, bf16[4,2,256,640]{3,2,1,0:T(8,128)(2,1)S(1)} %copy-done, bf16[32,576,128]{2,1,0:T(8,128)(2,1)} %bitcast.3, bf16[32,512,128]{2,1,0:T(8,128)(2,1)} %values.1), custom_call_target="tpu_custom_call" | custom-call | tf_op jit(solution)/shard_map/attend/pallas_call | solution.py:524
  98.1 0.0 copy-done.3
  98.1 1.1 %copy.14 = bf16[64,16,576]{2,1,0:T(8,128)(2,1)} copy(bf16[64,16,576]{2,1,0:T(8,128)(2,1)S(1)} %copy-done.3) | data formatting | bytes 2359296
Async XLA Ops:
  0.6 44.9 %copy-start.2 = (s32[32]{0:T(128)S(1)}, s32[32]{0:T(128)}, u32[]{:S(2)}) copy-start(s32[32]{0:T(128)} %length.3) | copy-start | bytes 388
  0.6 44.9 %copy-start.1 = (s32[32]{0:T(128)S(1)}, s32[32]{0:T(128)}, u32[]{:S(2)}) copy-start(s32[32]{0:T(128)} %prefix.3) | copy-start | bytes 388
  45.5 1.7 %copy-start = (bf16[4,2,256,640]{3,2,1,0:T(8,128)(2,1)S(1)}, bf16[4,2,256,640]{3,2,1,0:T(8,128)(2,1)}, u32[]{:S(2)}) copy-start(bf16[4,2,256,640]{3,2,1,0:T(8,128)(2,1)} %get-tuple-element.4.keys) | copy-start | bytes 7864324
  47.3 50.8 %copy-start.3 = (bf16[64,16,576]{2,1,0:T(8,128)(2,1)S(1)}, bf16[64,16,576]{2,1,0:T(8,128)(2,1)}, u32[]{:S(2)}) copy-start(bf16[64,16,576]{2,1,0:T(8,128)(2,1)} %get-tuple-element.9) | copy-start | bytes 3538948

commit v5 on v3

--- a/solution.py
+++ b/solution.py
@@ -1,5 +1,4 @@
 import functools
-import math
 
 import jax
 import jax.numpy as jnp
@@ -18,9 +17,10 @@
 WIDE = 640
 ROPE = WIDTH - LATENT
 HALF = 256
-SCALE = 192.0 ** (-0.5) * math.log2(math.e)
+SCALE = 192.0 ** (-0.5)
 HIDDEN = -1e30
 EPSILON = 1e-06
+GROUP = 4
 MESH = pl.DeviceIdType.MESH
 
 
@@ -56,6 +56,8 @@
     near,
     far,
     keys_t,
+    scores,
+    weights,
     acc,
     high,
     norm,
@@ -168,8 +170,6 @@
         copy.start()
         sums.append(copy)
 
-    send_blocks(1)
-
     mark_row = lax.broadcasted_iota(jnp.int32, (WIDE - WIDTH, SUFFIX), 0)
     one_mark = jnp.where(mark_row == 0, 1.0, 0.0).astype(jnp.bfloat16)
 
@@ -251,6 +251,8 @@
     def gather_blocks(parity):
         others = arrived[parity].at[pl.ds(0, pool_count - 1)]
         pltpu.make_async_copy(others, others, block_recv.at[parity]).wait()
+        if parity == 0:
+            send_blocks(1)
 
         @pl.loop(0, groups - 1)
         def _(k):
@@ -308,61 +310,79 @@
             keys_t[:, rows] = keys[rows, :LATENT].T
         hidden = [base + new_row > token_lane for base in bases]
 
-        def scores_of(group):
-            query = jnp.concatenate([queries[head] for head in group], axis=1)
-            return jnp.dot(keys[...], query, preferred_element_type=jnp.float32)
-
-        def weigh(group, scores):
-            weights, decays, sums_of = [], [], []
-            for j, head in enumerate(group):
-                score = scores[:, j * SUFFIX : (j + 1) * SUFFIX]
-                parts = []
-                for half, hide in enumerate(hidden):
-                    end = (half + 1) * HALF
-                    parts.append(score[half * HALF : end - piece])
-                    parts.append(jnp.where(hide, HIDDEN, score[end - piece : end]))
-                score = jnp.concatenate(parts, axis=0).reshape(count // 8, 8, SUFFIX)
-                top = jnp.max(jnp.max(score, axis=0), axis=0, keepdims=True) * SCALE
-                top = jnp.broadcast_to(top, (8, SUFFIX))
+        def score(group, place):
+            query = jnp.concatenate([queries[GROUP * group + j] for j in range(GROUP)], axis=1)
+            scores[place, :count] = jnp.dot(
+                keys[...], query, preferred_element_type=jnp.float32
+            )
+            for half, hide in enumerate(hidden):
+                rows = slice((half + 1) * HALF - piece, (half + 1) * HALF)
+                for j in range(GROUP):
+                    lanes = slice(j * SUFFIX, (j + 1) * SUFFIX)
+                    scores[place, rows, lanes] = jnp.where(hide, HIDDEN, scores[place, rows, lanes])
+
+        def weigh(group, place):
+            decays, shares = [], []
+            for j in range(GROUP):
+                head = GROUP * group + j
+                lanes = slice(j * SUFFIX, (j + 1) * SUFFIX)
+                top = jnp.max(scores[place, :count, lanes].reshape(count // 8, 8, SUFFIX), axis=0)
+                top = jnp.broadcast_to(jnp.max(top, axis=0, keepdims=True), (8, SUFFIX))
                 if not first:
                     old = high[head]
                     top = jnp.maximum(old, top)
-                    decay = jnp.exp2(old - top)
+                    decay = jnp.exp((old - top) * SCALE)
                     decays.append(decay)
-                raised = jnp.exp2(score * SCALE - top[None])
-                total = jnp.sum(raised, axis=0)
+                total = None
+                for row in range(0, count, 64):
+                    part = scores[place, row : row + 64, lanes].reshape(8, 8, SUFFIX)
+                    raised = jnp.exp((part - top[None]) * SCALE)
+                    weights[place, row : row + 64, lanes] = raised.reshape(64, SUFFIX).astype(
+                        jnp.bfloat16
+                    )
+                    raised = jnp.sum(raised, axis=0)
+                    total = raised if total is None else total + raised
                 if not first:
                     total = total + norm[head] * decay
                 if last:
                     total = 1.0 / jnp.sum(total, axis=0, keepdims=True)
-                    sums_of.append(jnp.broadcast_to(total, (8, SUFFIX)))
+                    shares.append(jnp.broadcast_to(total, (8, SUFFIX)))
                 else:
                     high[head] = top
                     norm[head] = total
-                weights.append(raised.reshape(count, SUFFIX).astype(jnp.bfloat16))
+            return decays, shares
+
+        def mix(group, place, decays, shares):
             mixed = jnp.dot(
-                keys_t[:, :count],
-                jnp.concatenate(weights, axis=1),
-                preferred_element_type=jnp.float32,
+                keys_t[:, :count], weights[place, :count], preferred_element_type=jnp.float32
             )
-            for j, head in enumerate(group):
+            for j in range(GROUP):
+                head = GROUP * group + j
                 part = mixed[:, j * SUFFIX : (j + 1) * SUFFIX].reshape(LATENT // 8, 8, SUFFIX)
                 if not first:
                     part = part + acc[head].reshape(LATENT // 8, 8, SUFFIX) * decays[j][None]
                 if last:
-                    part = (part * sums_of[j][None]).reshape(LATENT, SUFFIX).astype(jnp.bfloat16)
+                    part = (part * shares[j][None]).reshape(LATENT, SUFFIX).astype(jnp.bfloat16)
                     value = jnp.dot(value_t[head], part, preferred_element_type=jnp.float32).T
                     columns = pl.ds(pl.multiple_of(head * VALUE_DIM, VALUE_DIM), VALUE_DIM)
                     out_v[:, columns] = jnp.where(live, value, 0.0).astype(jnp.bfloat16)
                 else:
                     acc[head] = part.reshape(LATENT, SUFFIX)
 
-        @pl.loop(0, heads // 4)
-        def _(quad):
-            groups_of = [[4 * quad + 2 * j, 4 * quad + 2 * j + 1] for j in range(2)]
-            scores = [scores_of(group) for group in groups_of]
-            for group, score in zip(groups_of, scores):
-                weigh(group, score)
+        def two_groups(group, more):
+            score(group + 1, 1)
+            mix(group, 0, *weigh(group, 0))
+            if more:
+                score(group + 2, 0)
+            mix(group + 1, 1, *weigh(group + 1, 1))
+
+        score(0, 0)
+
+        @pl.loop(0, heads // GROUP // 2 - 1)
+        def _(pair):
+            two_groups(2 * pair, True)
+
+        two_groups(heads // GROUP - 2, False)
 
     gather_blocks(0)
     attend(own.at[0], [tp * piece], first=True)
@@ -481,6 +501,8 @@
             pltpu.VMEM((2, 2 * HALF, WIDE), bf16),
             pltpu.VMEM((2 * HALF, WIDE), bf16),
             pltpu.VMEM((LATENT, 2 * HALF), bf16),
+            pltpu.VMEM((2, 2 * HALF, GROUP * SUFFIX), f32),
+            pltpu.VMEM((2, 2 * HALF, GROUP * SUFFIX), bf16),
             pltpu.VMEM((heads, LATENT, SUFFIX), f32),
             pltpu.VMEM((heads, 8, SUFFIX), f32),
             pltpu.VMEM((heads, 8, SUFFIX), f32),

time: 80 us -> 71 us (0.89)
  Pallas kernels: 75.1 us -> 65.7 us
    pallas_call x1, Pallas kernels: 75.1 us -> 65.7 us  [on_device(): pl.pallas_call(functools.partial(kernel, pool_count, tp_count), out_shape...]
where the time goes in v5:
time: 71 us; the launch traced here: 69.8 us
  Pallas kernels  65.7 us (93%)
  local copies, waits for them, and re-layouts  3.45 us (5%)
    pallas_call x1, Pallas kernels, on_device(): pl.pallas_call(functools.partial(kernel, pool_count, tp_count), out_shape...  65.7 us
    unnamed x4, local copies, waits for them, and re-layouts  3.45 us

profile of v5, /device:TPU:0, one launch (start us, length us, event | category | flops | bytes accessed | tf_op | source)
XLA Modules:
  0.0 69.8 jit_solution(15979667407286769605)
XLA Ops:
  0.6 65.7 %latent_attention.1 = (bf16[128,4096]{1,0:T(8,128)(2,1)}, bf16[64,16,576]{2,1,0:T(8,128)(2,1)}) custom-call(s32[32,32]{1,0:T(8,128)} %holder.1, s32[32,32]{1,0:T(8,128)} %slot.1, s32[32]{0:T(128)} %prefix.1, s32[32]{0:T(128)} %length.1, f32[1,512]{1,0:T(1,128)} %bitcast.5, f32[1,64]{1,0:T(1,128)} %constant.2.clone.frequency, bf16[128,1792]{1,0:T(8,128)(2,1)} %tokens_h.1, ...), custom_call_target="tpu_custom_call" | custom-call | tf_op jit(solution)/shard_map/latent_attention/pallas_call | solution.py:479
  66.4 0.0 copy-start
  66.4 2.4 %copy.15 = bf16[128,4096]{1,0:T(8,128)(2,1)} copy(bf16[128,4096]{1,0:T(8,128)(2,1)} %get-tuple-element.4) | data formatting | bytes 2097152
  68.8 0.0 copy-done
  68.8 1.1 %copy.16 = bf16[64,16,576]{2,1,0:T(8,128)(2,1)} copy(bf16[64,16,576]{2,1,0:T(8,128)(2,1)S(1)} %copy-done) | data formatting | bytes 2359296
Async XLA Ops:
  66.4 2.4 %copy-start = (bf16[64,16,576]{2,1,0:T(8,128)(2,1)S(1)}, bf16[64,16,576]{2,1,0:T(8,128)(2,1)}, u32[]{:S(2)}) copy-start(bf16[64,16,576]{2,1,0:T(8,128)(2,1)} %get-tuple-element.5) | copy-start | bytes 3538948

commit v6 on v5

--- a/solution.py
+++ b/solution.py
@@ -39,7 +39,7 @@
     value_h,
     pool_h,
     out_h,
-    new_pool_h,
+    fresh_h,
     tokens_v,
     down_v,
     queries,
@@ -47,6 +47,7 @@
     value_t,
     pool_v,
     leaving,
+    relay,
     arrived_even,
     arrived_odd,
     partial_v,
@@ -62,12 +63,10 @@
     high,
     norm,
     out_v,
-    new_pool_v,
-    index_v,
-    index_s,
     entry_s,
     load_sem,
-    index_sem,
+    relay_send,
+    relay_recv,
     block_send,
     block_recv,
     sum_send,
@@ -128,21 +127,81 @@
             entry_s[request] = at
         return slot[request, entry_s[request] + parity]
 
+    def stage(parity, to_core, to_x, to_z):
+        request = (to_x * 4 + to_z) * 2 + to_core
+        leaving[parity, to_core, to_x, to_z] = pool_v[wanted(request, parity)]
+        return request
+
+    def bundles(parity):
+        return (
+            pltpu.make_async_remote_copy(
+                src_ref=leaving.at[parity, core, (x + 2) % 4],
+                dst_ref=relay.at[parity, 0],
+                send_sem=relay_send.at[parity, 0],
+                recv_sem=relay_recv.at[parity, 0],
+                device_id=(((x + 3) % 4 * 4 + z) * 2 + core, tp),
+                device_id_type=MESH,
+            ),
+            pltpu.make_async_remote_copy(
+                src_ref=leaving.at[parity, 1 - core, :, (z + 2) % 4],
+                dst_ref=relay.at[parity, 1],
+                send_sem=relay_send.at[parity, 1],
+                recv_sem=relay_recv.at[parity, 1],
+                device_id=((x * 4 + (z + 3) % 4) * 2 + core, tp),
+                device_id_type=MESH,
+            ),
+        )
+
+    def send_block(parity, source, origin, to):
+        pltpu.make_async_remote_copy(
+            src_ref=source,
+            dst_ref=arrived[parity].at[origin],
+            send_sem=block_send.at[parity],
+            recv_sem=block_recv.at[parity],
+            device_id=(to, tp),
+            device_id_type=MESH,
+        ).start()
+
     def send_blocks(parity):
+        @pl.loop(0, 4)
+        def _(k):
+            stage(parity, core, (x + 2) % 4, k)
+            stage(parity, 1 - core, k, (z + 2) % 4)
+
+        for bundle in bundles(parity):
+            bundle.start()
+
         @pl.loop(1, pool_count)
         def _(step):
-            request = peer(step)
-            leaving[parity, request] = pool_v[wanted(request, parity)]
-            pltpu.make_async_remote_copy(
-                src_ref=leaving.at[parity, request],
-                dst_ref=arrived[parity].at[me],
-                send_sem=block_send.at[parity],
-                recv_sem=block_recv.at[parity],
-                device_id=(request, tp),
-                device_id_type=MESH,
-            ).start()
+            by_core, by_z, by_x = step % 2, (step // 2) % 4, step // 8
+            relayed = ((by_core == 0) & (by_x == 2)) | ((by_core == 1) & (by_z == 2))
+
+            @pl.when(jnp.logical_not(relayed))
+            def _():
+                to_core, to_x, to_z = (core + by_core) % 2, (x + by_x) % 4, (z + by_z) % 4
+                request = stage(parity, to_core, to_x, to_z)
+                send_block(parity, leaving.at[parity, to_core, to_x, to_z], me, request)
 
         arrived[parity][me] = pool_v[wanted(me, parity)]
+
+    def pass_on(parity):
+        for bundle in bundles(parity):
+            bundle.wait_recv()
+
+        @pl.loop(0, 4)
+        def _(k):
+            send_block(
+                parity,
+                relay.at[parity, 0, k],
+                ((x + 1) % 4 * 4 + z) * 2 + core,
+                ((x + 3) % 4 * 4 + k) * 2 + core,
+            )
+            send_block(
+                parity,
+                relay.at[parity, 1, k],
+                (x * 4 + (z + 1) % 4) * 2 + core,
+                (k * 4 + (z + 3) % 4) * 2 + 1 - core,
+            )
 
     send_blocks(0)
 
@@ -176,6 +235,8 @@
     @pl.loop(0, heads)
     def _(head):
         queries[head, WIDTH:, :] = one_mark
+
+    pass_on(0)
 
     for copy in sums:
         copy.wait_recv()
@@ -204,9 +265,6 @@
         fresh_in[fresh_at + b, :, LATENT:] = last[:, :ROPE]
         own[b, (groups - 1) * piece : groups * piece, :LATENT] = normed[rows]
         own[b, (groups - 1) * piece : groups * piece, LATENT:] = last
-
-    def fresh_place(at_core, at_z, at_x):
-        return 2 * ((at_core * 4 + at_z) * 4 + at_x)
 
     def along_x(step):
         here = fresh_in.at[pl.ds(fresh_place(core, z, x), 2)]
@@ -385,6 +443,7 @@
         two_groups(heads // GROUP - 2, False)
 
     gather_blocks(0)
+    pass_on(1)
     attend(own.at[0], [tp * piece], first=True)
     gather_blocks(1)
     attend(own.at[1], [BLOCK + tp * piece])
@@ -408,39 +467,17 @@
     store_out = pltpu.make_async_copy(out_v, out_h, load_sem.at[1])
     store_out.start()
 
-    lane_slot = lax.broadcasted_iota(jnp.int32, (8, 128), 1)
-
-    def mark_slot(request, index):
-        for b in range(2):
-            entry = prefix[request] + b
-            here = holder[request, entry] == me
-            target = jnp.where(here, slot[request, entry], -1)
-            index = jnp.where(lane_slot == target, fresh_place(request % 2, (request // 2) % 4, request // 8) + b, index)
-        return index
-
-    index_v[...] = lax.fori_loop(0, pool_count, mark_slot, jnp.full((8, 128), -1, jnp.int32))
-    to_scalars = pltpu.make_async_copy(index_v, index_s, index_sem)
-    to_scalars.start()
     to_other_core().wait_recv()
-    to_scalars.wait()
-
-    @pl.loop(0, slots)
-    def _(place):
-        at = index_s[0, place]
-        replaced = jnp.where(at >= 0, 1.0, 0.0)
-        kept = pool_v[place]
-        taken = fresh_in[jnp.maximum(at, 0)]
-        new_pool_v[place] = jnp.where(replaced > 0.5, taken, kept)
-
-    store_pool = pltpu.make_async_copy(new_pool_v, new_pool_h, load_sem.at[0])
-    store_pool.start()
-
+    store_fresh = pltpu.make_async_copy(fresh_in, fresh_h, load_sem.at[0])
+    store_fresh.start()
 
     for copy in sums:
         copy.wait_send()
     for parity in range(2):
-        sent = leaving.at[parity, pl.ds(0, pool_count - 1)]
+        sent = arrived[parity].at[pl.ds(0, pool_count - 1)]
         pltpu.make_async_copy(sent, sent, block_send.at[parity]).wait()
+        for bundle in bundles(parity):
+            bundle.wait_send()
         for side, to in enumerate((ahead, behind)):
             near_copy(parity, side, to).wait_send()
             far_copy(parity, side, to).wait_send()
@@ -448,8 +485,46 @@
         along_x(step).wait_send()
         along_z(step).wait_send()
     to_other_core().wait_send()
-    store_pool.wait()
+    store_fresh.wait()
     store_out.wait()
+
+
+def fresh_place(at_core, at_z, at_x):
+    return 2 * ((at_core * 4 + at_z) * 4 + at_x)
+
+
+def finish(holder, slot, prefix, result, fresh, pool, out, new_pool, sems, block_sems):
+    me = lax.axis_index("pool")
+    copies = [
+        pltpu.make_async_copy(pool, new_pool, sems.at[0]),
+        pltpu.make_async_copy(result, out, sems.at[1]),
+    ]
+    for copy in copies:
+        copy.start()
+    copies[0].wait()
+
+    def place(request, b, act):
+        entry = prefix[request] + b
+
+        @pl.when(holder[request, entry] == me)
+        def _():
+            source = fresh_place(request % 2, (request // 2) % 4, request // 8) + b
+            copy = pltpu.make_async_copy(
+                fresh.at[source], new_pool.at[slot[request, entry]], block_sems.at[request, b]
+            )
+            act(copy)
+
+    @pl.loop(0, holder.shape[0])
+    def _(request):
+        for b in range(2):
+            place(request, b, lambda copy: copy.start())
+
+    @pl.loop(0, holder.shape[0])
+    def _(request):
+        for b in range(2):
+            place(request, b, lambda copy: copy.wait())
+
+    copies[1].wait()
 
 
 def on_device(
@@ -476,11 +551,11 @@
     vmem = pl.BlockSpec(memory_space=pltpu.VMEM)
     anywhere = pl.BlockSpec(memory_space=pl.ANY)
     dma = pltpu.SemaphoreType.DMA
-    return pl.pallas_call(
+    result, fresh = pl.pallas_call(
         functools.partial(kernel, pool_count, tp_count),
         out_shape=(
             jax.ShapeDtypeStruct((SUFFIX, heads * VALUE_DIM), bf16),
-            jax.ShapeDtypeStruct(pool.shape, bf16),
+            jax.ShapeDtypeStruct((2 * pool_count, piece, WIDTH), bf16),
         ),
         in_specs=[smem] * 4 + [vmem] * 2 + [anywhere] * 5,
         out_specs=(anywhere, anywhere),
@@ -491,7 +566,8 @@
             pltpu.VMEM(value_weight.shape, bf16),
             pltpu.VMEM((heads, VALUE_DIM, LATENT), bf16),
             pltpu.VMEM(pool.shape, bf16),
-            pltpu.VMEM((2, pool_count, piece, WIDTH), bf16),
+            pltpu.VMEM((2, 2, 4, 4, piece, WIDTH), bf16),
+            pltpu.VMEM((2, 2, 4, piece, WIDTH), bf16),
             pltpu.VMEM((pool_count, piece, WIDTH), bf16),
             pltpu.VMEM((pool_count, piece, WIDTH), bf16),
             pltpu.VMEM((tp_count, 2 * piece, WIDTH), f32),
@@ -507,12 +583,10 @@
             pltpu.VMEM((heads, 8, SUFFIX), f32),
             pltpu.VMEM((heads, 8, SUFFIX), f32),
             pltpu.VMEM((SUFFIX, heads * VALUE_DIM), bf16),
-            pltpu.VMEM(pool.shape, bf16),
-            pltpu.VMEM((8, 128), jnp.int32),
-            pltpu.SMEM((8, 128), jnp.int32),
             pltpu.SMEM((pool_count,), jnp.int32),
             dma((5,)),
-            dma,
+            dma((2, 2)),
+            dma((2, 2)),
             dma((2,)),
             dma((2,)),
             dma((tp_count - 1,)),
@@ -541,6 +615,17 @@
         value_weight,
         pool,
     )
+    return pl.pallas_call(
+        finish,
+        out_shape=(
+            jax.ShapeDtypeStruct(result.shape, bf16),
+            jax.ShapeDtypeStruct(pool.shape, bf16),
+        ),
+        in_specs=[smem] * 3 + [anywhere] * 3,
+        out_specs=(anywhere, anywhere),
+        scratch_shapes=[dma((2,)), dma((pool_count, 2))],
+        name="finish",
+    )(block_holder, block_slot, prefix_blocks, result, fresh, pool)
 
 
 def solution(mesh):

time: 71 us -> 143 us (2.01); the launches traced: 69.8 us -> 140 us
  Pallas kernels: 65.7 us -> 139 us
  local copies, waits for them, and re-layouts: 3.45 us -> 0 us
    pallas_call x0 -> x1, Pallas kernels: none -> 75 us  [on_device(): pl.pallas_call(finish, out_shape=(jax.ShapeDtypeStruct(result.shape, bf16...]
    unnamed x4 -> x0, local copies, waits for them, and re-layouts: 3.45 us -> none
    pallas_call x1, Pallas kernels: 65.7 us -> 64.3 us  [on_device(): pl.pallas_call(functools.partial(kernel, pool_count, tp_count), out_shape...]
where the time goes in v6:
time: 143 us; the launch traced here: 140 us
  Pallas kernels  139 us (97%)
    pallas_call x1, Pallas kernels, on_device(): pl.pallas_call(finish, out_shape=(jax.ShapeDtypeStruct(result.shape, bf16...  75 us
    pallas_call x1, Pallas kernels, on_device(): pl.pallas_call(functools.partial(kernel, pool_count, tp_count), out_shape...  64.3 us

profile of v6, /device:TPU:0, one launch (start us, length us, event | category | flops | bytes accessed | tf_op | source)
XLA Modules:
  0.0 140.1 jit_solution(3546961728579476162)
XLA Ops:
  0.6 64.3 %latent_attention.1 = (bf16[128,4096]{1,0:T(8,128)(2,1)}, bf16[64,16,576]{2,1,0:T(8,128)(2,1)}) custom-call(s32[32,32]{1,0:T(8,128)} %holder.3, s32[32,32]{1,0:T(8,128)} %slot.3, s32[32]{0:T(128)} %prefix.3, s32[32]{0:T(128)} %length.1, f32[1,512]{1,0:T(1,128)} %bitcast.5, f32[1,64]{1,0:T(1,128)} %constant.2.clone.frequency, bf16[128,1792]{1,0:T(8,128)(2,1)} %tokens_h.1, ...), custom_call_target="tpu_custom_call" | custom-call | tf_op jit(solution)/shard_map/latent_attention/pallas_call | solution.py:554
  64.9 75.0 %finish.1 = (bf16[128,4096]{1,0:T(8,128)(2,1)}, bf16[64,16,576]{2,1,0:T(8,128)(2,1)}) custom-call(s32[32,32]{1,0:T(8,128)} %holder.3, s32[32,32]{1,0:T(8,128)} %slot.3, s32[32]{0:T(128)} %prefix.3, bf16[128,4096]{1,0:T(8,128)(2,1)} %get-tuple-element.4.result, bf16[64,16,576]{2,1,0:T(8,128)(2,1)} %get-tuple-element.5.fresh, bf16[64,16,576]{2,1,0:T(8,128)(2,1)} %pool.1), custom_call_target="tpu_custom_call" | custom-call | tf_op jit(solution)/shard_map/finish/pallas_call | solution.py:618

commit v7 on v5

--- a/solution.py
+++ b/solution.py
@@ -1,4 +1,5 @@
 import functools
+import math
 
 import jax
 import jax.numpy as jnp
@@ -17,7 +18,7 @@
 WIDE = 640
 ROPE = WIDTH - LATENT
 HALF = 256
-SCALE = 192.0 ** (-0.5)
+SCALE = 192.0 ** (-0.5) * math.log2(math.e)
 HIDDEN = -1e30
 EPSILON = 1e-06
 GROUP = 4
@@ -39,12 +40,11 @@
     value_h,
     pool_h,
     out_h,
-    new_pool_h,
+    fresh_h,
     tokens_v,
     down_v,
     queries,
     value_v,
-    value_t,
     pool_v,
     leaving,
     arrived_even,
@@ -62,12 +62,8 @@
     high,
     norm,
     out_v,
-    new_pool_v,
-    index_v,
-    index_s,
     entry_s,
     load_sem,
-    index_sem,
     block_send,
     block_recv,
     sum_send,
@@ -116,23 +112,25 @@
         pl.semaphore_signal(
             barrier, inc=1, device_id=(me, (tp + step) % tp_count), device_id_type=MESH
         )
+
+    loads[0].wait()
+
+    @pl.loop(0, pool_count)
+    def _(request):
+        at = jnp.int32(0)
+        for k in range(groups - 1):
+            at = jnp.where(holder[request, 2 * k] == me, 2 * k, at)
+        entry_s[request] = at
+        leaving[0, request] = pool_v[slot[request, at]]
+
+    arrived[0][me] = pool_v[slot[me, entry_s[me]]]
+
     pl.semaphore_wait(barrier, pool_count - 1 + tp_count - 1)
-
-    loads[0].wait()
-
-    def wanted(request, parity):
-        if parity == 0:
-            at = jnp.int32(0)
-            for k in range(groups - 1):
-                at = jnp.where(holder[request, 2 * k] == me, 2 * k, at)
-            entry_s[request] = at
-        return slot[request, entry_s[request] + parity]
 
     def send_blocks(parity):
         @pl.loop(1, pool_count)
         def _(step):
             request = peer(step)
-            leaving[parity, request] = pool_v[wanted(request, parity)]
             pltpu.make_async_remote_copy(
                 src_ref=leaving.at[parity, request],
                 dst_ref=arrived[parity].at[me],
@@ -142,9 +140,13 @@
                 device_id_type=MESH,
             ).start()
 
-        arrived[parity][me] = pool_v[wanted(me, parity)]
-
     send_blocks(0)
+
+    @pl.loop(0, pool_count)
+    def _(request):
+        leaving[1, request] = pool_v[slot[request, entry_s[request] + 1]]
+
+    arrived[1][me] = pool_v[slot[me, entry_s[me] + 1]]
 
     loads[1].wait()
     loads[2].wait()
@@ -205,9 +207,6 @@
         own[b, (groups - 1) * piece : groups * piece, :LATENT] = normed[rows]
         own[b, (groups - 1) * piece : groups * piece, LATENT:] = last
 
-    def fresh_place(at_core, at_z, at_x):
-        return 2 * ((at_core * 4 + at_z) * 4 + at_x)
-
     def along_x(step):
         here = fresh_in.at[pl.ds(fresh_place(core, z, x), 2)]
         to = (((x + step) % 4) * 4 + z) * 2 + core
@@ -263,60 +262,65 @@
             own[parity, rows, :LATENT] = block[:, :LATENT]
             own[parity, rows, LATENT:] = jnp.concatenate([block[:, LATENT:], marks], axis=1)
 
-        for side, to in enumerate((ahead, behind)):
-            near_copy(parity, side, to).start()
-
-    def near_copy(parity, side, to):
+        for part in range(2):
+            for side in range(2):
+                near_copy(parity, part, side).start()
+
+    neighbours = (ahead, behind)
+    third = HALF // 2
+
+    def near_copy(parity, part, side):
         return pltpu.make_async_remote_copy(
-            src_ref=own.at[parity],
-            dst_ref=near.at[parity, pl.ds(side * HALF, HALF)],
-            send_sem=near_send.at[parity, side],
-            recv_sem=near_recv.at[parity, side],
-            device_id=(me, to),
+            src_ref=own.at[parity, pl.ds(part * third, third)],
+            dst_ref=near.at[parity, part, pl.ds(side * third, third)],
+            send_sem=near_send.at[parity, part, side],
+            recv_sem=near_recv.at[parity, part, side],
+            device_id=(me, neighbours[side]),
             device_id_type=MESH,
         )
 
-    def far_copy(parity, side, to):
-        rows = HALF // 2
+    def far_copy(parity, side):
+        rows = pl.ds(side * third, third)
         return pltpu.make_async_remote_copy(
-            src_ref=near.at[parity, pl.ds(side * (HALF + rows), rows)],
-            dst_ref=far.at[pl.ds(parity * HALF + side * rows, rows)],
+            src_ref=near.at[parity, side, rows],
+            dst_ref=far.at[parity, rows],
             send_sem=far_send.at[parity, side],
             recv_sem=far_recv.at[parity, side],
-            device_id=(me, to),
+            device_id=(me, neighbours[side]),
             device_id_type=MESH,
         )
 
-    def forward(parity):
-        for side, to in enumerate((ahead, behind)):
-            near_copy(parity, side, to).wait_recv()
-            far_copy(parity, side, to).start()
+    def take(parity, part):
+        for side in range(2):
+            near_copy(parity, part, side).wait_recv()
+        far_copy(parity, part).start()
+
+    def take_far(parity):
+        for side in range(2):
+            far_copy(parity, side).wait_recv()
 
     loads[3].wait()
-    loads[4].wait()
-
-    @pl.loop(0, heads)
-    def _(head):
-        value_t[head] = value_v[head].T
 
     new_row = lax.broadcasted_iota(jnp.int32, (piece, SUFFIX), 0)
     token_lane = lax.broadcasted_iota(jnp.int32, (piece, SUFFIX), 1)
     live = lax.broadcasted_iota(jnp.int32, (SUFFIX, VALUE_DIM), 0) < length[me]
 
-    def attend(keys, bases, first=False, last=False):
-        count = len(bases) * HALF
-        for half in range(len(bases)):
-            rows = slice(half * HALF, (half + 1) * HALF)
-            keys_t[:, rows] = keys[rows, :LATENT].T
-        hidden = [base + new_row > token_lane for base in bases]
+    def attend(pieces, fresh_rows, first=False, last=False):
+        count = sum(piece_of.shape[0] for piece_of in pieces)
+        starts = [sum(p.shape[0] for p in pieces[:n]) for n in range(len(pieces))]
+        for start, keys in zip(starts, pieces):
+            for row in range(0, keys.shape[0], HALF):
+                keys_t[:, start + row : start + row + HALF] = keys[row : row + HALF, :LATENT].T
+        hidden = [(row, base + new_row > token_lane) for row, base in fresh_rows]
 
         def score(group, place):
             query = jnp.concatenate([queries[GROUP * group + j] for j in range(GROUP)], axis=1)
-            scores[place, :count] = jnp.dot(
-                keys[...], query, preferred_element_type=jnp.float32
-            )
-            for half, hide in enumerate(hidden):
-                rows = slice((half + 1) * HALF - piece, (half + 1) * HALF)
+            for start, keys in zip(starts, pieces):
+                scores[place, start : start + keys.shape[0]] = jnp.dot(
+                    keys[...], query, preferred_element_type=jnp.float32
+                )
+            for row, hide in hidden:
+                rows = slice(row, row + piece)
                 for j in range(GROUP):
                     lanes = slice(j * SUFFIX, (j + 1) * SUFFIX)
                     scores[place, rows, lanes] = jnp.where(hide, HIDDEN, scores[place, rows, lanes])
@@ -327,16 +331,17 @@
                 head = GROUP * group + j
                 lanes = slice(j * SUFFIX, (j + 1) * SUFFIX)
                 top = jnp.max(scores[place, :count, lanes].reshape(count // 8, 8, SUFFIX), axis=0)
-                top = jnp.broadcast_to(jnp.max(top, axis=0, keepdims=True), (8, SUFFIX))
+                top = jnp.max(top, axis=0, keepdims=True) * SCALE
+                top = jnp.broadcast_to(top, (8, SUFFIX))
                 if not first:
                     old = high[head]
                     top = jnp.maximum(old, top)
-                    decay = jnp.exp((old - top) * SCALE)
+                    decay = jnp.exp2(old - top)
                     decays.append(decay)
                 total = None
                 for row in range(0, count, 64):
                     part = scores[place, row : row + 64, lanes].reshape(8, 8, SUFFIX)
-                    raised = jnp.exp((part - top[None]) * SCALE)
+                    raised = jnp.exp2(part * SCALE - top[None])
                     weights[place, row : row + 64, lanes] = raised.reshape(64, SUFFIX).astype(
                         jnp.bfloat16
                     )
@@ -363,7 +368,7 @@
                     part = part + acc[head].reshape(LATENT // 8, 8, SUFFIX) * decays[j][None]
                 if last:
                     part = (part * shares[j][None]).reshape(LATENT, SUFFIX).astype(jnp.bfloat16)
-                    value = jnp.dot(value_t[head], part, preferred_element_type=jnp.float32).T
+                    value = jnp.dot(value_v[head].T, part, preferred_element_type=jnp.float32).T
                     columns = pl.ds(pl.multiple_of(head * VALUE_DIM, VALUE_DIM), VALUE_DIM)
                     out_v[:, columns] = jnp.where(live, value, 0.0).astype(jnp.bfloat16)
                 else:
@@ -384,72 +389,101 @@
 
         two_groups(heads // GROUP - 2, False)
 
+    def first_new(parity, owner):
+        return parity * BLOCK + owner * piece
+
     gather_blocks(0)
-    attend(own.at[0], [tp * piece], first=True)
+    attend([own.at[0]], [(HALF - piece, first_new(0, tp))], first=True)
+    take(0, 0)
+    attend([near.at[0, 0]], [])
     gather_blocks(1)
-    attend(own.at[1], [BLOCK + tp * piece])
+    take(0, 1)
     for step in range(1, 4):
         along_x(step).wait_recv()
     for step in range(1, 4):
         along_z(step).start()
-    for parity in range(2):
-        forward(parity)
-        attend(near.at[parity], [parity * BLOCK + side * piece for side in (behind, ahead)])
-
+    attend(
+        [near.at[0, 1]],
+        [(third - piece, first_new(0, behind)), (HALF - piece, first_new(0, ahead))],
+    )
+    take_far(0)
+    attend(
+        [far.at[0], own.at[1]],
+        [(HALF - piece, first_new(0, across)), (2 * HALF - piece, first_new(1, tp))],
+    )
+    for part in range(2):
+        take(1, part)
     for step in range(1, 4):
         along_z(step).wait_recv()
     to_other_core().start()
-
-    for parity in range(2):
-        for side, to in enumerate((ahead, behind)):
-            far_copy(parity, side, to).wait_recv()
-    attend(far, [parity * BLOCK + across * piece for parity in range(2)], last=True)
+    attend(
+        [near.at[1, 0], near.at[1, 1]],
+        [
+            (HALF + third - piece, first_new(1, behind)),
+            (2 * HALF - piece, first_new(1, ahead)),
+        ],
+    )
+    to_other_core().wait_recv()
+    store_fresh = pltpu.make_async_copy(fresh_in, fresh_h, load_sem.at[0])
+    store_fresh.start()
+    take_far(1)
+    loads[4].wait()
+    attend([far.at[1]], [(HALF - piece, first_new(1, across))], last=True)
 
     store_out = pltpu.make_async_copy(out_v, out_h, load_sem.at[1])
     store_out.start()
-
-    lane_slot = lax.broadcasted_iota(jnp.int32, (8, 128), 1)
-
-    def mark_slot(request, index):
-        for b in range(2):
-            entry = prefix[request] + b
-            here = holder[request, entry] == me
-            target = jnp.where(here, slot[request, entry], -1)
-            index = jnp.where(lane_slot == target, fresh_place(request % 2, (request // 2) % 4, request // 8) + b, index)
-        return index
-
-    index_v[...] = lax.fori_loop(0, pool_count, mark_slot, jnp.full((8, 128), -1, jnp.int32))
-    to_scalars = pltpu.make_async_copy(index_v, index_s, index_sem)
-    to_scalars.start()
-    to_other_core().wait_recv()
-    to_scalars.wait()
-
-    @pl.loop(0, slots)
-    def _(place):
-        at = index_s[0, place]
-        replaced = jnp.where(at >= 0, 1.0, 0.0)
-        kept = pool_v[place]
-        taken = fresh_in[jnp.maximum(at, 0)]
-        new_pool_v[place] = jnp.where(replaced > 0.5, taken, kept)
-
-    store_pool = pltpu.make_async_copy(new_pool_v, new_pool_h, load_sem.at[0])
-    store_pool.start()
-
 
     for copy in sums:
         copy.wait_send()
     for parity in range(2):
-        sent = leaving.at[parity, pl.ds(0, pool_count - 1)]
+        sent = arrived[parity].at[pl.ds(0, pool_count - 1)]
         pltpu.make_async_copy(sent, sent, block_send.at[parity]).wait()
-        for side, to in enumerate((ahead, behind)):
-            near_copy(parity, side, to).wait_send()
-            far_copy(parity, side, to).wait_send()
+        for side in range(2):
+            for part in range(2):
+                near_copy(parity, part, side).wait_send()
+            far_copy(parity, side).wait_send()
     for step in range(1, 4):
         along_x(step).wait_send()
         along_z(step).wait_send()
     to_other_core().wait_send()
+    store_fresh.wait()
+    store_out.wait()
+
+
+def fresh_place(at_core, at_z, at_x):
+    return 2 * ((at_core * 4 + at_z) * 4 + at_x)
+
+
+def finish(
+    holder, slot, prefix, result_h, fresh_h, pool_h, out_h, new_pool_h, result, fresh, pool, sems
+):
+    me = lax.axis_index("pool")
+    loads = [
+        pltpu.make_async_copy(pool_h, pool, sems.at[0]),
+        pltpu.make_async_copy(fresh_h, fresh, sems.at[1]),
+        pltpu.make_async_copy(result_h, result, sems.at[2]),
+    ]
+    for load in loads:
+        load.start()
+    for load in loads:
+        load.wait()
+    store_out = pltpu.make_async_copy(result, out_h, sems.at[2])
+    store_out.start()
+
+    @pl.loop(0, holder.shape[0])
+    def _(request):
+        for b in range(2):
+            entry = prefix[request] + b
+
+            @pl.when(holder[request, entry] == me)
+            def _():
+                source = fresh_place(request % 2, (request // 2) % 4, request // 8) + b
+                pool[slot[request, entry]] = fresh[source]
+
+    store_pool = pltpu.make_async_copy(pool, new_pool_h, sems.at[0])
+    store_pool.start()
+    store_out.wait()
     store_pool.wait()
-    store_out.wait()
 
 
 def on_device(
@@ -476,11 +510,11 @@
     vmem = pl.BlockSpec(memory_space=pltpu.VMEM)
     anywhere = pl.BlockSpec(memory_space=pl.ANY)
     dma = pltpu.SemaphoreType.DMA
-    return pl.pallas_call(
+    result, fresh = pl.pallas_call(
         functools.partial(kernel, pool_count, tp_count),
         out_shape=(
             jax.ShapeDtypeStruct((SUFFIX, heads * VALUE_DIM), bf16),
-            jax.ShapeDtypeStruct(pool.shape, bf16),
+            jax.ShapeDtypeStruct((2 * pool_count, piece, WIDTH), bf16),
         ),
         in_specs=[smem] * 4 + [vmem] * 2 + [anywhere] * 5,
         out_specs=(anywhere, anywhere),
@@ -489,7 +523,6 @@
             pltpu.VMEM(down_weight.shape[::-1], bf16),
             pltpu.VMEM((heads, WIDE, SUFFIX), bf16),
             pltpu.VMEM(value_weight.shape, bf16),
-            pltpu.VMEM((heads, VALUE_DIM, LATENT), bf16),
             pltpu.VMEM(pool.shape, bf16),
             pltpu.VMEM((2, pool_count, piece, WIDTH), bf16),
             pltpu.VMEM((pool_count, piece, WIDTH), bf16),
@@ -498,8 +531,8 @@
             pltpu.VMEM((tp_count - 1, 2 * piece, WIDTH), f32),
             pltpu.VMEM((2 * pool_count, piece, WIDTH), bf16),
             pltpu.VMEM((2, HALF, WIDE), bf16),
-            pltpu.VMEM((2, 2 * HALF, WIDE), bf16),
-            pltpu.VMEM((2 * HALF, WIDE), bf16),
+            pltpu.VMEM((2, 2, HALF, WIDE), bf16),
+            pltpu.VMEM((2, HALF, WIDE), bf16),
             pltpu.VMEM((LATENT, 2 * HALF), bf16),
             pltpu.VMEM((2, 2 * HALF, GROUP * SUFFIX), f32),
             pltpu.VMEM((2, 2 * HALF, GROUP * SUFFIX), bf16),
@@ -507,20 +540,16 @@
             pltpu.VMEM((heads, 8, SUFFIX), f32),
             pltpu.VMEM((heads, 8, SUFFIX), f32),
             pltpu.VMEM((SUFFIX, heads * VALUE_DIM), bf16),
-            pltpu.VMEM(pool.shape, bf16),
-            pltpu.VMEM((8, 128), jnp.int32),
-            pltpu.SMEM((8, 128), jnp.int32),
             pltpu.SMEM((pool_count,), jnp.int32),
             dma((5,)),
-            dma,
             dma((2,)),
             dma((2,)),
             dma((tp_count - 1,)),
             dma((tp_count - 1,)),
             dma((7,)),
             dma((7,)),
-            dma((2, 2)),
-            dma((2, 2)),
+            dma((2, 2, 2)),
+            dma((2, 2, 2)),
             dma((2, 2)),
             dma((2, 2)),
         ],
@@ -541,6 +570,22 @@
         value_weight,
         pool,
     )
+    return pl.pallas_call(
+        finish,
+        out_shape=(
+            jax.ShapeDtypeStruct(result.shape, bf16),
+            jax.ShapeDtypeStruct(pool.shape, bf16),
+        ),
+        in_specs=[smem] * 3 + [anywhere] * 3,
+        out_specs=(anywhere, anywhere),
+        scratch_shapes=[
+            pltpu.VMEM(result.shape, bf16),
+            pltpu.VMEM(fresh.shape, bf16),
+            pltpu.VMEM(pool.shape, bf16),
+            dma((3,)),
+        ],
+        name="finish",
+    )(block_holder, block_slot, prefix_blocks, result, fresh, pool)
 
 
 def solution(mesh):

time: 71 us -> 73.1 us (1.030); the launches traced: 69.8 us -> 72.8 us
  Pallas kernels: 65.7 us -> 72 us
  local copies, waits for them, and re-layouts: 3.45 us -> 0 us
    pallas_call x0 -> x1, Pallas kernels: none -> 4.64 us  [on_device(): pl.pallas_call(finish, out_shape=(jax.ShapeDtypeStruct(result.shape, bf16...]
    unnamed x4 -> x0, local copies, waits for them, and re-layouts: 3.45 us -> none
    pallas_call x1, Pallas kernels: 65.7 us -> 67.4 us  [on_device(): pl.pallas_call(functools.partial(kernel, pool_count, tp_count), out_shape...]
where the time goes in v7:
time: 73.1 us; the launch traced here: 72.8 us
  Pallas kernels  72 us (98%)
  between operations  0.8 us (1%)
    pallas_call x1, Pallas kernels, on_device(): pl.pallas_call(functools.partial(kernel, pool_count, tp_count), out_shape...  67.4 us
    pallas_call x1, Pallas kernels, on_device(): pl.pallas_call(finish, out_shape=(jax.ShapeDtypeStruct(result.shape, bf16...  4.64 us

profile of v7, /device:TPU:0, one launch (start us, length us, event | category | flops | bytes accessed | tf_op | source)
XLA Modules:
  0.0 72.8 jit_solution(7678663726365421785)
XLA Ops:
  0.6 67.4 %latent_attention.1 = (bf16[128,4096]{1,0:T(8,128)(2,1)}, bf16[64,16,576]{2,1,0:T(8,128)(2,1)}) custom-call(s32[32,32]{1,0:T(8,128)} %holder.3, s32[32,32]{1,0:T(8,128)} %slot.3, s32[32]{0:T(128)} %prefix.3, s32[32]{0:T(128)} %length.1, f32[1,512]{1,0:T(1,128)} %bitcast.5, f32[1,64]{1,0:T(1,128)} %constant.2.clone.frequency, bf16[128,1792]{1,0:T(8,128)(2,1)} %tokens_h.1, ...), custom_call_target="tpu_custom_call" | custom-call | tf_op jit(solution)/shard_map/latent_attention/pallas_call | solution.py:513
  68.0 4.6 %finish.1 = (bf16[128,4096]{1,0:T(8,128)(2,1)}, bf16[64,16,576]{2,1,0:T(8,128)(2,1)}) custom-call(s32[32,32]{1,0:T(8,128)} %holder.3, s32[32,32]{1,0:T(8,128)} %slot.3, s32[32]{0:T(128)} %prefix.3, bf16[128,4096]{1,0:T(8,128)(2,1)} %get-tuple-element.4.result_h, bf16[64,16,576]{2,1,0:T(8,128)(2,1)} %get-tuple-element.5.fresh_h, bf16[64,16,576]{2,1,0:T(8,128)(2,1)} %pool_h.3), custom_call_target="tpu_custom_call" | custom-call | tf_op jit(solution)/shard_map/finish/pallas_call | solution.py:573

commit v8 on v3

v8 whole, which is shorter than its diff:
```python
import functools
import math

import jax
import jax.numpy as jnp
import numpy as np
from jax import lax
from jax.experimental import pallas as pl
from jax.experimental.pallas import tpu as pltpu
from jax.sharding import PartitionSpec as P

LATENT = 512
VALUE_DIM = 128
BLOCK = 64
SUFFIX = 128
TABLE = 32
WIDTH = 576
WIDE = 640
ROPE = WIDTH - LATENT
HALF = 256
SCALE = 192.0 ** (-0.5) * math.log2(math.e)
HIDDEN = -1e30
EPSILON = 1e-06
ROWS = 1024
STRIP = 32
LOWEST = -3e38
MESH = pl.DeviceIdType.MESH


def kernel(
    pool_count,
    tp_count,
    holder,
    slot,
    prefix,
    length,
    gain,
    frequency,
    tokens_h,
    down_h,
    queries_h,
    value_h,
    pool_h,
    out_h,
    new_pool_h,
    tokens_v,
    down_v,
    queries_in,
    queries,
    value_v,
    pool_v,
    leaving,
    arrived_even,
    arrived_odd,
    partial_v,
    partial_in,
    fresh_in,
    keys,
    keys_t,
    bias,
    scores_a,
    scores_b,
    weights_a,
    weights_b,
    decay_a,
    decay_b,
    acc,
    high,
    norm,
    out_v,
    new_pool_v,
    index_v,
    index_s,
    entry_s,
    load_sem,
    index_sem,
    block_send,
    block_recv,
    sum_send,
    sum_recv,
    fresh_send,
    fresh_recv,
    near_send,
    near_recv,
    far_send,
    far_recv,
):
    me = lax.axis_index("pool")
    tp = lax.axis_index("tp")
    core, z, x = me % 2, (me // 2) % 4, me // 8
    ahead, behind = (tp + 1) % tp_count, (tp + tp_count - 1) % tp_count
    across = (tp + 2) % tp_count
    heads = queries_in.shape[0]
    slots = pool_v.shape[0]
    piece = pool_v.shape[1]
    groups = TABLE // 2
    arrived = (arrived_even, arrived_odd)
    scores, weights = (scores_a, scores_b), (weights_a, weights_b)
    decay = (decay_a, decay_b)

    def peer(step):
        to_core = (core + step % 2) % 2
        to_z = (z + (step // 2) % 4) % 4
        to_x = (x + step // 8) % 4
        return (to_x * 4 + to_z) * 2 + to_core

    loads = [
        pltpu.make_async_copy(pool_h, pool_v, load_sem.at[0]),
        pltpu.make_async_copy(tokens_h, tokens_v, load_sem.at[1]),
        pltpu.make_async_copy(down_h, down_v, load_sem.at[2]),
        pltpu.make_async_copy(queries_h, queries_in, load_sem.at[3]),
        pltpu.make_async_copy(value_h, value_v, load_sem.at[4]),
    ]
    for load in loads:
        load.start()

    barrier = pltpu.get_barrier_semaphore()

    @pl.loop(1, pool_count)
    def _(step):
        pl.semaphore_signal(barrier, inc=1, device_id=(peer(step), tp), device_id_type=MESH)

    for step in range(1, tp_count):
        pl.semaphore_signal(
            barrier, inc=1, device_id=(me, (tp + step) % tp_count), device_id_type=MESH
        )

    loads[0].wait()

    @pl.loop(0, pool_count)
    def _(request):
        at = jnp.int32(0)
        for k in range(groups - 1):
            at = jnp.where(holder[request, 2 * k] == me, 2 * k, at)
        entry_s[request] = at
        leaving[0, request] = pool_v[slot[request, at]]

    arrived[0][me] = pool_v[slot[me, entry_s[me]]]

    pl.semaphore_wait(barrier, pool_count - 1 + tp_count - 1)

    def send_blocks(parity):
        @pl.loop(1, pool_count)
        def _(step):
            request = peer(step)
            pltpu.make_async_remote_copy(
                src_ref=leaving.at[parity, request],
                dst_ref=arrived[parity].at[me],
                send_sem=block_send.at[parity],
                recv_sem=block_recv.at[parity],
                device_id=(request, tp),
                device_id_type=MESH,
            ).start()

    send_blocks(0)

    @pl.loop(0, pool_count)
    def _(request):
        leaving[1, request] = pool_v[slot[request, entry_s[request] + 1]]

    arrived[1][me] = pool_v[slot[me, entry_s[me] + 1]]

    loads[1].wait()
    loads[2].wait()
    partial = lax.dot_general(
        tokens_v[...], down_v[...], (((1,), (1,)), ((), ())), preferred_element_type=jnp.float32
    )
    for owner in range(tp_count):
        for b in range(2):
            partial_v[owner, b * piece : (b + 1) * piece, :] = partial[
                b * BLOCK + owner * piece : b * BLOCK + (owner + 1) * piece, :
            ]
    sums = []
    for step in range(1, tp_count):
        to = (tp + step) % tp_count
        copy = pltpu.make_async_remote_copy(
            src_ref=partial_v.at[to],
            dst_ref=partial_in.at[step - 1],
            send_sem=sum_send.at[step - 1],
            recv_sem=sum_recv.at[step - 1],
            device_id=(me, to),
            device_id_type=MESH,
        )
        copy.start()
        sums.append(copy)

    for copy in sums:
        copy.wait_recv()
    latent = partial_v[tp] + partial_in[0] + partial_in[1] + partial_in[2]
    content = latent[:, :LATENT]
    rotary = latent[:, LATENT:]
    inverse = lax.rsqrt(jnp.mean(content * content, axis=1, keepdims=True) + EPSILON)
    normed = content * inverse * gain[...]
    row = lax.broadcasted_iota(jnp.int32, (2 * piece, ROPE), 0)
    lane = lax.broadcasted_iota(jnp.int32, (2 * piece, ROPE), 1)
    token = (row // piece) * BLOCK + tp * piece + row % piece
    angles = (prefix[me] * BLOCK + token).astype(jnp.float32) * frequency[...]
    turned_by = jnp.concatenate([rotary[:, ROPE // 2 :], rotary[:, : ROPE // 2]], axis=1)
    sine = jnp.where(lane < ROPE // 2, -1.0, 1.0) * jnp.sin(angles)
    turned = rotary * jnp.cos(angles) + turned_by * sine
    row512 = lax.broadcasted_iota(jnp.int32, (2 * piece, LATENT), 0)
    token512 = (row512 // piece) * BLOCK + tp * piece + row512 % piece
    normed = jnp.where(token512 < length[me], normed, 0.0).astype(jnp.bfloat16)
    turned = jnp.where(token < length[me], turned, 0.0)
    fresh_at = 2 * ((core * 4 + z) * 4 + x)
    plain = jnp.zeros((piece, WIDE - WIDTH), jnp.float32)
    for b in range(2):
        rows = slice(b * piece, (b + 1) * piece)
        last = jnp.concatenate([turned[rows], plain], axis=1).astype(jnp.bfloat16)
        fresh_in[fresh_at + b, :, :LATENT] = normed[rows]
        fresh_in[fresh_at + b, :, LATENT:] = last[:, :ROPE]
        keys[b, (groups - 1) * piece : groups * piece, :LATENT] = normed[rows]
        keys[b, (groups - 1) * piece : groups * piece, LATENT:] = last

    def along_x(step):
        here = fresh_in.at[pl.ds(fresh_place(core, z, x), 2)]
        to = (((x + step) % 4) * 4 + z) * 2 + core
        return pltpu.make_async_remote_copy(
            src_ref=here,
            dst_ref=here,
            send_sem=fresh_send.at[step - 1],
            recv_sem=fresh_recv.at[step - 1],
            device_id=(to, tp),
            device_id_type=MESH,
        )

    def along_z(step):
        here = fresh_in.at[pl.ds(fresh_place(core, z, 0), 8)]
        to = (x * 4 + (z + step) % 4) * 2 + core
        return pltpu.make_async_remote_copy(
            src_ref=here,
            dst_ref=here,
            send_sem=fresh_send.at[step + 2],
            recv_sem=fresh_recv.at[step + 2],
            device_id=(to, tp),
            device_id_type=MESH,
        )

    def to_other_core():
        here = fresh_in.at[pl.ds(fresh_place(core, 0, 0), 32)]
        return pltpu.make_async_remote_copy(
            src_ref=here,
            dst_ref=here,
            send_sem=fresh_send.at[6],
            recv_sem=fresh_recv.at[6],
            device_id=((x * 4 + z) * 2 + 1 - core, tp),
            device_id_type=MESH,
        )

    for step in range(1, 4):
        along_x(step).start()

    lane_mark = lax.broadcasted_iota(jnp.int32, (piece, WIDE - WIDTH), 1)

    def gather_blocks(parity):
        others = arrived[parity].at[pl.ds(0, pool_count - 1)]
        pltpu.make_async_copy(others, others, block_recv.at[parity]).wait()
        if parity == 0:
            send_blocks(1)

        @pl.loop(0, groups - 1)
        def _(k):
            block = arrived[parity][holder[me, 2 * k + parity]]
            mark = jnp.where(2 * k + parity < prefix[me], 0.0, HIDDEN)
            marks = jnp.where(lane_mark == 0, mark, 0.0).astype(jnp.bfloat16)
            rows = pl.ds(pl.multiple_of(k * piece, piece), piece)
            keys[parity, rows, :LATENT] = block[:, :LATENT]
            keys[parity, rows, LATENT:] = jnp.concatenate([block[:, LATENT:], marks], axis=1)

        for part in range(2):
            for side in range(2):
                near_copy(parity, part, side).start()

    neighbours = (ahead, behind)
    third = HALF // 2

    def near_copy(parity, part, side):
        return pltpu.make_async_remote_copy(
            src_ref=keys.at[parity, pl.ds(part * third, third)],
            dst_ref=keys.at[2 * parity + part, pl.ds(HALF + side * third, third)],
            send_sem=near_send.at[parity, part, side],
            recv_sem=near_recv.at[parity, part, side],
            device_id=(me, neighbours[side]),
            device_id_type=MESH,
        )

    def far_copy(parity, side):
        return pltpu.make_async_remote_copy(
            src_ref=keys.at[2 * parity + side, pl.ds(HALF + side * third, third)],
            dst_ref=keys.at[2 + parity, pl.ds(side * third, third)],
            send_sem=far_send.at[parity, side],
            recv_sem=far_recv.at[parity, side],
            device_id=(me, neighbours[side]),
            device_id_type=MESH,
        )

    def take(parity, part):
        for side in range(2):
            near_copy(parity, part, side).wait_recv()
        far_copy(parity, part).start()

    def take_far(parity):
        for side in range(2):
            far_copy(parity, side).wait_recv()

    mark_lane = lax.broadcasted_iota(jnp.int32, (SUFFIX, WIDE - WIDTH), 1)
    one_mark = jnp.where(mark_lane == 0, 1.0, 0.0).astype(jnp.bfloat16)

    def turn(head):
        rows = pl.ds(pl.multiple_of(head * SUFFIX, SUFFIX), SUFFIX)
        turned_query = queries_in[head].T
        queries[rows, :LATENT] = turned_query[:, :LATENT]
        queries[rows, LATENT:] = jnp.concatenate([turned_query[:, LATENT:], one_mark], axis=1)

    loads[3].wait()
    early = heads * 5 // 8

    @pl.loop(0, early)
    def _(head):
        turn(head)

    gather_blocks(0)

    @pl.loop(early, heads)
    def _(head):
        turn(head)

    acc[...] = jnp.zeros_like(acc)
    norm[...] = jnp.zeros_like(norm)
    high[...] = jnp.full(high.shape, LOWEST, jnp.float32)

    lane = lax.broadcasted_iota(jnp.int32, (SUFFIX, 128), 1)
    row_token = lax.broadcasted_iota(jnp.int32, (SUFFIX, 128), 0)
    new_lane = lane - (128 - piece)

    def score(tile, place):
        rows = slice(tile * ROWS, (tile + 1) * ROWS)
        scores[place][...] = jnp.dot(
            queries[rows, :], keys_t[...], preferred_element_type=jnp.float32
        )

    def weigh(tile, place):
        for start in range(0, ROWS, STRIP):
            rows = slice(start, start + STRIP)
            all_rows = slice(tile * ROWS + start, tile * ROWS + start + STRIP)
            tokens_of = slice(start % SUFFIX, start % SUFFIX + STRIP)
            parts = [scores[place][rows, j * 128 : (j + 1) * 128] for j in range(4)]
            for j in range(1, 4):
                parts[j] = parts[j] + bias[j - 1, tokens_of, :]
            top = functools.reduce(jnp.maximum, parts)
            top = jnp.max(top, axis=1, keepdims=True) * SCALE
            old = high[all_rows, :]
            top = jnp.maximum(old, top)
            fade = jnp.exp2(old - top)
            raised = [jnp.exp2(part * SCALE - top) for part in parts]
            high[all_rows, :] = top
            decay[place][rows, :] = fade
            norm[all_rows, :] = norm[all_rows, :] * fade + functools.reduce(jnp.add, raised)
            for j in range(4):
                weights[place][rows, j * 128 : (j + 1) * 128] = raised[j].astype(jnp.bfloat16)

    def mix(tile, place, step):
        rows = slice(tile * ROWS, (tile + 1) * ROWS)
        mixed = jnp.dot(
            weights[place][...], keys[step, :, :LATENT], preferred_element_type=jnp.float32
        )
        for j in range(LATENT // 128):
            lanes = slice(j * 128, (j + 1) * 128)
            acc[rows, lanes] = acc[rows, lanes] * decay[place][...] + mixed[:, lanes]

    @pl.loop(0, 4)
    def _(step):
        @pl.when(step == 0)
        def _():
            take(0, 0)

        @pl.when(step == 1)
        def _():
            gather_blocks(1)
            take(0, 1)
            for hop in range(1, 4):
                along_x(hop).wait_recv()
            for hop in range(1, 4):
                along_z(hop).start()

        @pl.when(step == 2)
        def _():
            take(1, 0)
            take(1, 1)
            take_far(0)
            for hop in range(1, 4):
                along_z(hop).wait_recv()
            to_other_core().start()

        @pl.when(step == 3)
        def _():
            take_far(1)

        first_part = (step % 2) * BLOCK + jnp.where(step < 2, tp, across) * piece
        near_part = (step // 2) * BLOCK
        shown = (1 - step % 2) * -1000
        bases = (first_part, near_part + behind * piece + shown, near_part + ahead * piece + shown)
        for j, base in enumerate(bases):
            hide = (new_lane >= 0) & (base + new_lane > row_token)
            bias[j] = jnp.where(hide, HIDDEN, 0.0)
        keys_t[...] = keys[step].T

        tiles = queries.shape[0] // ROWS
        score(0, 0)
        for tile in range(tiles):
            if tile + 1 < tiles:
                score(tile + 1, (tile + 1) % 2)
            weigh(tile, tile % 2)
            mix(tile, tile % 2, step)

    loads[4].wait()
    live = lax.broadcasted_iota(jnp.int32, (SUFFIX, VALUE_DIM), 0) < length[me]

    @pl.loop(0, heads // 4)
    def _(quad):
        for inner in range(4):
            head = quad * 4 + inner
            rows = pl.ds(pl.multiple_of(head * SUFFIX, SUFFIX), SUFFIX)
            share = 1.0 / jnp.sum(norm[rows, :], axis=1, keepdims=True)
            mixed = (acc[rows, :] * share).astype(jnp.bfloat16)
            value = jnp.dot(mixed, value_v[head], preferred_element_type=jnp.float32)
            columns = pl.ds(pl.multiple_of(head * VALUE_DIM, VALUE_DIM), VALUE_DIM)
            out_v[:, columns] = jnp.where(live, value, 0.0).astype(jnp.bfloat16)

    store_out = pltpu.make_async_copy(out_v, out_h, load_sem.at[1])
    store_out.start()

    lane_slot = lax.broadcasted_iota(jnp.int32, (8, 128), 1)

    def mark_slot(request, index):
        for b in range(2):
            entry = prefix[request] + b
            here = holder[request, entry] == me
            target = jnp.where(here, slot[request, entry], -1)
            index = jnp.where(lane_slot == target, fresh_place(request % 2, (request // 2) % 4, request // 8) + b, index)
        return index

    index_v[...] = lax.fori_loop(0, pool_count, mark_slot, jnp.full((8, 128), -1, jnp.int32))
    to_scalars = pltpu.make_async_copy(index_v, index_s, index_sem)
    to_scalars.start()
    to_other_core().wait_recv()
    to_scalars.wait()

    @pl.loop(0, slots)
    def _(place):
        at = index_s[0, place]
        replaced = jnp.where(at >= 0, 1.0, 0.0)
        kept = pool_v[place]
        taken = fresh_in[jnp.maximum(at, 0)]
        new_pool_v[place] = jnp.where(replaced > 0.5, taken, kept)

    store_pool = pltpu.make_async_copy(new_pool_v, new_pool_h, load_sem.at[0])
    store_pool.start()


    for copy in sums:
        copy.wait_send()
    for parity in range(2):
        sent = arrived[parity].at[pl.ds(0, pool_count - 1)]
        pltpu.make_async_copy(sent, sent, block_send.at[parity]).wait()
        for side in range(2):
            for part in range(2):
                near_copy(parity, part, side).wait_send()
            far_copy(parity, side).wait_send()
    for step in range(1, 4):
        along_x(step).wait_send()
        along_z(step).wait_send()
    to_other_core().wait_send()
    store_pool.wait()
    store_out.wait()


def fresh_place(at_core, at_z, at_x):
    return 2 * ((at_core * 4 + at_z) * 4 + at_x)


def on_device(
    pool_count,
    tp_count,
    tokens,
    down_weight,
    kv_gain,
    queries,
    value_weight,
    pool,
    block_holder,
    block_slot,
    prefix_blocks,
    suffix_len,
):
    heads = queries.shape[1]
    piece = pool.shape[1]
    rows = SUFFIX * heads
    exponent = np.arange(ROPE // 2).astype(np.float32) * np.float32(2.0 / ROPE)
    inverse_frequency = np.power(np.float32(10000.0), -exponent).astype(np.float32)
    frequency = np.tile(inverse_frequency, 2)[None, :]
    bf16, f32 = jnp.bfloat16, jnp.float32
    smem = pl.BlockSpec(memory_space=pltpu.SMEM)
    vmem = pl.BlockSpec(memory_space=pltpu.VMEM)
    anywhere = pl.BlockSpec(memory_space=pl.ANY)
    dma = pltpu.SemaphoreType.DMA
    return pl.pallas_call(
        functools.partial(kernel, pool_count, tp_count),
        out_shape=(
            jax.ShapeDtypeStruct((SUFFIX, heads * VALUE_DIM), bf16),
            jax.ShapeDtypeStruct(pool.shape, bf16),
        ),
        in_specs=[smem] * 4 + [vmem] * 2 + [anywhere] * 5,
        out_specs=(anywhere, anywhere),
        scratch_shapes=[
            pltpu.VMEM(tokens.shape, bf16),
            pltpu.VMEM(down_weight.shape[::-1], bf16),
            pltpu.VMEM((heads, WIDTH, SUFFIX), bf16),
            pltpu.VMEM((rows, WIDE), bf16),
            pltpu.VMEM(value_weight.shape, bf16),
            pltpu.VMEM(pool.shape, bf16),
            pltpu.VMEM((2, pool_count, piece, WIDTH), bf16),
            pltpu.VMEM((pool_count, piece, WIDTH), bf16),
            pltpu.VMEM((pool_count, piece, WIDTH), bf16),
            pltpu.VMEM((tp_count, 2 * piece, WIDTH), f32),
            pltpu.VMEM((tp_count - 1, 2 * piece, WIDTH), f32),
            pltpu.VMEM((2 * pool_count, piece, WIDTH), bf16),
            pltpu.VMEM((4, 2 * HALF, WIDE), bf16),
            pltpu.VMEM((WIDE, 2 * HALF), bf16),
            pltpu.VMEM((3, SUFFIX, 128), f32),
            pltpu.VMEM((ROWS, 2 * HALF), f32),
            pltpu.VMEM((ROWS, 2 * HALF), f32),
            pltpu.VMEM((ROWS, 2 * HALF), bf16),
            pltpu.VMEM((ROWS, 2 * HALF), bf16),
            pltpu.VMEM((ROWS, 128), f32),
            pltpu.VMEM((ROWS, 128), f32),
            pltpu.VMEM((rows, LATENT), f32),
            pltpu.VMEM((rows, 128), f32),
            pltpu.VMEM((rows, 128), f32),
            pltpu.VMEM((SUFFIX, heads * VALUE_DIM), bf16),
            pltpu.VMEM(pool.shape, bf16),
            pltpu.VMEM((8, 128), jnp.int32),
            pltpu.SMEM((8, 128), jnp.int32),
            pltpu.SMEM((pool_count,), jnp.int32),
            dma((5,)),
            dma,
            dma((2,)),
            dma((2,)),
            dma((tp_count - 1,)),
            dma((tp_count - 1,)),
            dma((7,)),
            dma((7,)),
            dma((2, 2, 2)),
            dma((2, 2, 2)),
            dma((2, 2)),
            dma((2, 2)),
        ],
        compiler_params=pltpu.CompilerParams(
            collective_id=0, has_side_effects=True, vmem_limit_bytes=60 * 1024 * 1024
        ),
        name="latent_attention",
    )(
        block_holder,
        block_slot,
        prefix_blocks,
        suffix_len,
        kv_gain.reshape(1, LATENT),
        jnp.asarray(frequency),
        tokens,
        down_weight.T,
        queries.transpose(1, 2, 0),
        value_weight,
        pool,
    )


def solution(mesh):
    in_specs = (
        P("pool", "tp"),
        P("tp", None),
        P(),
        P("pool", "tp", None),
        P("tp", None, None),
        P("pool", "tp", None),
        P(),
        P(),
        P(),
        P(),
    )
    out_specs = (P("pool", "tp"), P("pool", "tp", None))
    return jax.shard_map(
        functools.partial(on_device, mesh.shape["pool"], mesh.shape["tp"]),
        mesh=mesh,
        in_specs=in_specs,
        out_specs=out_specs,
        check_vma=False,
    )
```

time: 80 us -> 71.4 us (0.89)
  Pallas kernels: 75.1 us -> 67.1 us
    pallas_call x1, Pallas kernels: 75.1 us -> 67.1 us  [on_device(): pl.pallas_call(functools.partial(kernel, pool_count, tp_count), out_shape...]
where the time goes in v8:
time: 71.4 us; the launch traced here: 71.2 us
  Pallas kernels  67.1 us (94%)
  local copies, waits for them, and re-layouts  3.45 us (5%)
    pallas_call x1, Pallas kernels, on_device(): pl.pallas_call(functools.partial(kernel, pool_count, tp_count), out_shape...  67.1 us
    unnamed x4, local copies, waits for them, and re-layouts  3.45 us

profile of v8, /device:TPU:0, one launch (start us, length us, event | category | flops | bytes accessed | tf_op | source)
XLA Modules:
  0.0 71.2 jit_solution(12084170753906658909)
XLA Ops:
  0.6 67.1 %latent_attention.1 = (bf16[128,4096]{1,0:T(8,128)(2,1)}, bf16[64,16,576]{2,1,0:T(8,128)(2,1)}) custom-call(s32[32,32]{1,0:T(8,128)} %holder.1, s32[32,32]{1,0:T(8,128)} %slot.1, s32[32]{0:T(128)} %prefix.1, s32[32]{0:T(128)} %length.1, f32[1,512]{1,0:T(1,128)} %bitcast.5, f32[1,64]{1,0:T(1,128)} %constant.2.clone.frequency, bf16[128,1792]{1,0:T(8,128)(2,1)} %tokens_h.1, ...), custom_call_target="tpu_custom_call" | custom-call | tf_op jit(solution)/shard_map/latent_attention/pallas_call | solution.py:507
  67.7 0.0 copy-start
  67.7 2.4 %copy.15 = bf16[128,4096]{1,0:T(8,128)(2,1)} copy(bf16[128,4096]{1,0:T(8,128)(2,1)} %get-tuple-element.4) | data formatting | bytes 2097152
  70.1 0.0 copy-done
  70.1 1.1 %copy.16 = bf16[64,16,576]{2,1,0:T(8,128)(2,1)} copy(bf16[64,16,576]{2,1,0:T(8,128)(2,1)S(1)} %copy-done) | data formatting | bytes 2359296
Async XLA Ops:
  67.7 2.4 %copy-start = (bf16[64,16,576]{2,1,0:T(8,128)(2,1)S(1)}, bf16[64,16,576]{2,1,0:T(8,128)(2,1)}, u32[]{:S(2)}) copy-start(bf16[64,16,576]{2,1,0:T(8,128)(2,1)} %get-tuple-element.5) | copy-start | bytes 3538948

commit v9 on v8

--- a/solution.py
+++ b/solution.py
@@ -21,7 +21,7 @@
 SCALE = 192.0 ** (-0.5) * math.log2(math.e)
 HIDDEN = -1e30
 EPSILON = 1e-06
-ROWS = 1024
+ROWS = 256
 STRIP = 32
 LOWEST = -3e38
 MESH = pl.DeviceIdType.MESH
@@ -312,6 +312,20 @@
         queries[rows, :LATENT] = turned_query[:, :LATENT]
         queries[rows, LATENT:] = jnp.concatenate([turned_query[:, LATENT:], one_mark], axis=1)
 
+    lane_slot = lax.broadcasted_iota(jnp.int32, (8, 128), 1)
+
+    def mark_slot(request, index):
+        for b in range(2):
+            entry = prefix[request] + b
+            here = holder[request, entry] == me
+            target = jnp.where(here, slot[request, entry], -1)
+            index = jnp.where(lane_slot == target, fresh_place(request % 2, (request // 2) % 4, request // 8) + b, index)
+        return index
+
+    index_v[...] = lax.fori_loop(0, pool_count, mark_slot, jnp.full((8, 128), -1, jnp.int32))
+    to_scalars = pltpu.make_async_copy(index_v, index_s, index_sem)
+    to_scalars.start()
+
     loads[3].wait()
     early = heads * 5 // 8
 
@@ -334,7 +348,7 @@
     new_lane = lane - (128 - piece)
 
     def score(tile, place):
-        rows = slice(tile * ROWS, (tile + 1) * ROWS)
+        rows = pl.ds(pl.multiple_of(tile * ROWS, ROWS), ROWS)
         scores[place][...] = jnp.dot(
             queries[rows, :], keys_t[...], preferred_element_type=jnp.float32
         )
@@ -342,7 +356,7 @@
     def weigh(tile, place):
         for start in range(0, ROWS, STRIP):
             rows = slice(start, start + STRIP)
-            all_rows = slice(tile * ROWS + start, tile * ROWS + start + STRIP)
+            all_rows = pl.ds(pl.multiple_of(tile * ROWS + start, STRIP), STRIP)
             tokens_of = slice(start % SUFFIX, start % SUFFIX + STRIP)
             parts = [scores[place][rows, j * 128 : (j + 1) * 128] for j in range(4)]
             for j in range(1, 4):
@@ -360,7 +374,7 @@
                 weights[place][rows, j * 128 : (j + 1) * 128] = raised[j].astype(jnp.bfloat16)
 
     def mix(tile, place, step):
-        rows = slice(tile * ROWS, (tile + 1) * ROWS)
+        rows = pl.ds(pl.multiple_of(tile * ROWS, ROWS), ROWS)
         mixed = jnp.dot(
             weights[place][...], keys[step, :, :LATENT], preferred_element_type=jnp.float32
         )
@@ -405,13 +419,23 @@
             bias[j] = jnp.where(hide, HIDDEN, 0.0)
         keys_t[...] = keys[step].T
 
+        def two_tiles(tile, more):
+            score(tile + 1, 1)
+            weigh(tile, 0)
+            mix(tile, 0, step)
+            if more:
+                score(tile + 2, 0)
+            weigh(tile + 1, 1)
+            mix(tile + 1, 1, step)
+
         tiles = queries.shape[0] // ROWS
         score(0, 0)
-        for tile in range(tiles):
-            if tile + 1 < tiles:
-                score(tile + 1, (tile + 1) % 2)
-            weigh(tile, tile % 2)
-            mix(tile, tile % 2, step)
+
+        @pl.loop(0, tiles // 2 - 1)
+        def _(pair):
+            two_tiles(2 * pair, True)
+
+        two_tiles(tiles - 2, False)
 
     loads[4].wait()
     live = lax.broadcasted_iota(jnp.int32, (SUFFIX, VALUE_DIM), 0) < length[me]
@@ -430,19 +454,6 @@
     store_out = pltpu.make_async_copy(out_v, out_h, load_sem.at[1])
     store_out.start()
 
-    lane_slot = lax.broadcasted_iota(jnp.int32, (8, 128), 1)
-
-    def mark_slot(request, index):
-        for b in range(2):
-            entry = prefix[request] + b
-            here = holder[request, entry] == me
-            target = jnp.where(here, slot[request, entry], -1)
-            index = jnp.where(lane_slot == target, fresh_place(request % 2, (request // 2) % 4, request // 8) + b, index)
-        return index
-
-    index_v[...] = lax.fori_loop(0, pool_count, mark_slot, jnp.full((8, 128), -1, jnp.int32))
-    to_scalars = pltpu.make_async_copy(index_v, index_s, index_sem)
-    to_scalars.start()
     to_other_core().wait_recv()
     to_scalars.wait()
 

time: 71.4 us -> 75.2 us (1.053)
  Pallas kernels: 67.1 us -> 70.9 us
    pallas_call x1, Pallas kernels: 67.1 us -> 70.9 us  [on_device(): pl.pallas_call(functools.partial(kernel, pool_count, tp_count), out_shape...]
where the time goes in v9:
time: 75.2 us; the launch traced here: 75 us
  Pallas kernels  70.9 us (94%)
  local copies, waits for them, and re-layouts  3.45 us (5%)
    pallas_call x1, Pallas kernels, on_device(): pl.pallas_call(functools.partial(kernel, pool_count, tp_count), out_shape...  70.9 us
    unnamed x4, local copies, waits for them, and re-layouts  3.45 us

profile of v9, /device:TPU:0, one launch (start us, length us, event | category | flops | bytes accessed | tf_op | source)
XLA Modules:
  0.0 75.0 jit_solution(6431600610011937064)
XLA Ops:
  0.6 70.9 %latent_attention.1 = (bf16[128,4096]{1,0:T(8,128)(2,1)}, bf16[64,16,576]{2,1,0:T(8,128)(2,1)}) custom-call(s32[32,32]{1,0:T(8,128)} %holder.1, s32[32,32]{1,0:T(8,128)} %slot.1, s32[32]{0:T(128)} %prefix.1, s32[32]{0:T(128)} %length.1, f32[1,512]{1,0:T(1,128)} %bitcast.5, f32[1,64]{1,0:T(1,128)} %constant.2.clone.frequency, bf16[128,1792]{1,0:T(8,128)(2,1)} %tokens_h.1, ...), custom_call_target="tpu_custom_call" | custom-call | tf_op jit(solution)/shard_map/latent_attention/pallas_call | solution.py:518
  71.5 0.0 copy-start
  71.5 2.4 %copy.15 = bf16[128,4096]{1,0:T(8,128)(2,1)} copy(bf16[128,4096]{1,0:T(8,128)(2,1)} %get-tuple-element.4) | data formatting | bytes 2097152
  73.9 0.0 copy-done
  73.9 1.1 %copy.16 = bf16[64,16,576]{2,1,0:T(8,128)(2,1)} copy(bf16[64,16,576]{2,1,0:T(8,128)(2,1)S(1)} %copy-done) | data formatting | bytes 2359296
Async XLA Ops:
  71.5 2.4 %copy-start = (bf16[64,16,576]{2,1,0:T(8,128)(2,1)S(1)}, bf16[64,16,576]{2,1,0:T(8,128)(2,1)}, u32[]{:S(2)}) copy-start(bf16[64,16,576]{2,1,0:T(8,128)(2,1)} %get-tuple-element.5) | copy-start | bytes 3538948

commit v10 on v9

--- a/solution.py
+++ b/solution.py
@@ -21,9 +21,8 @@
 SCALE = 192.0 ** (-0.5) * math.log2(math.e)
 HIDDEN = -1e30
 EPSILON = 1e-06
-ROWS = 256
+ROWS = 1024
 STRIP = 32
-LOWEST = -3e38
 MESH = pl.DeviceIdType.MESH
 
 
@@ -339,117 +338,144 @@
     def _(head):
         turn(head)
 
-    acc[...] = jnp.zeros_like(acc)
-    norm[...] = jnp.zeros_like(norm)
-    high[...] = jnp.full(high.shape, LOWEST, jnp.float32)
+    def before_near_even():
+        take(0, 0)
+
+    def before_own_odd():
+        gather_blocks(1)
+        take(0, 1)
+        for hop in range(1, 4):
+            along_x(hop).wait_recv()
+        for hop in range(1, 4):
+            along_z(hop).start()
+
+    def before_far_even():
+        take(1, 0)
+        take(1, 1)
+        take_far(0)
+        for hop in range(1, 4):
+            along_z(hop).wait_recv()
+        to_other_core().start()
+
+    def before_far_odd():
+        take_far(1)
+        loads[4].wait()
+
+    def first_new(parity, owner):
+        return parity * BLOCK + owner * piece
+
+    steps = (
+        (lambda: None, 0, 0, HALF, {1: first_new(0, tp)}),
+        (before_near_even, 0, HALF, HALF, {}),
+        (
+            before_own_odd,
+            1,
+            0,
+            2 * HALF,
+            {1: first_new(1, tp), 2: first_new(0, behind), 3: first_new(0, ahead)},
+        ),
+        (before_far_even, 2, 0, 2 * HALF, {1: first_new(0, across)}),
+        (
+            before_far_odd,
+            3,
+            0,
+            2 * HALF,
+            {1: first_new(1, across), 2: first_new(1, behind), 3: first_new(1, ahead)},
+        ),
+    )
 
     lane = lax.broadcasted_iota(jnp.int32, (SUFFIX, 128), 1)
     row_token = lax.broadcasted_iota(jnp.int32, (SUFFIX, 128), 0)
     new_lane = lane - (128 - piece)
-
-    def score(tile, place):
-        rows = pl.ds(pl.multiple_of(tile * ROWS, ROWS), ROWS)
-        scores[place][...] = jnp.dot(
-            queries[rows, :], keys_t[...], preferred_element_type=jnp.float32
-        )
-
-    def weigh(tile, place):
+    masks = []
+    for step in steps:
+        places = {}
+        for tile, base in step[4].items():
+            number = sum(len(m) for m in masks) + len(places)
+            hide = (new_lane >= 0) & (base + new_lane > row_token)
+            bias[number] = jnp.where(hide, HIDDEN, 0.0)
+            places[tile] = number
+        masks.append(places)
+    live = lax.broadcasted_iota(jnp.int32, (SUFFIX, VALUE_DIM), 0) < length[me]
+    tiles = queries.shape[0] // ROWS
+
+    def prepare(step):
+        before, number, start, count, _ = steps[step]
+        before()
+        keys_t[step % 2, :, :count] = keys[number, start : start + count].T
+
+    def score(step, tile, place):
+        count = steps[step][3]
+        rows = slice(tile * ROWS, (tile + 1) * ROWS)
+        scores[place][:, :count] = jnp.dot(
+            queries[rows, :], keys_t[step % 2, :, :count], preferred_element_type=jnp.float32
+        )
+
+    def weigh(step, tile, place):
         for start in range(0, ROWS, STRIP):
             rows = slice(start, start + STRIP)
-            all_rows = pl.ds(pl.multiple_of(tile * ROWS + start, STRIP), STRIP)
+            all_rows = slice(tile * ROWS + start, tile * ROWS + start + STRIP)
             tokens_of = slice(start % SUFFIX, start % SUFFIX + STRIP)
-            parts = [scores[place][rows, j * 128 : (j + 1) * 128] for j in range(4)]
-            for j in range(1, 4):
-                parts[j] = parts[j] + bias[j - 1, tokens_of, :]
+            columns = [slice(j * 128, (j + 1) * 128) for j in range(steps[step][3] // 128)]
+            parts = [scores[place][rows, lanes] for lanes in columns]
+            for j, number in masks[step].items():
+                parts[j] = parts[j] + bias[number, tokens_of, :]
             top = functools.reduce(jnp.maximum, parts)
             top = jnp.max(top, axis=1, keepdims=True) * SCALE
-            old = high[all_rows, :]
-            top = jnp.maximum(old, top)
-            fade = jnp.exp2(old - top)
+            if step == 0:
+                top = jnp.broadcast_to(top, (STRIP, 128))
+            else:
+                old = high[all_rows, :]
+                top = jnp.maximum(old, top)
+                fade = jnp.exp2(old - top)
+                decay[place][rows, :] = fade
             raised = [jnp.exp2(part * SCALE - top) for part in parts]
+            total = functools.reduce(jnp.add, raised)
+            if step > 0:
+                total = total + norm[all_rows, :] * fade
             high[all_rows, :] = top
-            decay[place][rows, :] = fade
-            norm[all_rows, :] = norm[all_rows, :] * fade + functools.reduce(jnp.add, raised)
-            for j in range(4):
-                weights[place][rows, j * 128 : (j + 1) * 128] = raised[j].astype(jnp.bfloat16)
-
-    def mix(tile, place, step):
-        rows = pl.ds(pl.multiple_of(tile * ROWS, ROWS), ROWS)
+            norm[all_rows, :] = total
+            for lanes, part in zip(columns, raised):
+                weights[place][rows, lanes] = part.astype(jnp.bfloat16)
+
+    def mix(step, tile, place):
+        _, number, start, count, _ = steps[step]
+        rows = slice(tile * ROWS, (tile + 1) * ROWS)
         mixed = jnp.dot(
-            weights[place][...], keys[step, :, :LATENT], preferred_element_type=jnp.float32
+            weights[place][:, :count],
+            keys[number, start : start + count, :LATENT],
+            preferred_element_type=jnp.float32,
         )
         for j in range(LATENT // 128):
             lanes = slice(j * 128, (j + 1) * 128)
-            acc[rows, lanes] = acc[rows, lanes] * decay[place][...] + mixed[:, lanes]
-
-    @pl.loop(0, 4)
-    def _(step):
-        @pl.when(step == 0)
-        def _():
-            take(0, 0)
-
-        @pl.when(step == 1)
-        def _():
-            gather_blocks(1)
-            take(0, 1)
-            for hop in range(1, 4):
-                along_x(hop).wait_recv()
-            for hop in range(1, 4):
-                along_z(hop).start()
-
-        @pl.when(step == 2)
-        def _():
-            take(1, 0)
-            take(1, 1)
-            take_far(0)
-            for hop in range(1, 4):
-                along_z(hop).wait_recv()
-            to_other_core().start()
-
-        @pl.when(step == 3)
-        def _():
-            take_far(1)
-
-        first_part = (step % 2) * BLOCK + jnp.where(step < 2, tp, across) * piece
-        near_part = (step // 2) * BLOCK
-        shown = (1 - step % 2) * -1000
-        bases = (first_part, near_part + behind * piece + shown, near_part + ahead * piece + shown)
-        for j, base in enumerate(bases):
-            hide = (new_lane >= 0) & (base + new_lane > row_token)
-            bias[j] = jnp.where(hide, HIDDEN, 0.0)
-        keys_t[...] = keys[step].T
-
-        def two_tiles(tile, more):
-            score(tile + 1, 1)
-            weigh(tile, 0)
-            mix(tile, 0, step)
-            if more:
-                score(tile + 2, 0)
-            weigh(tile + 1, 1)
-            mix(tile + 1, 1, step)
-
-        tiles = queries.shape[0] // ROWS
-        score(0, 0)
-
-        @pl.loop(0, tiles // 2 - 1)
-        def _(pair):
-            two_tiles(2 * pair, True)
-
-        two_tiles(tiles - 2, False)
-
-    loads[4].wait()
-    live = lax.broadcasted_iota(jnp.int32, (SUFFIX, VALUE_DIM), 0) < length[me]
-
-    @pl.loop(0, heads // 4)
-    def _(quad):
-        for inner in range(4):
-            head = quad * 4 + inner
-            rows = pl.ds(pl.multiple_of(head * SUFFIX, SUFFIX), SUFFIX)
+            part = mixed[:, lanes]
+            if step > 0:
+                part = part + acc[rows, lanes] * decay[place][...]
+            acc[rows, lanes] = part
+
+    def project(tile):
+        for inner in range(ROWS // SUFFIX):
+            head = tile * (ROWS // SUFFIX) + inner
+            rows = slice(head * SUFFIX, (head + 1) * SUFFIX)
             share = 1.0 / jnp.sum(norm[rows, :], axis=1, keepdims=True)
             mixed = (acc[rows, :] * share).astype(jnp.bfloat16)
             value = jnp.dot(mixed, value_v[head], preferred_element_type=jnp.float32)
-            columns = pl.ds(pl.multiple_of(head * VALUE_DIM, VALUE_DIM), VALUE_DIM)
+            columns = slice(head * VALUE_DIM, (head + 1) * VALUE_DIM)
             out_v[:, columns] = jnp.where(live, value, 0.0).astype(jnp.bfloat16)
+
+    work = [(step, tile) for step in range(len(steps)) for tile in range(tiles)]
+    prepare(0)
+    score(0, 0, 0)
+    for at, (step, tile) in enumerate(work):
+        if at + 1 < len(work):
+            after_step, after_tile = work[at + 1]
+            if after_step != step:
+                prepare(after_step)
+            score(after_step, after_tile, (at + 1) % 2)
+        weigh(step, tile, at % 2)
+        mix(step, tile, at % 2)
+        if step == len(steps) - 1:
+            project(tile)
 
     store_out = pltpu.make_async_copy(out_v, out_h, load_sem.at[1])
     store_out.start()
@@ -537,8 +563,8 @@
             pltpu.VMEM((tp_count - 1, 2 * piece, WIDTH), f32),
             pltpu.VMEM((2 * pool_count, piece, WIDTH), bf16),
             pltpu.VMEM((4, 2 * HALF, WIDE), bf16),
-            pltpu.VMEM((WIDE, 2 * HALF), bf16),
-            pltpu.VMEM((3, SUFFIX, 128), f32),
+            pltpu.VMEM((2, WIDE, 2 * HALF), bf16),
+            pltpu.VMEM((8, SUFFIX, 128), f32),
             pltpu.VMEM((ROWS, 2 * HALF), f32),
             pltpu.VMEM((ROWS, 2 * HALF), f32),
             pltpu.VMEM((ROWS, 2 * HALF), bf16),

time: 75.2 us -> 67 us (0.89)
  Pallas kernels: 70.9 us -> 62.5 us
    pallas_call x1, Pallas kernels: 70.9 us -> 62.5 us  [on_device(): pl.pallas_call(functools.partial(kernel, pool_count, tp_count), out_shape...]
where the time goes in v10:
time: 67 us; the launch traced here: 66.6 us
  Pallas kernels  62.5 us (93%)
  local copies, waits for them, and re-layouts  3.45 us (5%)
    pallas_call x1, Pallas kernels, on_device(): pl.pallas_call(functools.partial(kernel, pool_count, tp_count), out_shape...  62.5 us
    unnamed x4, local copies, waits for them, and re-layouts  3.45 us

profile of v10, /device:TPU:0, one launch (start us, length us, event | category | flops | bytes accessed | tf_op | source)
XLA Modules:
  0.0 66.6 jit_solution(2703655875770327635)
XLA Ops:
  0.6 62.5 %latent_attention.1 = (bf16[128,4096]{1,0:T(8,128)(2,1)}, bf16[64,16,576]{2,1,0:T(8,128)(2,1)}) custom-call(s32[32,32]{1,0:T(8,128)} %holder.1, s32[32,32]{1,0:T(8,128)} %slot.1, s32[32]{0:T(128)} %prefix.1, s32[32]{0:T(128)} %length.1, f32[1,512]{1,0:T(1,128)} %bitcast.5, f32[1,64]{1,0:T(1,128)} %constant.2.clone.frequency, bf16[128,1792]{1,0:T(8,128)(2,1)} %tokens_h.1, ...), custom_call_target="tpu_custom_call" | custom-call | tf_op jit(solution)/shard_map/latent_attention/pallas_call | solution.py:544
  63.2 0.0 copy-start
  63.2 2.4 %copy.15 = bf16[128,4096]{1,0:T(8,128)(2,1)} copy(bf16[128,4096]{1,0:T(8,128)(2,1)} %get-tuple-element.4) | data formatting | bytes 2097152
  65.6 0.0 copy-done
  65.6 1.1 %copy.16 = bf16[64,16,576]{2,1,0:T(8,128)(2,1)} copy(bf16[64,16,576]{2,1,0:T(8,128)(2,1)S(1)} %copy-done) | data formatting | bytes 2359296
Async XLA Ops:
  63.2 2.4 %copy-start = (bf16[64,16,576]{2,1,0:T(8,128)(2,1)S(1)}, bf16[64,16,576]{2,1,0:T(8,128)(2,1)}, u32[]{:S(2)}) copy-start(bf16[64,16,576]{2,1,0:T(8,128)(2,1)} %get-tuple-element.5) | copy-start | bytes 3538948

commit v11 on v10

--- a/solution.py
+++ b/solution.py
@@ -151,6 +151,10 @@
                 device_id_type=MESH,
             ).start()
 
+    def blocks_sent(parity):
+        sent = leaving.at[parity, pl.ds(0, pool_count - 1)]
+        return pltpu.make_async_copy(sent, sent, block_send.at[parity])
+
     send_blocks(0)
 
     @pl.loop(0, pool_count)
@@ -254,8 +258,6 @@
     def gather_blocks(parity):
         others = arrived[parity].at[pl.ds(0, pool_count - 1)]
         pltpu.make_async_copy(others, others, block_recv.at[parity]).wait()
-        if parity == 0:
-            send_blocks(1)
 
         @pl.loop(0, groups - 1)
         def _(k):
@@ -326,17 +328,21 @@
     to_scalars.start()
 
     loads[3].wait()
-    early = heads * 5 // 8
-
-    @pl.loop(0, early)
+    tiles = queries.shape[0] // ROWS
+    tile_heads = ROWS // SUFFIX
+
+    @pl.loop(0, tile_heads)
     def _(head):
         turn(head)
 
-    gather_blocks(0)
-
-    @pl.loop(early, heads)
+    blocks_sent(0).wait()
+    send_blocks(1)
+
+    @pl.loop(tile_heads, 2 * tile_heads)
     def _(head):
         turn(head)
+
+    gather_blocks(0)
 
     def before_near_even():
         take(0, 0)
@@ -397,8 +403,6 @@
             places[tile] = number
         masks.append(places)
     live = lax.broadcasted_iota(jnp.int32, (SUFFIX, VALUE_DIM), 0) < length[me]
-    tiles = queries.shape[0] // ROWS
-
     def prepare(step):
         before, number, start, count, _ = steps[step]
         before()
@@ -454,8 +458,8 @@
             acc[rows, lanes] = part
 
     def project(tile):
-        for inner in range(ROWS // SUFFIX):
-            head = tile * (ROWS // SUFFIX) + inner
+        for inner in range(tile_heads):
+            head = tile * tile_heads + inner
             rows = slice(head * SUFFIX, (head + 1) * SUFFIX)
             share = 1.0 / jnp.sum(norm[rows, :], axis=1, keepdims=True)
             mixed = (acc[rows, :] * share).astype(jnp.bfloat16)
@@ -472,6 +476,9 @@
             if after_step != step:
                 prepare(after_step)
             score(after_step, after_tile, (at + 1) % 2)
+        if step == 0 and tile + 2 < tiles:
+            for head in range((tile + 2) * tile_heads, (tile + 3) * tile_heads):
+                turn(head)
         weigh(step, tile, at % 2)
         mix(step, tile, at % 2)
         if step == len(steps) - 1:
@@ -497,9 +504,8 @@
 
     for copy in sums:
         copy.wait_send()
+    blocks_sent(1).wait()
     for parity in range(2):
-        sent = arrived[parity].at[pl.ds(0, pool_count - 1)]
-        pltpu.make_async_copy(sent, sent, block_send.at[parity]).wait()
         for side in range(2):
             for part in range(2):
                 near_copy(parity, part, side).wait_send()

time: 67 us -> 66.6 us (level)
  Pallas kernels: 62.5 us -> 61.8 us
    pallas_call x1, Pallas kernels: 62.5 us -> 61.8 us  [on_device(): pl.pallas_call(functools.partial(kernel, pool_count, tp_count), out_shape...]
where the time goes in v11:
time: 66.6 us; the launch traced here: 65.9 us
  Pallas kernels  61.8 us (93%)
  local copies, waits for them, and re-layouts  3.45 us (5%)
    pallas_call x1, Pallas kernels, on_device(): pl.pallas_call(functools.partial(kernel, pool_count, tp_count), out_shape...  61.8 us
    unnamed x4, local copies, waits for them, and re-layouts  3.45 us

profile of v11, /device:TPU:0, one launch (start us, length us, event | category | flops | bytes accessed | tf_op | source)
XLA Modules:
  0.0 65.9 jit_solution(16616974331624820015)
XLA Ops:
  0.6 61.8 %latent_attention.1 = (bf16[128,4096]{1,0:T(8,128)(2,1)}, bf16[64,16,576]{2,1,0:T(8,128)(2,1)}) custom-call(s32[32,32]{1,0:T(8,128)} %holder.1, s32[32,32]{1,0:T(8,128)} %slot.1, s32[32]{0:T(128)} %prefix.1, s32[32]{0:T(128)} %length.1, f32[1,512]{1,0:T(1,128)} %bitcast.5, f32[1,64]{1,0:T(1,128)} %constant.2.clone.frequency, bf16[128,1792]{1,0:T(8,128)(2,1)} %tokens_h.1, ...), custom_call_target="tpu_custom_call" | custom-call | tf_op jit(solution)/shard_map/latent_attention/pallas_call | solution.py:550
  62.5 0.0 copy-start
  62.5 2.4 %copy.15 = bf16[128,4096]{1,0:T(8,128)(2,1)} copy(bf16[128,4096]{1,0:T(8,128)(2,1)} %get-tuple-element.4) | data formatting | bytes 2097152
  64.9 0.0 copy-done
  64.9 1.1 %copy.16 = bf16[64,16,576]{2,1,0:T(8,128)(2,1)} copy(bf16[64,16,576]{2,1,0:T(8,128)(2,1)S(1)} %copy-done) | data formatting | bytes 2359296
Async XLA Ops:
  62.5 2.4 %copy-start = (bf16[64,16,576]{2,1,0:T(8,128)(2,1)S(1)}, bf16[64,16,576]{2,1,0:T(8,128)(2,1)}, u32[]{:S(2)}) copy-start(bf16[64,16,576]{2,1,0:T(8,128)(2,1)} %get-tuple-element.5) | copy-start | bytes 3538948

commit v12 on v11

--- a/solution.py
+++ b/solution.py
@@ -363,7 +363,23 @@
             along_z(hop).wait_recv()
         to_other_core().start()
 
+    store_pool = pltpu.make_async_copy(new_pool_v, new_pool_h, load_sem.at[0])
+
     def before_far_odd():
+        to_other_core().wait_recv()
+        to_scalars.wait()
+
+        @pl.loop(0, slots // 4)
+        def _(quad):
+            for inner in range(4):
+                place = quad * 4 + inner
+                at = index_s[0, place]
+                replaced = jnp.where(at >= 0, 1.0, 0.0)
+                kept = pool_v[place]
+                taken = fresh_in[jnp.maximum(at, 0)]
+                new_pool_v[place] = jnp.where(replaced > 0.5, taken, kept)
+
+        store_pool.start()
         take_far(1)
         loads[4].wait()
 
@@ -486,21 +502,6 @@
 
     store_out = pltpu.make_async_copy(out_v, out_h, load_sem.at[1])
     store_out.start()
-
-    to_other_core().wait_recv()
-    to_scalars.wait()
-
-    @pl.loop(0, slots)
-    def _(place):
-        at = index_s[0, place]
-        replaced = jnp.where(at >= 0, 1.0, 0.0)
-        kept = pool_v[place]
-        taken = fresh_in[jnp.maximum(at, 0)]
-        new_pool_v[place] = jnp.where(replaced > 0.5, taken, kept)
-
-    store_pool = pltpu.make_async_copy(new_pool_v, new_pool_h, load_sem.at[0])
-    store_pool.start()
-
 
     for copy in sums:
         copy.wait_send()

time: 66.6 us -> 66.2 us (level)
  no operation moved by 1% of the time
where the time goes in v12:
time: 66.2 us; the launch traced here: 65.5 us
  Pallas kernels  61.4 us (93%)
  local copies, waits for them, and re-layouts  3.45 us (5%)
    pallas_call x1, Pallas kernels, on_device(): pl.pallas_call(functools.partial(kernel, pool_count, tp_count), out_shape...  61.4 us
    unnamed x4, local copies, waits for them, and re-layouts  3.45 us

profile of v12, /device:TPU:0, one launch (start us, length us, event | category | flops | bytes accessed | tf_op | source)
XLA Modules:
  0.0 65.5 jit_solution(15805108552608753339)
XLA Ops:
  0.6 61.4 %latent_attention.1 = (bf16[128,4096]{1,0:T(8,128)(2,1)}, bf16[64,16,576]{2,1,0:T(8,128)(2,1)}) custom-call(s32[32,32]{1,0:T(8,128)} %holder.1, s32[32,32]{1,0:T(8,128)} %slot.1, s32[32]{0:T(128)} %prefix.1, s32[32]{0:T(128)} %length.1, f32[1,512]{1,0:T(1,128)} %bitcast.5, f32[1,64]{1,0:T(1,128)} %constant.2.clone.frequency, bf16[128,1792]{1,0:T(8,128)(2,1)} %tokens_h.1, ...), custom_call_target="tpu_custom_call" | custom-call | tf_op jit(solution)/shard_map/latent_attention/pallas_call | solution.py:551
  62.0 0.0 copy-start
  62.0 2.4 %copy.15 = bf16[128,4096]{1,0:T(8,128)(2,1)} copy(bf16[128,4096]{1,0:T(8,128)(2,1)} %get-tuple-element.4) | data formatting | bytes 2097152
  64.4 0.0 copy-done
  64.4 1.1 %copy.16 = bf16[64,16,576]{2,1,0:T(8,128)(2,1)} copy(bf16[64,16,576]{2,1,0:T(8,128)(2,1)S(1)} %copy-done) | data formatting | bytes 2359296
Async XLA Ops:
  62.0 2.4 %copy-start = (bf16[64,16,576]{2,1,0:T(8,128)(2,1)S(1)}, bf16[64,16,576]{2,1,0:T(8,128)(2,1)}, u32[]{:S(2)}) copy-start(bf16[64,16,576]{2,1,0:T(8,128)(2,1)} %get-tuple-element.5) | copy-start | bytes 3538948
